TPU v7x, 128 devices: a whole 4x4x4 slice. The times are simulated.
128 devices in a mesh: row: 8 (over z, core), col: 16 (over y, x).
Axes of the slice: x: 4, y: 4, z: 4, core: 2. Of those that a mesh axis runs over, the one named last changes fastest.
Arguments:
- currents: float32 [2, 524288], P(None, ('row', 'col')), may hold values from -6 to 6
- near_blocks: bfloat16 [16384, 2, 128, 128], P(('row', 'col')), may hold values from -0.5 to 0.5
- pair_local: int32 [128, 128], P(('row', 'col')), may hold values from 0 to 31
- pair_ghost: int32 [128, 128], P(('row', 'col')), may hold values from 0 to 287, as said below
- pair_counts: int32 [128], P(('row', 'col')), may hold values from 1 to 128, 9830 in all
- projection: float32 [4096, 128, 128], P(('row', 'col')), may hold values from -0.5 to 0.5
- stencil_cells: int32 [4096, 128], P(('row', 'col')), may hold values from 0 to 287231, as said below
- green: float32 [2, 32, 1024, 1024], P(None, 'col', 'row'), may hold values from -24 to 24
Outputs:
- product: float32 [2, 524288], P(None, ('row', 'col'))
Inputs may be any that keep to these rules, and one draw needn't show every extreme that they name: `stencil_cells`: every index lies in a box of 4 x 4 x 8 cells of the tile with rims, the box's corner drawn per block; the extreme boxes occur. `pair_ghost`: n = entry // 32 names the tile offset (n // 3 - 1, n % 3 - 1) around the holder's tile, wrapping on the torus of tiles, and entry % 32 a block of that tile; no slot pairs a block with itself.
All inputs are finite; a program needn't handle non-finite values. No bound on the sum of `pair_counts` on one device may be relied on, other than what follows from the above.
Results may differ from a plain program's by a relative error of at most 0.005.
Values may be sent and summed in bfloat16 or wider, within the bound.
A program may use at most 128 MiB of HBM per device.

v0:
```python
import math

import jax
import jax.numpy as jnp
from jax import lax
from jax.sharding import PartitionSpec as P

NGX = 1024
NGY = 1024
NGZ = 32
BOXX = 4
BOXY = 4
BOXZ = 8
RIM = 2


def with_halo(value, sides, width):
    for axis, dim in sides:
        peers, length = (lax.axis_size(axis), value.shape[dim])
        up = [(i, (i + 1) % peers) for i in range(peers)]
        down = [(j, i) for i, j in up]
        last = lax.slice_in_dim(value, length - width, length, axis=dim)
        first = lax.slice_in_dim(value, 0, width, axis=dim)
        before = lax.ppermute(last, axis, up)
        after = lax.ppermute(first, axis, down)
        value = jnp.concatenate([before, value, after], axis=dim)
    return value


def combine_parts(products):
    return jnp.stack(
        [products[:, 0, 0] - products[:, 1, 1], products[:, 0, 1] + products[:, 1, 0]], axis=1
    )


def with_rims(field):
    return with_halo(field, (("row", 1), ("col", 2)), RIM)


def fold_rims(field, axis_pos, inner, width):
    middle = lax.slice_in_dim(field, 2 * width, 2 * width + inner, axis=axis_pos)
    lower = lax.slice_in_dim(field, 0, width, axis=axis_pos)
    upper = lax.slice_in_dim(field, inner + 3 * width, inner + 4 * width, axis=axis_pos)
    lower_pads = [(0, 0)] * field.ndim
    upper_pads = [(0, 0)] * field.ndim
    lower_pads[axis_pos] = (0, inner - width)
    upper_pads[axis_pos] = (inner - width, 0)
    return middle + jnp.pad(lower, lower_pads) + jnp.pad(upper, upper_pads)


def dft_table(rows_len, cols_len, length, sign):
    index = (
        jnp.arange(rows_len, dtype=jnp.int32)[:, None]
        * jnp.arange(cols_len, dtype=jnp.int32)[None, :]
        % length
    )
    angle = index.astype(jnp.float32) * (2.0 * math.pi / length)
    return (jnp.cos(angle), sign * jnp.sin(angle))


def dft_along(field, axis_pos, inverse):
    moved = jnp.moveaxis(field, axis_pos, -1)
    length = moved.shape[-1]
    first = 1 << (length.bit_length() - 1) // 2
    second = length // first
    sign = 1.0 if inverse else -1.0
    leading = moved.shape[1:-1]
    real_part = moved[0].reshape(leading + (first, second))
    imag_part = moved[1].reshape(leading + (first, second))
    high = lax.Precision.HIGHEST
    cos_one, sin_one = dft_table(first, first, first, sign)
    outer_real = jnp.einsum("ka,...ab->...kb", cos_one, real_part, precision=high) - jnp.einsum(
        "ka,...ab->...kb", sin_one, imag_part, precision=high
    )
    outer_imag = jnp.einsum("ka,...ab->...kb", sin_one, real_part, precision=high) + jnp.einsum(
        "ka,...ab->...kb", cos_one, imag_part, precision=high
    )
    twist_cos, twist_sin = dft_table(first, second, length, sign)
    turned_real = outer_real * twist_cos - outer_imag * twist_sin
    turned_imag = outer_real * twist_sin + outer_imag * twist_cos
    cos_two, sin_two = dft_table(second, second, second, sign)
    inner_real = jnp.einsum("kb,...ab->...ka", cos_two, turned_real, precision=high) - jnp.einsum(
        "kb,...ab->...ka", sin_two, turned_imag, precision=high
    )
    inner_imag = jnp.einsum("kb,...ab->...ka", sin_two, turned_real, precision=high) + jnp.einsum(
        "kb,...ab->...ka", cos_two, turned_imag, precision=high
    )
    result = jnp.stack([inner_real, inner_imag]).reshape((2,) + leading + (length,))
    if inverse:
        result = result * (1.0 / length)
    return jnp.moveaxis(result, -1, axis_pos)


def forward_second(piece):
    return dft_along(piece, 2, False)


def forward_first(piece):
    return dft_along(piece, 1, False)


def inverse_second(piece):
    return dft_along(piece, 2, True)


def inverse_third(piece):
    return dft_along(piece, 3, True)


def box_tables(stencil_cells, wide_x, wide_y, depth):
    cell_x = stencil_cells // (wide_y * depth)
    cell_y = stencil_cells // depth % wide_y
    cell_z = stencil_cells % depth
    corner_x = jnp.min(cell_x, axis=1)
    corner_y = jnp.min(cell_y, axis=1)
    corner_z = jnp.min(cell_z, axis=1)
    offset_x = cell_x - corner_x[:, None]
    offset_y = cell_y - corner_y[:, None]
    offset_z = cell_z - corner_z[:, None]
    box_index = (offset_x * BOXY + offset_y) * BOXZ + offset_z
    box_len = BOXX * BOXY * BOXZ
    entry_hits = (
        box_index[:, :, None] == jnp.arange(box_len, dtype=jnp.int32)[None, None, :]
    ).astype(jnp.float32)
    hits_x = (
        corner_x[:, None, None] + jnp.arange(BOXX, dtype=jnp.int32)[None, :, None]
        == jnp.arange(wide_x, dtype=jnp.int32)[None, None, :]
    ).astype(jnp.float32)
    hits_y = (
        corner_y[:, None, None] + jnp.arange(BOXY, dtype=jnp.int32)[None, :, None]
        == jnp.arange(wide_y, dtype=jnp.int32)[None, None, :]
    ).astype(jnp.float32)
    hits_z = (
        corner_z[:, None, None] + jnp.arange(BOXZ, dtype=jnp.int32)[None, :, None]
        == jnp.arange(depth, dtype=jnp.int32)[None, None, :]
    ).astype(jnp.float32)
    return (entry_hits, hits_x, hits_y, hits_z)


def per_device(
    currents, near_blocks, pair_local, pair_ghost, pair_counts, projection, stencil_cells, green
):
    num_blocks = projection.shape[0]
    block_len = projection.shape[2]
    stencil_len = projection.shape[1]
    rows_count = lax.axis_size("row")
    cols_count = lax.axis_size("col")
    pair_slots = pair_ghost.shape[1]
    high = lax.Precision.HIGHEST
    blocks = currents.reshape(2, num_blocks, block_len)
    local_bf = blocks.astype(jnp.bfloat16)
    beside_all = with_halo(
        local_bf.reshape(2, 1, 1, num_blocks, block_len), (("row", 1), ("col", 2)), 1
    )
    beside_all = beside_all.reshape(2, 9 * num_blocks, block_len)
    picks = pair_ghost[0]
    owned = pair_local[0]
    living = (jnp.arange(pair_slots, dtype=jnp.int32) < pair_counts[0]).astype(jnp.float32)
    owner_table = owned[:, None] == jnp.arange(num_blocks, dtype=jnp.int32)[None, :]
    ghost_table = picks[:, None] == jnp.arange(9 * num_blocks, dtype=jnp.int32)[None, :]
    remote_vals = jnp.einsum(
        "ho,som->shm",
        ghost_table.astype(jnp.bfloat16),
        beside_all,
        preferred_element_type=jnp.float32,
    ).astype(jnp.bfloat16)
    local_vals = jnp.einsum(
        "ho,som->shm",
        owner_table.astype(jnp.bfloat16),
        local_bf,
        preferred_element_type=jnp.float32,
    ).astype(jnp.bfloat16)
    onward = jnp.einsum(
        "pcij,dpj->pcdi", near_blocks, remote_vals, preferred_element_type=jnp.float32
    )
    backward = jnp.einsum(
        "pcij,dpi->pcdj", near_blocks, local_vals, preferred_element_type=jnp.float32
    )
    onward = combine_parts(onward) * living[:, None, None]
    backward = combine_parts(backward) * living[:, None, None]
    near_own = jnp.einsum("pn,pcb->cnb", owner_table.astype(jnp.float32), onward, precision=high)
    spread_back = jnp.einsum(
        "pn,pcb->cnb", ghost_table.astype(jnp.float32), backward, precision=high
    )
    spread_back = spread_back.reshape(2, 3, 3, num_blocks, block_len)
    widened_back = with_halo(spread_back.astype(jnp.bfloat16), (("row", 1), ("col", 2)), 1).astype(
        spread_back.dtype
    )
    returned = fold_rims(fold_rims(widened_back, 1, 1, 1), 2, 1, 1).reshape(
        2, num_blocks, block_len
    )
    cells_x = NGX // rows_count
    cells_y = NGY // cols_count
    wide_x = cells_x + 2 * RIM
    wide_y = cells_y + 2 * RIM
    entry_hits, hits_x, hits_y, hits_z = box_tables(stencil_cells, wide_x, wide_y, NGZ)
    values = jnp.einsum("nkb,cnb->cnk", projection, blocks, precision=high)
    boxed = jnp.einsum("gkm,cgk->cgm", entry_hits, values, precision=high)
    boxed = boxed.reshape(2, num_blocks, BOXX, BOXY, BOXZ)
    placed_z = jnp.einsum("gzw,cgxyz->cgxyw", hits_z, boxed, precision=high)
    placed_y = jnp.einsum("gyv,cgxyw->cgxvw", hits_y, placed_z, precision=high)
    extended = jnp.einsum("gxu,cgxvw->cuvw", hits_x, placed_y, precision=high)
    widened = with_rims(extended)
    tile = fold_rims(fold_rims(widened, 1, cells_x, RIM), 2, cells_y, RIM)
    spectral = dft_along(tile, 3, False)
    spectral = forward_second(
        lax.all_to_all(spectral, "col", split_axis=3, concat_axis=2, tiled=True)
    )
    spectral = forward_first(
        lax.all_to_all(spectral, "row", split_axis=2, concat_axis=1, tiled=True)
    )
    kernel = jnp.transpose(green, (0, 3, 2, 1))
    spectral = jnp.stack(
        [
            spectral[0] * kernel[0] - spectral[1] * kernel[1],
            spectral[0] * kernel[1] + spectral[1] * kernel[0],
        ]
    )
    spectral = dft_along(spectral, 1, True)
    spectral = inverse_second(
        lax.all_to_all(spectral, "row", split_axis=1, concat_axis=2, tiled=True)
    )
    potential = inverse_third(
        lax.all_to_all(spectral, "col", split_axis=2, concat_axis=3, tiled=True)
    )
    rimmed = with_rims(potential)
    taken_x = jnp.einsum("gxu,cuvw->cgxvw", hits_x, rimmed, precision=high)
    taken_y = jnp.einsum("gyv,cgxvw->cgxyw", hits_y, taken_x, precision=high)
    taken_z = jnp.einsum("gzw,cgxyw->cgxyz", hits_z, taken_y, precision=high)
    box_vals = taken_z.reshape(2, num_blocks, stencil_len)
    picked = jnp.einsum("gkm,cgm->cgk", entry_hits, box_vals, precision=high)
    far = jnp.einsum("nkb,cnk->cnb", projection, picked, precision=high)
    total = far + near_own + returned
    return total.reshape(2, num_blocks * block_len)


def solution(mesh):
    in_specs = (
        P(None, ("row", "col")),
        P(("row", "col"), None, None, None),
        P(("row", "col"), None),
        P(("row", "col"), None),
        P(("row", "col")),
        P(("row", "col"), None, None),
        P(("row", "col"), None),
        P(None, "col", "row", None),
    )
    out_specs = P(None, ("row", "col"))
    return jax.shard_map(
        per_device, mesh=mesh, in_specs=in_specs, out_specs=out_specs, check_vma=False
    )
```

profile of v0, /device:TPU:1, one launch (start us, length us, event | category | flops | bytes accessed | tf_op | source)
XLA Modules:
  0.0 402.5 jit_solution(9147301353524302181)
XLA Ops:
  2.0 4.1 %convolution_bitcast_fusion.6 = f32[2,32,128]{2,0,1:T(2,128)S(1)} fusion(f32[32,128,128]{2,1,0:T(8,128)S(1)} %copy-done, f32[2,4096]{1,0:T(2,128)} %param.8), kind=kOutput, calls=%fused_computation.99 | convolution fusion | flops 12582912 | bytes 2162688 | tf_op jit(solution)/shard_map/nkb,cnb->cnk/dot_general | solution.py:197
  9.4 5.2 %convolution_bitcast_fusion.1 = f32[2,32,4,68,32]{3,4,2,0,1:T(8,128)} fusion(f32[2,32,4,4,32]{4,3,2,0,1:T(4,128)S(1)} %convolution_bitcast_fusion.3, s32[32,4]{1,0:T(8,128)S(1)} %iota_add_fusion), kind=kOutput, calls=%fused_computation.20 | convolution fusion | flops 26747392 | bytes 2359808 | tf_op jit(solution)/shard_map/gyv,cgxyw->cgxvw/dot_general | solution.py:201
  14.6 11.1 %copy.322 = f32[2,32,4,68,32]{1,4,2,3,0:T(8,128)} copy(f32[2,32,4,68,32]{3,4,2,0,1:T(8,128)} %convolution_bitcast_fusion.1) | data formatting | bytes 4456448 | tf_op jit(solution)/shard_map/gyv,cgxyw->cgxvw/transpose | solution.py:201
  25.7 6.7 %convolution_bitcast_fusion = f32[2,132,68,32]{1,3,2,0:T(8,128)S(1)} fusion(f32[2,32,4,68,32]{1,4,2,3,0:T(8,128)} %copy.322, s32[32,4]{0,1:T(4,128)S(1)} %iota_add_fusion.2), kind=kOutput, calls=%fused_computation.18 | convolution fusion | flops 882393600 | bytes 4526592 | tf_op jit(solution)/shard_map/gxu,cgxvw->cuvw/dot_general | solution.py:202
  32.3 3.3 fusion.538
  44.5 3.2 copy.325
  48.2 3.1 copy.326
  54.2 3.8 collective-permute-start.3
  81.0 6.3 %all-to-all-start = ((f32[2,128,64,32]{1,2,0,3:T(8,128)}), f32[2,128,64,32]{1,2,0,3:T(8,128)}, u32[]{:S(2)}, u32[]{:S(2)}) async-start(f32[2,128,64,32]{1,2,0,3:T(8,128)} %copy.337), calls=%async_computation | async-start | bytes 4194304 | tf_op jit(solution)/shard_map/all_to_all | solution.py:207
  87.7 24.9 %all-to-all-done = f32[2,128,64,32]{1,2,0,3:T(8,128)} async-done(((f32[2,128,64,32]{1,2,0,3:T(8,128)}), f32[2,128,64,32]{1,2,0,3:T(8,128)}, u32[]{:S(2)}, u32[]{:S(2)}) %all-to-all-start) | async-done | bytes 2097184 | tf_op jit(solution)/shard_map/all_to_all | solution.py:207
  133.3 13.2 %all-to-all-start.1 = ((f32[2,128,1024,2]{1,3,0,2:T(2,128)}), f32[2,128,1024,2]{1,3,0,2:T(2,128)}, u32[]{:S(2)}, u32[]{:S(2)}) async-start(f32[2,128,1024,2]{1,3,0,2:T(2,128)} %copy.352), calls=%async_computation.1 | async-start | bytes 4194304 | tf_op jit(solution)/shard_map/all_to_all | solution.py:210
  149.6 23.4 %all-to-all-done.1 = f32[2,128,1024,2]{1,3,0,2:T(2,128)} async-done(((f32[2,128,1024,2]{1,3,0,2:T(2,128)}), f32[2,128,1024,2]{1,3,0,2:T(2,128)}, u32[]{:S(2)}, u32[]{:S(2)}) %all-to-all-start.1) | async-done | bytes 2097184 | tf_op jit(solution)/shard_map/all_to_all | solution.py:210
  173.0 3.1 copy.353
  217.5 5.2 %all-to-all-start.2 = ((f32[2,1024,128,2]{2,3,0,1:T(2,128)}), f32[2,1024,128,2]{2,3,0,1:T(2,128)}, u32[]{:S(2)}, u32[]{:S(2)}) async-start(f32[2,1024,128,2]{2,3,0,1:T(2,128)} %copy.377), calls=%async_computation.2 | async-start | bytes 4194304 | tf_op jit(solution)/shard_map/all_to_all | solution.py:221
  224.7 4.6 %fusion.148 = f32[128,2,2,128]{3,1,2,0:T(2,128)S(1)} fusion(bf16[128,2,128,128]{3,2,1,0:T(8,128)(2,1)} %param.9, bf16[2,128,128,1]{2,1,0,3:T(8,128)(2,1)S(1)} %fusion.49), kind=kOutput, calls=%fused_computation.224 | convolution fusion | flops 16777216 | bytes 8716288 | tf_op jit(solution)/shard_map/pcij,dpi->pcdj/dot_general | solution.py:176
  230.5 18.7 %all-to-all-done.2 = f32[2,1024,128,2]{2,3,0,1:T(2,128)} async-done(((f32[2,1024,128,2]{2,3,0,1:T(2,128)}), f32[2,1024,128,2]{2,3,0,1:T(2,128)}, u32[]{:S(2)}, u32[]{:S(2)}) %all-to-all-start.2) | async-done | bytes 2097184 | tf_op jit(solution)/shard_map/all_to_all | solution.py:221
  249.2 3.1 copy.378
  252.3 3.1 copy.379
  276.1 4.4 %all-to-all-start.3 = ((f32[2,128,1024,2]{1,3,0,2:T(2,128)}), f32[2,128,1024,2]{1,3,0,2:T(2,128)}, u32[]{:S(2)}, u32[]{:S(2)}) async-start(f32[2,128,1024,2]{1,3,0,2:T(2,128)} %copy.390), calls=%async_computation.3 | async-start | bytes 4194304 | tf_op jit(solution)/shard_map/all_to_all | solution.py:224
  284.0 3.5 collective-permute-start.11
  288.4 4.9 %collective-permute-start.15 = (bf16[2,5,1,32,128]{4,0,3,2,1:T(2,128)(2,1)}, bf16[2,5,1,32,128]{4,0,3,2,1:T(2,128)(2,1)}, u32[]{:S(2)}, u32[]{:S(2)}) collective-permute-start(bf16[2,5,1,32,128]{4,0,3,2,1:T(2,128)(2,1)} %get-tuple-element.48), channel_id=1, source_target_pairs={{1,0},{2,1},{3,2},{4,3},{5,4},{6,5},{7,6},{8,7},{9,8},{10,9},{11,1... | collective-permute-start | bytes 245768 | tf_op jit(solution)/shard_map/ppermute | solution.py:25
  293.3 16.3 %collective-permute-done.10 = bf16[2,3,1,32,128]{4,3,2,1,0:T(8,128)(2,1)S(1)} collective-permute-done((bf16[2,3,1,32,128]{4,3,2,1,0:T(8,128)(2,1)S(1)}, bf16[2,3,1,32,128]{4,3,2,1,0:T(8,128)(2,1)S(1)}, u32[]{:S(2)}, u32[]{:S(2)}) %collective-permute-start.10) | collective-permute-done | bytes 49184 | tf_op jit(solution)/shard_map/ppermute | solution.py:24
  310.0 5.6 %convolution_bitcast_fusion.4 = f32[128,2,2,128]{3,2,1,0:T(2,128)S(1)} fusion(bf16[2,128,128,1]{2,0,3,1:T(2,128)(2,1)S(1)} %copy.438, bf16[128,2,128,128]{3,2,1,0:T(8,128)(2,1)} %param.9), kind=kOutput, calls=%fused_computation.86 | convolution fusion | flops 16777216 | bytes 8716288 | tf_op jit(solution)/shard_map/pcij,dpj->pcdi/dot_general | solution.py:173
  325.9 3.5 multiply_add_fusion
  335.1 3.2 copy.404
  343.1 3.1 maximum_multiply_fusion
  353.7 4.9 %fusion.537 = (f32[2,132,2,32]{2,1,3,0:T(8,128)}, f32[2,132,2,32]{2,1,3,0:T(8,128)}) fusion(f32[2,132,64,32]{2,1,3,0:T(8,128)S(1)} %pad_maximum_fusion.1), kind=kLoop, calls=%fused_computation.603 | loop fusion | bytes 270336 | tf_op jit(solution)/shard_map/slice | solution.py:22
  358.6 4.0 %copy.410 = f32[2,132,2,32]{1,3,2,0:T(8,128)S(1)} copy(f32[2,132,2,32]{2,1,3,0:T(8,128)} %get-tuple-element.10) | data formatting | bytes 135168 | tf_op jit(solution)/shard_map/slice | solution.py:22
  362.7 4.0 %copy.411 = f32[2,132,2,32]{1,3,2,0:T(8,128)S(1)} copy(f32[2,132,2,32]{2,1,3,0:T(8,128)} %get-tuple-element.11) | data formatting | bytes 135168 | tf_op jit(solution)/shard_map/slice | solution.py:23
  366.8 5.0 %collective-permute-start.7 = (f32[2,132,2,32]{1,3,2,0:T(8,128)S(1)}, f32[2,132,2,32]{1,3,2,0:T(8,128)S(1)}, u32[]{:S(2)}, u32[]{:S(2)}) collective-permute-start(f32[2,132,2,32]{1,3,2,0:T(8,128)S(1)} %copy.411), channel_id=1, source_target_pairs={{1,0},{2,1},{3,2},{4,3},{5,4},{6,5},{7,6},{8,7},{9,8},{10,9},{11,1... | collective-permute-start | bytes 202760 | tf_op jit(solution)/shard_map/ppermute | solution.py:25
  378.9 7.9 %fusion.13 = f32[2,32,4,68,32]{3,1,2,4,0:T(8,128)S(1)} fusion(f32[2,132,2,32]{2,1,3,0:T(8,128)} %copy.413, f32[2,2,64,32]{2,1,3,0:T(2,128)S(1)} %copy.409, f32[2,128,64,32]{2,1,3,0:T(8,128)} %copy-done.4, f32[2,2,64,32]{2,1,3,0:T(2,128)S(1)} %copy.408, f32[2,132,2,32]{2,1,3,0:T(8,128)} %copy.412, s32[32,4]{0,1:T(4,128)S(1)} %copy-done.13), kind=kOutput, calls=%fused_computation.19 | convolution fusion | flops 884691456 | bytes 4526592 | tf_op jit(solution)/shard_map/gxu,cuvw->cgxvw/dot_general | solution.py:227
  386.7 9.7 %fusion.44 = f32[2,32,4,4,32]{4,3,2,0,1:T(4,128)S(1)} fusion(f32[2,32,4,68,32]{3,1,2,4,0:T(8,128)S(1)} %fusion.13, s32[32,4]{1,0:T(8,128)S(1)} %iota_add_fusion), kind=kOutput, calls=%fused_computation.83 | convolution fusion | flops 26747392 | bytes 2359808 | tf_op jit(solution)/shard_map/gyv,cgxvw->cgxyw/dot_general | solution.py:228
  (216 shorter events, 174.3 us)
Async XLA Ops:
  2.0 6.2 %copy-start.10 = (s32[32,128]{1,0:T(8,128)}, s32[32,128]{1,0:T(8,128)S(1)}, u32[]{:S(2)}) copy-start(s32[32,128]{1,0:T(8,128)S(1)} %subtract_add_fusion) | copy-start | bytes 49156
  2.0 23.7 %copy-start.12 = (s32[32,4]{0,1:T(4,128)}, s32[32,4]{0,1:T(4,128)S(1)}, u32[]{:S(2)}) copy-start(s32[32,4]{0,1:T(4,128)S(1)} %iota_add_fusion.2) | copy-start | bytes 1540
  38.6 5.8 %collective-permute-start = (f32[2,2,68,32]{2,3,1,0:T(8,128)S(1)}, f32[2,2,68,32]{2,3,1,0:T(8,128)S(1)}, u32[]{:S(2)}, u32[]{:S(2)}) collective-permute-start(f32[2,2,68,32]{2,3,1,0:T(8,128)S(1)} %copy.323), channel_id=1, source_target_pairs={{0,16},{16,32},{32,48},{48,64},{64,80},{80,96},{96,112},{112,0},{1... | collective-permute-start | bytes 104456 | tf_op jit(solution)/shard_map/ppermute | solution.py:24
  44.5 3.7 collective-permute-start.1
  48.2 12.1 %slice-start = ((s8[4456448]{0:T(1024)(128)(4,1)}), s8[262144]{0:T(1024)(128)(4,1)S(1)}, s32[]{:S(2)}) async-start(s8[4456448]{0:T(1024)(128)(4,1)} %bitcast.371), calls=%async_computation.4 | async-start | bytes 524288
  51.3 8.9 %slice-start.1 = ((s8[4456448]{0:T(1024)(128)(4,1)}), s8[4194304]{0:T(1024)(128)(4,1)S(1)}, s32[]{:S(2)}) async-start(s8[4456448]{0:T(1024)(128)(4,1)} %bitcast.371), calls=%async_computation.5 | async-start | bytes 8388608
  51.3 8.9 %copy-start.2 = (f32[2,2,68,32]{1,3,2,0:T(8,128)S(1)}, f32[2,2,68,32]{1,3,2,0:T(8,128)}, u32[]{:S(2)}) copy-start(f32[2,2,68,32]{1,3,2,0:T(8,128)} %copy.325) | copy-start | bytes 104452
  51.3 8.9 %copy-start.3 = (f32[2,2,68,32]{1,3,2,0:T(8,128)S(1)}, f32[2,2,68,32]{1,3,2,0:T(8,128)}, u32[]{:S(2)}) copy-start(f32[2,2,68,32]{1,3,2,0:T(8,128)} %copy.326) | copy-start | bytes 104452
  52.7 7.5 %collective-permute-start.2 = (f32[2,136,2,32]{1,3,2,0:T(8,128)S(1)}, f32[2,136,2,32]{1,3,2,0:T(8,128)S(1)}, u32[]{:S(2)}, u32[]{:S(2)}) collective-permute-start(f32[2,136,2,32]{1,3,2,0:T(8,128)S(1)} %get-tuple-element.8), channel_id=1, source_target_pairs={{0,1},{1,2},{2,3},{3,4},{4,5},{5,6},{6,7},{7,8},{8,9},{9,10},{10,1... | collective-permute-start | bytes 208904 | tf_op jit(solution)/shard_map/ppermute | solution.py:24
  54.2 6.1 %collective-permute-start.3 = (f32[2,136,2,32]{1,3,2,0:T(8,128)S(1)}, f32[2,136,2,32]{1,3,2,0:T(8,128)S(1)}, u32[]{:S(2)}, u32[]{:S(2)}) collective-permute-start(f32[2,136,2,32]{1,3,2,0:T(8,128)S(1)} %get-tuple-element.9), channel_id=1, source_target_pairs={{1,0},{2,1},{3,2},{4,3},{5,4},{6,5},{7,6},{8,7},{9,8},{10,9},{11,1... | collective-permute-start | bytes 208904 | tf_op jit(solution)/shard_map/ppermute | solution.py:25
  58.0 13.0 %copy-start.7 = (f32[4,8]{0,1:T(8,128)}, f32[4,8]{0,1:T(8,128)S(1)}, u32[]{:S(2)}) copy-start(f32[4,8]{0,1:T(8,128)S(1)} %get-tuple-element.52) | copy-start | bytes 388
  81.0 31.6 %all-to-all-start = ((f32[2,128,64,32]{1,2,0,3:T(8,128)}), f32[2,128,64,32]{1,2,0,3:T(8,128)}, u32[]{:S(2)}, u32[]{:S(2)}) async-start(f32[2,128,64,32]{1,2,0,3:T(8,128)} %copy.337), calls=%async_computation | async-start | bytes 4194304 | tf_op jit(solution)/shard_map/all_to_all | solution.py:207
  133.3 39.7 %all-to-all-start.1 = ((f32[2,128,1024,2]{1,3,0,2:T(2,128)}), f32[2,128,1024,2]{1,3,0,2:T(2,128)}, u32[]{:S(2)}, u32[]{:S(2)}) async-start(f32[2,128,1024,2]{1,3,0,2:T(2,128)} %copy.352), calls=%async_computation.1 | async-start | bytes 4194304 | tf_op jit(solution)/shard_map/all_to_all | solution.py:210
  217.5 6.9 %copy-start.15 = (s32[1,128]{1,0:T(1,128)S(1)}, s32[1,128]{1,0:T(1,128)}, u32[]{:S(2)}) copy-start(s32[1,128]{1,0:T(1,128)} %param.10) | copy-start | bytes 1540
  217.5 31.7 %all-to-all-start.2 = ((f32[2,1024,128,2]{2,3,0,1:T(2,128)}), f32[2,1024,128,2]{2,3,0,1:T(2,128)}, u32[]{:S(2)}, u32[]{:S(2)}) async-start(f32[2,1024,128,2]{2,3,0,1:T(2,128)} %copy.377), calls=%async_computation.2 | async-start | bytes 4194304 | tf_op jit(solution)/shard_map/all_to_all | solution.py:221
  222.8 59.6 %collective-permute-start.8 = (bf16[2,1,1,32,128]{4,3,2,1,0:T(8,128)(2,1)S(1)}, bf16[2,1,1,32,128]{4,3,2,1,0:T(8,128)(2,1)S(1)}, u32[]{:S(2)}, u32[]{:S(2)}) collective-permute-start(bf16[2,1,1,32,128]{4,3,2,1,0:T(8,128)(2,1)S(1)} %bitcast.423), channel_id=1, source_target_pairs={{0,16},{16,32},{32,48},{48,64},{64,80},{80,96},{96,112},{112,0},{1... | collective-permute-start | bytes 49160 | tf_op jit(solution)/shard_map/ppermute | solution.py:24
  224.4 58.0 %collective-permute-start.9 = (bf16[2,1,1,32,128]{4,3,2,1,0:T(8,128)(2,1)S(1)}, bf16[2,1,1,32,128]{4,3,2,1,0:T(8,128)(2,1)S(1)}, u32[]{:S(2)}, u32[]{:S(2)}) collective-permute-start(bf16[2,1,1,32,128]{4,3,2,1,0:T(8,128)(2,1)S(1)} %bitcast.424), channel_id=1, source_target_pairs={{16,0},{32,16},{48,32},{64,48},{80,64},{96,80},{112,96},{0,112},{1... | collective-permute-start | bytes 49160 | tf_op jit(solution)/shard_map/ppermute | solution.py:25
  229.9 22.4 %copy-start.17 = (f32[128]{0:T(128)}, f32[128]{0:T(128)S(1)}, u32[]{:S(2)}) copy-start(f32[128]{0:T(128)S(1)} %compare_convert_fusion) | copy-start | bytes 1540
  276.1 39.7 %all-to-all-start.3 = ((f32[2,128,1024,2]{1,3,0,2:T(2,128)}), f32[2,128,1024,2]{1,3,0,2:T(2,128)}, u32[]{:S(2)}, u32[]{:S(2)}) async-start(f32[2,128,1024,2]{1,3,0,2:T(2,128)} %copy.390), calls=%async_computation.3 | async-start | bytes 4194304 | tf_op jit(solution)/shard_map/all_to_all | solution.py:224
  280.7 6.8 %collective-permute-start.12 = (bf16[2,1,3,32,128]{4,0,3,2,1:T(2,128)(2,1)S(1)}, bf16[2,1,3,32,128]{4,0,3,2,1:T(2,128)(2,1)S(1)}, u32[]{:S(2)}, u32[]{:S(2)}) collective-permute-start(bf16[2,1,3,32,128]{4,0,3,2,1:T(2,128)(2,1)S(1)} %get-tuple-element.49), channel_id=1, source_target_pairs={{0,16},{16,32},{32,48},{48,64},{64,80},{80,96},{96,112},{112,0},{1... | collective-permute-start | bytes 147464 | tf_op jit(solution)/shard_map/ppermute | solution.py:24
  281.7 5.7 %collective-permute-start.13 = (bf16[2,1,3,32,128]{4,0,3,2,1:T(2,128)(2,1)S(1)}, bf16[2,1,3,32,128]{4,0,3,2,1:T(2,128)(2,1)S(1)}, u32[]{:S(2)}, u32[]{:S(2)}) collective-permute-start(bf16[2,1,3,32,128]{4,0,3,2,1:T(2,128)(2,1)S(1)} %get-tuple-element.50), channel_id=1, source_target_pairs={{16,0},{32,16},{48,32},{64,48},{80,64},{96,80},{112,96},{0,112},{1... | collective-permute-start | bytes 147464 | tf_op jit(solution)/shard_map/ppermute | solution.py:25
  282.4 27.1 %collective-permute-start.10 = (bf16[2,3,1,32,128]{4,3,2,1,0:T(8,128)(2,1)S(1)}, bf16[2,3,1,32,128]{4,3,2,1,0:T(8,128)(2,1)S(1)}, u32[]{:S(2)}, u32[]{:S(2)}) collective-permute-start(bf16[2,3,1,32,128]{4,3,2,1,0:T(8,128)(2,1)S(1)} %constant_dynamic-update-slice_fusion), channel_id=1, source_target_pairs={{0,1},{1,2},{2,3},{3,4},{4,5},{5,6},{6,7},{7,8},{8,9},{9,10},{10,1... | collective-permute-start | bytes 147464 | tf_op jit(solution)/shard_map/ppermute | solution.py:24
  284.0 25.6 %collective-permute-start.11 = (bf16[2,3,1,32,128]{4,3,2,1,0:T(8,128)(2,1)S(1)}, bf16[2,3,1,32,128]{4,3,2,1,0:T(8,128)(2,1)S(1)}, u32[]{:S(2)}, u32[]{:S(2)}) collective-permute-start(bf16[2,3,1,32,128]{4,3,2,1,0:T(8,128)(2,1)S(1)} %constant_dynamic-update-slice_fusion), channel_id=1, source_target_pairs={{1,0},{2,1},{3,2},{4,3},{5,4},{6,5},{7,6},{8,7},{9,8},{10,9},{11,1... | collective-permute-start | bytes 147464 | tf_op jit(solution)/shard_map/ppermute | solution.py:25
  288.4 83.4 %collective-permute-start.14 = (bf16[2,5,1,32,128]{4,0,3,2,1:T(2,128)(2,1)}, bf16[2,5,1,32,128]{4,0,3,2,1:T(2,128)(2,1)}, u32[]{:S(2)}, u32[]{:S(2)}) collective-permute-start(bf16[2,5,1,32,128]{4,0,3,2,1:T(2,128)(2,1)} %get-tuple-element.47), channel_id=1, source_target_pairs={{0,1},{1,2},{2,3},{3,4},{4,5},{5,6},{6,7},{7,8},{8,9},{9,10},{10,1... | collective-permute-start | bytes 245768 | tf_op jit(solution)/shard_map/ppermute | solution.py:24
  288.4 83.4 %collective-permute-start.15 = (bf16[2,5,1,32,128]{4,0,3,2,1:T(2,128)(2,1)}, bf16[2,5,1,32,128]{4,0,3,2,1:T(2,128)(2,1)}, u32[]{:S(2)}, u32[]{:S(2)}) collective-permute-start(bf16[2,5,1,32,128]{4,0,3,2,1:T(2,128)(2,1)} %get-tuple-element.48), channel_id=1, source_target_pairs={{1,0},{2,1},{3,2},{4,3},{5,4},{6,5},{7,6},{8,7},{9,8},{10,9},{11,1... | collective-permute-start | bytes 245768 | tf_op jit(solution)/shard_map/ppermute | solution.py:25
  343.1 6.1 %copy-start.18 = (f32[128]{0:T(128)S(1)}, f32[128]{0:T(128)}, u32[]{:S(2)}) copy-start(f32[128]{0:T(128)} %copy-done.17) | copy-start | bytes 1540
  346.2 6.8 %copy-start.4 = (f32[2,128,64,32]{2,1,3,0:T(8,128)}, f32[2,128,64,32]{2,1,3,0:T(8,128)S(1)}, u32[]{:S(2)}) copy-start(f32[2,128,64,32]{2,1,3,0:T(8,128)S(1)} %maximum_multiply_fusion) | copy-start | bytes 6291460
  346.3 4.3 %collective-permute-start.4 = (f32[2,2,64,32]{2,3,1,0:T(8,128)S(1)}, f32[2,2,64,32]{2,3,1,0:T(8,128)S(1)}, u32[]{:S(2)}, u32[]{:S(2)}) collective-permute-start(f32[2,2,64,32]{2,3,1,0:T(8,128)S(1)} %copy.406), channel_id=1, source_target_pairs={{0,16},{16,32},{32,48},{48,64},{64,80},{80,96},{96,112},{112,0},{1... | collective-permute-start | bytes 98312 | tf_op jit(solution)/shard_map/ppermute | solution.py:24
  349.3 3.7 collective-permute-start.5
  362.6 10.3 %collective-permute-start.6 = (f32[2,132,2,32]{1,3,2,0:T(8,128)S(1)}, f32[2,132,2,32]{1,3,2,0:T(8,128)S(1)}, u32[]{:S(2)}, u32[]{:S(2)}) collective-permute-start(f32[2,132,2,32]{1,3,2,0:T(8,128)S(1)} %copy.410), channel_id=1, source_target_pairs={{0,1},{1,2},{2,3},{3,4},{4,5},{5,6},{6,7},{7,8},{8,9},{9,10},{10,1... | collective-permute-start | bytes 202760 | tf_op jit(solution)/shard_map/ppermute | solution.py:24
  366.8 9.2 %collective-permute-start.7 = (f32[2,132,2,32]{1,3,2,0:T(8,128)S(1)}, f32[2,132,2,32]{1,3,2,0:T(8,128)S(1)}, u32[]{:S(2)}, u32[]{:S(2)}) collective-permute-start(f32[2,132,2,32]{1,3,2,0:T(8,128)S(1)} %copy.411), channel_id=1, source_target_pairs={{1,0},{2,1},{3,2},{4,3},{5,4},{6,5},{7,6},{8,7},{9,8},{10,9},{11,1... | collective-permute-start | bytes 202760 | tf_op jit(solution)/shard_map/ppermute | solution.py:25
  386.7 10.8 %copy-start.11 = (s32[32,128]{1,0:T(8,128)S(1)}, s32[32,128]{1,0:T(8,128)}, u32[]{:S(2)}) copy-start(s32[32,128]{1,0:T(8,128)} %copy-done.10) | copy-start | bytes 49156
  (11 other events, 34.5 us)
where the time goes:
time: 406 us; the launch traced here: 403 us
  matrix products  141 us (35%)
  local copies, waits for them, and re-layouts  96.3 us (24%)
  waiting for transfers between devices  89.4 us (22%)
  starting transfers between devices  58.2 us (14%)
  other arithmetic  15.3 us (4%)
    all_to_all x1, waiting for transfers between devices, per_device(): lax.all_to_all(spectral, 'col', split_axis=3, concat_axis=2, tiled=True)  24.9 us
    all_to_all x1, waiting for transfers between devices, per_device(): lax.all_to_all(spectral, 'row', split_axis=2, concat_axis=1, tiled=True)  23.4 us
    ppermute x8, waiting for transfers between devices, with_halo(): before = lax.ppermute(last, axis, up)  19.5 us
    all_to_all x1, waiting for transfers between devices, per_device(): lax.all_to_all(spectral, 'row', split_axis=1, concat_axis=2, tiled=True)  18.7 us
    ppermute x8, starting transfers between devices, with_halo(): after = lax.ppermute(first, axis, down)  17.3 us
    slice x7, local copies, waits for them, and re-layouts, with_halo(): last = lax.slice_in_dim(value, length - width, length, axis=dim)  15.2 us
    dot_general x6, matrix products, dft_along(): jnp.einsum('ka,...ab->...kb', cos_one, imag_part, precision=high)  14.7 us
    all_to_all x1, starting transfers between devices, per_device(): lax.all_to_all(spectral, 'row', split_axis=2, concat_axis=1, tiled=True)  13.2 us
  transfers between devices with their start and end apart: 20, of which 8 were waited for; matrix products, arithmetic and copies ran while one was open for 24% of the time, Pallas kernels for 0%

commit v1 on v0

v1 whole, which is shorter than its diff:
```python
import math

import jax
import jax.numpy as jnp
import ml_dtypes
import numpy as np
from jax import lax
from jax.experimental import pallas as pl
from jax.experimental.pallas import tpu as pltpu
from jax.sharding import PartitionSpec as P

N = 1024
NGZ = 32
NROW = 8
NCOL = 16
NB = 32
BLK = 128
XR = 144
WIDE_Y = 68
BF = jnp.bfloat16
F32 = jnp.float32
VMEM_LIMIT = 60 * 1024 * 1024


def bf(a):
    return np.asarray(a, dtype=np.float64).astype(ml_dtypes.bfloat16)


def split_np(a):
    high = bf(a)
    return high, bf(a - high.astype(np.float64))


def grid_tables():
    index = np.arange(N)[:, None] * np.arange(N)[None, :] % N
    angle = index * (2.0 * math.pi / N)
    return bf(np.cos(angle)), bf(np.sin(angle))


def depth_tables():
    index = np.arange(NGZ)[:, None] * np.arange(NGZ)[None, :] % NGZ
    angle = index * (2.0 * math.pi / NGZ)
    eye = np.eye(16)
    cos_high, cos_low = split_np(np.kron(np.cos(angle), eye))
    sin_high, sin_low = split_np(np.kron(np.sin(angle), eye))
    return cos_high, cos_low, sin_high, sin_low


def spread_table():
    lane = np.arange(128)[:, None]
    plane, ex, b = lane // 16, lane // 4 % 4, lane % 4
    wide = np.arange(2048)[None, :]
    hits = (wide // 512 == ex) & (wide // 128 % 4 == plane) & ((wide + 2) % 4 == b) & (lane < 64)
    return bf(hits.astype(np.float64))


def dot(a, b):
    return jnp.dot(a, b, preferred_element_type=F32)


def dot_nt(a, b):
    return lax.dot_general(a, b, (((1,), (1,)), ((), ())), preferred_element_type=F32)


def iota(shape, dim):
    return lax.broadcasted_iota(jnp.int32, shape, dim)


def high_low(a):
    high = a.astype(BF)
    return high, (a - high.astype(F32)).astype(BF)


def rows_high_low(a):
    high = a.astype(BF).astype(F32)
    return jnp.concatenate([high, a - high], axis=0).astype(BF)


def cell_codes(cells):
    z = cells & (NGZ - 1)
    t = cells >> 5
    x = (t * 15421) >> 20
    y = t - x * WIDE_Y
    corner_x = jnp.min(x, axis=1, keepdims=True)
    corner_y = jnp.min(y, axis=1, keepdims=True)
    code = z * 16 + (x - corner_x) * 4 + (y & 3)
    return code, corner_x, corner_y


def one_hot_rows(code_row):
    return jnp.where(iota((512, 128), 0) == code_row, 1.0, 0.0).astype(BF)


def project_kernel(cur, proj, cells, tch, tcl, tsh, tsl, out, codes, boxed):
    code, corner_x, corner_y = cell_codes(cells[...])
    codes[...] = code

    def block(i, carry):
        for u in range(4):
            g = i * 4 + u
            lhs = rows_high_low(cur[g])
            p_high, p_low = high_low(proj[g])
            first = dot_nt(lhs, p_high)
            values = first[0:2] + first[2:4] + dot_nt(lhs, p_low)[0:2]
            hot = one_hot_rows(codes[pl.ds(g, 1), :])
            placed = dot_nt(rows_high_low(values), hot)
            boxed[pl.ds(g, 1), :] = placed[0:1] + placed[2:3]
            boxed[pl.ds(NB + g, 1), :] = placed[1:2] + placed[3:4]
        return carry

    lax.fori_loop(0, NB // 4, block, 0)
    b_high, b_low = high_low(boxed[...])
    along_cos = dot(b_high, tch[...]) + dot(b_low, tch[...]) + dot(b_high, tcl[...])
    along_sin = dot(b_high, tsh[...]) + dot(b_low, tsh[...]) + dot(b_high, tsl[...])
    real = along_cos[:NB] + along_sin[NB:]
    imag = along_cos[NB:] - along_sin[:NB]
    lane = iota((NB, 64), 1)
    corners = jnp.where(lane == 0, corner_x, jnp.where(lane == 1, corner_y, 0)).astype(F32)
    for c in range(NCOL):
        part = slice(32 * c, 32 * c + 32)
        out[c] = jnp.concatenate([real[:, part], imag[:, part], corners], axis=1).astype(BF)


def local_x_of_row(shape, dim):
    row = iota(shape, dim)
    return jnp.where(row < 130, row + 2, jnp.where(row >= 142, row - 142, -64))


def store_starts(recv, starts):
    block = iota((512, 1), 0)
    start = recv[:, 65:66].astype(jnp.int32) + (block // NB) * 64 - 2
    starts[NB : NB + 512, :] = jnp.broadcast_to(start, (512, 128))
    starts[0:NB, :] = starts[512 : 512 + NB, :]
    starts[NB + 512 :, :] = starts[NB : 2 * NB, :]


def chunk_mask(starts, q):
    cell = 128 * q + iota((128, 128), 1)
    inside = ((cell - starts[64 * q : 64 * q + 128, :]) & (N - 1)) < 4
    return jnp.where(inside, 1.0, 0.0)


def image_kernel(recv, spread, cos, sin, out, wide, starts, img):
    def spread_rows(i, carry):
        rows = pl.ds(pl.multiple_of(i * 128, 128), 128)
        wide_rows = pl.ds(pl.multiple_of(i * 128 + NB, NB), 128)
        wide[wide_rows, :] = dot(recv[rows, :], spread[...]).astype(BF)
        return carry

    lax.fori_loop(0, 4, spread_rows, 0)
    wide[0:NB, :] = wide[512 : 512 + NB, :]
    wide[NB + 512 :, :] = wide[NB : 2 * NB, :]
    store_starts(recv, starts)
    pick = jnp.where(iota((16, 128), 1) == 64, 1.0, 0.0).astype(BF)
    corner = dot_nt(pick, recv[...])[0:8]
    corner = jnp.concatenate([corner[:, 480:], corner, corner[:, :NB]], axis=1)
    local_x = local_x_of_row((XR, 128), 0)
    for q in range(8):
        mask = chunk_mask(starts, q).astype(BF)
        mask = jnp.concatenate([mask] * 4, axis=1)
        corner_q = corner[0:1, 64 * q : 64 * q + 128].astype(jnp.int32)
        offset = local_x - corner_q
        lhs = [jnp.where(offset == ex, 1.0, 0.0).astype(BF) for ex in range(4)]
        rhs = [wide[64 * q : 64 * q + 128, 512 * ex : 512 * ex + 512] * mask for ex in range(4)]
        cells = dot(jnp.concatenate(lhs, axis=1), jnp.concatenate(rhs, axis=0)).astype(BF)
        for p in range(4):
            img[XR * p : XR * p + XR, 128 * q : 128 * q + 128] = cells[:, 128 * p : 128 * p + 128]

    def along_y(i, carry):
        lanes = pl.ds(pl.multiple_of(i * 256, 256), 256)
        real, imag = img[0 : 2 * XR, :], img[2 * XR :, :]
        cos_i, sin_i = cos[:, lanes], sin[:, lanes]
        out_real = (dot(real, cos_i) + dot(imag, sin_i)).astype(BF)
        out_imag = (dot(imag, cos_i) - dot(real, sin_i)).astype(BF)
        for j in range(2):
            out[2 * i + j, 0 : 2 * XR, :] = out_real[:, 128 * j : 128 * j + 128]
            out[2 * i + j, 2 * XR :, :] = out_imag[:, 128 * j : 128 * j + 128]
        return carry

    lax.fori_loop(0, 4, along_y, 0)


def spectrum_kernel(recv, green, cos, sin, out, d_one, d_two, h_one, h_two):
    low_rows = iota((16, 128), 0) < 8
    for r in range(NROW):
        before, after = (r - 1) % NROW, (r + 1) % NROW
        for p in range(4):
            base = XR * p
            main = recv[r, base : base + 128, :]
            lower = recv[before, base + 128 : base + XR, :].astype(F32)
            upper = recv[after, base + 128 : base + XR, :].astype(F32)
            head = main[0:16].astype(F32) + jnp.where(low_rows, lower, 0.0)
            tail = main[112:128].astype(F32) + jnp.where(low_rows, 0.0, upper)
            band = jnp.concatenate([head.astype(BF), main[16:112], tail.astype(BF)], axis=0)
            d_one[128 * r : 128 * r + 128, 128 * p : 128 * p + 128] = band
            if p < 2:
                d_two[128 * r : 128 * r + 128, 256 + 128 * p : 384 + 128 * p] = -band
            else:
                d_two[128 * r : 128 * r + 128, 128 * p - 256 : 128 * p - 128] = band

    def forward(i, carry):
        rows = pl.ds(pl.multiple_of(i * 256, 256), 256)
        spec = dot(cos[rows, :], d_one[...]) + dot(sin[rows, :], d_two[...])
        real, imag = spec[:, :256], spec[:, 256:]
        g_real, g_imag = green[0, rows, :], green[1, rows, :]
        h_real = (real * g_real - imag * g_imag).astype(BF)
        h_imag = (real * g_imag + imag * g_real).astype(BF)
        h_one[rows, 0:256] = h_real
        h_one[rows, 256:512] = h_imag
        h_two[rows, 0:256] = -h_imag
        h_two[rows, 256:512] = h_real
        return carry

    lax.fori_loop(0, 4, forward, 0)

    def inverse(i, carry):
        rows = pl.ds(pl.multiple_of(i * 256, 256), 256)
        back = (dot(cos[rows, :], h_one[...]) + dot(sin[rows, :], h_two[...])).astype(BF)
        for j in range(2):
            for p in range(4):
                out[2 * i + j, XR * p : XR * p + 128, :] = back[
                    128 * j : 128 * j + 128, 128 * p : 128 * p + 128
                ]
        return carry

    lax.fori_loop(0, 4, inverse, 0)
    for r in range(NROW):
        before, after = (r - 1) % NROW, (r + 1) % NROW
        for p in range(4):
            base = XR * p
            above = out[after, base : base + 16, :].astype(F32)
            below = out[before, base + 112 : base + 128, :].astype(F32)
            out[r, base + 128 : base + XR, :] = jnp.where(low_rows, above, below).astype(BF)


def gather_kernel(recv, near_info, spread, cos, sin, out, spec, pot, starts, hot, acc):
    for r in range(NROW):
        spec[:, 128 * r : 128 * r + 128] = recv[r]

    def along_y(i, carry):
        lanes = pl.ds(pl.multiple_of(i * 256, 256), 256)
        real, imag = spec[0 : 2 * XR, :], spec[2 * XR :, :]
        cos_i, sin_i = cos[:, lanes], sin[:, lanes]
        pot[0 : 2 * XR, lanes] = (dot(real, cos_i) - dot(imag, sin_i)).astype(BF)
        pot[2 * XR :, lanes] = (dot(imag, cos_i) + dot(real, sin_i)).astype(BF)
        return carry

    lax.fori_loop(0, 4, along_y, 0)
    store_starts(near_info, starts)
    local_x = local_x_of_row((512, XR), 1)
    offset = local_x - near_info[:, 64:65].astype(jnp.int32)
    for ex in range(4):
        hot[ex, NB : NB + 512, :] = jnp.where(offset == ex, 1.0, 0.0).astype(BF)
    hot[:, 0:NB, :] = hot[:, 512 : 512 + NB, :]
    hot[:, NB + 512 :, :] = hot[:, NB : 2 * NB, :]
    acc[...] = jnp.zeros_like(acc)
    for q in range(8):
        mask = chunk_mask(starts, q)
        mask = jnp.concatenate([mask] * 4, axis=1)
        cells = [pot[XR * p : XR * p + XR, 128 * q : 128 * q + 128] for p in range(4)]
        cells = jnp.concatenate(cells, axis=1)
        rows = slice(64 * q, 64 * q + 128)
        for ex in range(4):
            taken = (dot(hot[ex, rows, :], cells) * mask).astype(BF)
            lanes = slice(512 * ex, 512 * ex + 512)
            acc[rows, lanes] = acc[rows, lanes] + taken
    acc[512 : 512 + NB, :] = acc[512 : 512 + NB, :] + acc[0:NB, :]
    acc[NB : 2 * NB, :] = acc[NB : 2 * NB, :] + acc[NB + 512 :, :]

    def fold(i, carry):
        rows = pl.ds(pl.multiple_of(i * 128, 128), 128)
        wide_rows = pl.ds(pl.multiple_of(i * 128 + NB, NB), 128)
        out[rows, :] = dot_nt(acc[wide_rows, :], spread[...]).astype(BF)
        return carry

    lax.fori_loop(0, 4, fold, 0)


def back_kernel(recv, proj, cells, near, tch, tcl, tsh, tsl, out, codes, box_real, box_imag):
    code, _, _ = cell_codes(cells[...])
    codes[...] = code
    real = jnp.concatenate([recv[c, :, 0:32] for c in range(NCOL)], axis=1)
    imag = jnp.concatenate([recv[c, :, 32:64] for c in range(NCOL)], axis=1)
    both = jnp.concatenate([real, imag], axis=0)
    along_cos = dot(both, tch[...]) + dot(both, tcl[...])
    along_sin = dot(both, tsh[...]) + dot(both, tsl[...])
    box_real[...] = along_cos[:NB] - along_sin[NB:]
    box_imag[...] = along_cos[NB:] + along_sin[:NB]

    def block(i, carry):
        for u in range(4):
            g = i * 4 + u
            box = jnp.concatenate([box_real[pl.ds(g, 1), :], box_imag[pl.ds(g, 1), :]], axis=0)
            hot = one_hot_rows(codes[pl.ds(g, 1), :])
            picked = dot(rows_high_low(box), hot)
            lhs = rows_high_low(picked[0:2] + picked[2:4])
            p_high, p_low = high_low(proj[g])
            first = dot(lhs, p_high)
            out[g] = first[0:2] + first[2:4] + dot(lhs, p_low)[0:2] + near[g]
        return carry

    lax.fori_loop(0, NB // 4, block, 0)


def call(kernel, out_shape, scratch, *args):
    return pl.pallas_call(
        kernel,
        out_shape=out_shape,
        in_specs=[pl.BlockSpec(memory_space=pltpu.VMEM)] * len(args),
        out_specs=pl.BlockSpec(memory_space=pltpu.VMEM),
        scratch_shapes=scratch,
        compiler_params=pltpu.CompilerParams(vmem_limit_bytes=VMEM_LIMIT),
    )(*args)


def with_halo(value, sides, width):
    for axis, dim in sides:
        peers, length = (lax.axis_size(axis), value.shape[dim])
        up = [(i, (i + 1) % peers) for i in range(peers)]
        down = [(j, i) for i, j in up]
        last = lax.slice_in_dim(value, length - width, length, axis=dim)
        first = lax.slice_in_dim(value, 0, width, axis=dim)
        before = lax.ppermute(last, axis, up)
        after = lax.ppermute(first, axis, down)
        value = jnp.concatenate([before, value, after], axis=dim)
    return value


def combine_parts(products):
    return jnp.stack(
        [products[:, 0, 0] - products[:, 1, 1], products[:, 0, 1] + products[:, 1, 0]], axis=1
    )


def fold_rims(field, axis_pos, inner, width):
    middle = lax.slice_in_dim(field, 2 * width, 2 * width + inner, axis=axis_pos)
    lower = lax.slice_in_dim(field, 0, width, axis=axis_pos)
    upper = lax.slice_in_dim(field, inner + 3 * width, inner + 4 * width, axis=axis_pos)
    lower_pads = [(0, 0)] * field.ndim
    upper_pads = [(0, 0)] * field.ndim
    lower_pads[axis_pos] = (0, inner - width)
    upper_pads[axis_pos] = (inner - width, 0)
    return middle + jnp.pad(lower, lower_pads) + jnp.pad(upper, upper_pads)


def near_part(blocks, near_blocks, pair_local, pair_ghost, pair_counts):
    num_blocks, block_len = NB, BLK
    pair_slots = pair_ghost.shape[1]
    high = lax.Precision.HIGHEST
    local_bf = blocks.astype(BF)
    beside_all = with_halo(
        local_bf.reshape(2, 1, 1, num_blocks, block_len), (("row", 1), ("col", 2)), 1
    )
    beside_all = beside_all.reshape(2, 9 * num_blocks, block_len)
    picks = pair_ghost[0]
    owned = pair_local[0]
    living = (jnp.arange(pair_slots, dtype=jnp.int32) < pair_counts[0]).astype(F32)
    owner_table = owned[:, None] == jnp.arange(num_blocks, dtype=jnp.int32)[None, :]
    ghost_table = picks[:, None] == jnp.arange(9 * num_blocks, dtype=jnp.int32)[None, :]
    remote_vals = jnp.einsum(
        "ho,som->shm", ghost_table.astype(BF), beside_all, preferred_element_type=F32
    ).astype(BF)
    local_vals = jnp.einsum(
        "ho,som->shm", owner_table.astype(BF), local_bf, preferred_element_type=F32
    ).astype(BF)
    onward = jnp.einsum("pcij,dpj->pcdi", near_blocks, remote_vals, preferred_element_type=F32)
    backward = jnp.einsum("pcij,dpi->pcdj", near_blocks, local_vals, preferred_element_type=F32)
    onward = combine_parts(onward) * living[:, None, None]
    backward = combine_parts(backward) * living[:, None, None]
    near_own = jnp.einsum("pn,pcb->cnb", owner_table.astype(F32), onward, precision=high)
    spread_back = jnp.einsum("pn,pcb->cnb", ghost_table.astype(F32), backward, precision=high)
    spread_back = spread_back.reshape(2, 3, 3, num_blocks, block_len)
    widened_back = with_halo(spread_back.astype(BF), (("row", 1), ("col", 2)), 1).astype(F32)
    returned = fold_rims(fold_rims(widened_back, 1, 1, 1), 2, 1, 1).reshape(
        2, num_blocks, block_len
    )
    return near_own + returned


def per_device(
    currents, near_blocks, pair_local, pair_ghost, pair_counts, projection, stencil_cells, green
):
    cos, sin = (jnp.asarray(t) for t in grid_tables())
    depth = [jnp.asarray(t) for t in depth_tables()]
    spread = jnp.asarray(spread_table())
    shape = jax.ShapeDtypeStruct
    blocks = currents.reshape(2, NB, BLK)
    near = near_part(blocks, near_blocks, pair_local, pair_ghost, pair_counts)
    messages = call(
        project_kernel,
        shape((NCOL, NB, 128), BF),
        [pltpu.VMEM((NB, 128), jnp.int32), pltpu.VMEM((2 * NB, 512), F32)],
        jnp.transpose(blocks, (1, 0, 2)),
        projection,
        stencil_cells,
        *depth,
    )
    sources = lax.all_to_all(messages, "col", split_axis=0, concat_axis=0, tiled=True)
    sources = sources.reshape(NCOL * NB, 128)
    bands = call(
        image_kernel,
        shape((NROW, 4 * XR, 128), BF),
        [
            pltpu.VMEM((512 + 2 * NB, 2048), BF),
            pltpu.VMEM((512 + 2 * NB, 128), jnp.int32),
            pltpu.VMEM((4 * XR, N), BF),
        ],
        sources,
        spread,
        cos,
        sin,
    )
    pencils = lax.all_to_all(bands, "row", split_axis=0, concat_axis=0, tiled=True)
    turned = jnp.transpose(green, (0, 3, 1, 2)).reshape(2, N, 256) * (1.0 / (N * N * NGZ))
    pencils = call(
        spectrum_kernel,
        shape((NROW, 4 * XR, 128), BF),
        [pltpu.VMEM((N, 512), BF)] * 4,
        pencils,
        turned,
        cos,
        sin,
    )
    bands = lax.all_to_all(pencils, "row", split_axis=0, concat_axis=0, tiled=True)
    taken = call(
        gather_kernel,
        shape((NCOL * NB, 128), BF),
        [
            pltpu.VMEM((4 * XR, N), BF),
            pltpu.VMEM((4 * XR, N), BF),
            pltpu.VMEM((512 + 2 * NB, 128), jnp.int32),
            pltpu.VMEM((4, 512 + 2 * NB, XR), BF),
            pltpu.VMEM((512 + 2 * NB, 2048), BF),
        ],
        bands,
        sources,
        spread,
        cos,
        sin,
    )
    messages = lax.all_to_all(
        taken.reshape(NCOL, NB, 128), "col", split_axis=0, concat_axis=0, tiled=True
    )
    total = call(
        back_kernel,
        shape((NB, 2, BLK), F32),
        [pltpu.VMEM((NB, 128), jnp.int32), pltpu.VMEM((NB, 512), F32), pltpu.VMEM((NB, 512), F32)],
        messages,
        projection,
        stencil_cells,
        jnp.transpose(near, (1, 0, 2)),
        *depth,
    )
    return jnp.transpose(total, (1, 0, 2)).reshape(2, NB * BLK)


def solution(mesh):
    in_specs = (
        P(None, ("row", "col")),
        P(("row", "col"), None, None, None),
        P(("row", "col"), None),
        P(("row", "col"), None),
        P(("row", "col")),
        P(("row", "col"), None, None),
        P(("row", "col"), None),
        P(None, "col", "row", None),
    )
    out_specs = P(None, ("row", "col"))
    return jax.shard_map(
        per_device, mesh=mesh, in_specs=in_specs, out_specs=out_specs, check_vma=False
    )
```

time: 406 us -> 131 us (0.32)
  matrix products: 141 us -> 11.3 us
  local copies, waits for them, and re-layouts: 96.3 us -> 9.37 us
  waiting for transfers between devices: 89.4 us -> 15.7 us
  Pallas kernels: 0 us -> 47.7 us
  starting transfers between devices: 58.2 us -> 38.3 us
  other arithmetic: 15.3 us -> 5.71 us
    dot_general x64 -> x6, matrix products: 141 us -> 11.3 us  [the longest x1 5.65 us: near_part(): jnp.einsum('pcij,dpj->pcdi', near_blocks, remote_vals, preferred_element_...]
    all_to_all x4, waiting for transfers between devices: 67 us -> 15.3 us  [the longest x1 9.15 us: per_device(): lax.all_to_all(pencils, 'row', split_axis=0, concat_axis=0, tiled=True)]
    pallas_call x0 -> x5, Pallas kernels: none -> 47.7 us  [call(): pl.pallas_call(kernel, out_shape=out_shape, in_specs=[pl.BlockSpec(memory...]
    transpose x6 -> x0, local copies, waits for them, and re-layouts: 20.6 us -> none  [the longest x1 11.1 us: per_device(): placed_y = jnp.einsum('gyv,cgxyw->cgxvw', hits_y, placed_z, precision=high)]
    ppermute x8 -> x4, waiting for transfers between devices: 19.5 us -> 0.38 us  [with_halo(): before = lax.ppermute(last, axis, up)]
    all_to_all x6 -> x0, local copies, waits for them, and re-layouts: 15.7 us -> none  [the longest x2 6.2 us: per_device(): lax.all_to_all(spectral, 'row', split_axis=1, concat_axis=2, tiled=True)]
    slice x7 -> x1, local copies, waits for them, and re-layouts: 15.2 us -> 0.71 us  [with_halo(): last = lax.slice_in_dim(value, length - width, length, axis=dim)]
    ppermute x6 -> x0, local copies, waits for them, and re-layouts: 12.3 us -> none  [the longest x3 6.18 us: with_halo(): before = lax.ppermute(last, axis, up)]
  transfers between devices with their start and end apart: 20 -> 12, of which waited for: 8 -> 3; matrix products, arithmetic and copies ran while one was open for 24% -> 16% of each run, Pallas kernels for 0% -> 22%
where the time goes in v1:
time: 131 us; the launch traced here: 129 us
  Pallas kernels  47.7 us (36%)
  starting transfers between devices  38.3 us (29%)
  waiting for transfers between devices  15.7 us (12%)
  matrix products  11.3 us (9%)
  local copies, waits for them, and re-layouts  9.37 us (7%)
  other arithmetic  5.71 us (4%)
    pallas_call x5, Pallas kernels, call(): pl.pallas_call(kernel, out_shape=out_shape, in_specs=[pl.BlockSpec(memory...  47.7 us
    ppermute x4, starting transfers between devices, with_halo(): after = lax.ppermute(first, axis, down)  12.1 us
    all_to_all x1, waiting for transfers between devices, per_device(): lax.all_to_all(pencils, 'row', split_axis=0, concat_axis=0, tiled=True)  9.15 us
    all_to_all x1, starting transfers between devices, per_device(): lax.all_to_all(messages, 'col', split_axis=0, concat_axis=0, tiled=True)  6.76 us
    all_to_all x1, starting transfers between devices, per_device(): lax.all_to_all(pencils, 'row', split_axis=0, concat_axis=0, tiled=True)  6.23 us
    all_to_all x1, waiting for transfers between devices, per_device(): lax.all_to_all(taken.reshape(NCOL, NB, 128), 'col', split_axis=0, concat_...  6.19 us
    unnamed x28, local copies, waits for them, and re-layouts  5.95 us
    dot_general x1, matrix products, near_part(): jnp.einsum('pcij,dpj->pcdi', near_blocks, remote_vals, preferred_element_...  5.65 us
  transfers between devices with their start and end apart: 12, of which 3 were waited for; matrix products, arithmetic and copies ran while one was open for 16% of the time, Pallas kernels for 22%

profile of v1, /device:TPU:1, one launch (start us, length us, event | category | flops | bytes accessed | tf_op | source)
XLA Modules:
  0.0 129.0 jit_solution(4204531092088913215)
XLA Ops:
  0.0 0.9 convert_bitcast_fusion
  0.9 0.6 copy-done.4
  1.5 0.6 copy.49
  2.1 3.0 %collective-permute-start = (bf16[2,1,1,32,128]{4,3,2,1,0:T(8,128)(2,1)}, bf16[2,1,1,32,128]{4,3,2,1,0:T(8,128)(2,1)}, u32[]{:S(2)}, u32[]{:S(2)}) collective-permute-start(bf16[2,1,1,32,128]{4,3,2,1,0:T(8,128)(2,1)} %bitcast.75), channel_id=1, source_target_pairs={{0,16},{16,32},{32,48},{48,64},{64,80},{80,96},{96,112},{112,0},{1... | collective-permute-start | bytes 49160 | tf_op jit(solution)/shard_map/ppermute | solution.py:323
  5.1 9.8 %shard_map.145 = bf16[16,32,128]{2,1,0:T(8,128)(2,1)} custom-call(f32[32,2,128]{2,1,0:T(2,128)} %bitcast.89, f32[32,128,128]{2,1,0:T(8,128)} %proj.3, s32[32,128]{1,0:T(8,128)} %cells.3, bf16[512,512]{1,0:T(8,128)(2,1)} %constant.19.clone.tch, bf16[512,512]{1,0:T(8,128)(2,1)} %constant.20.clone.tcl, bf16[512,512]{1,0:T(8,128)(2,1)} %constant.21.clone.tsh, ...), custom_call_target="tpu_custom_call" | custom-call | tf_op jit(solution)/shard_map/pallas_call | solution.py:306
  14.9 6.8 %all-to-all-start = ((bf16[16,32,128]{2,1,0:T(8,128)(2,1)}), bf16[16,32,128]{2,1,0:T(8,128)(2,1)S(1)}, u32[]{:S(2)}, u32[]{:S(2)}) async-start(bf16[16,32,128]{2,1,0:T(8,128)(2,1)} %shard_map.145), calls=%async_computation | async-start | bytes 262144 | tf_op jit(solution)/shard_map/all_to_all | solution.py:398
  21.9 4.6 %fusion.12 = f32[128,2,2,128]{3,1,2,0:T(2,128)S(1)} fusion(bf16[128,2,128,128]{3,2,1,0:T(8,128)(2,1)} %param.16, bf16[128,2,128]{2,0,1:T(8,128)(2,1)S(1)} %convolution_convert_fusion.1), kind=kOutput, calls=%fused_computation.29 | convolution fusion | flops 16777216 | bytes 8716288 | tf_op jit(solution)/shard_map/pcij,dpi->pcdj/dot_general | solution.py:367
  28.2 0.7 fusion.30
  28.9 2.2 %collective-permute-start.5 = (bf16[2,1,3,32,128]{4,0,3,2,1:T(2,128)(2,1)}, bf16[2,1,3,32,128]{4,0,3,2,1:T(2,128)(2,1)}, u32[]{:S(2)}, u32[]{:S(2)}) collective-permute-start(bf16[2,1,3,32,128]{4,0,3,2,1:T(2,128)(2,1)} %get-tuple-element.13), channel_id=1, source_target_pairs={{16,0},{32,16},{48,32},{64,48},{80,64},{96,80},{112,96},{0,112},{1... | collective-permute-start | bytes 147464 | tf_op jit(solution)/shard_map/ppermute | solution.py:324
  31.2 0.6 copy-done.2
  31.8 8.9 %shard_map.146 = bf16[8,576,128]{2,1,0:T(8,128)(2,1)} custom-call(bf16[512,128]{1,0:T(8,128)(2,1)} %bitcast.81, bf16[128,2048]{1,0:T(8,128)(2,1)} %constant.23.clone.spread, bf16[1024,1024]{1,0:T(8,128)(2,1)} %constant.7.clone.cos, bf16[1024,1024]{1,0:T(8,128)(2,1)} %constant.18.clone.sin), custom_call_target="tpu_custom_call" | custom-call | tf_op jit(solution)/shard_map/pallas_call | solution.py:306
  40.7 4.8 %all-to-all-start.1 = ((bf16[8,576,128]{2,1,0:T(8,128)(2,1)}), bf16[8,576,128]{2,1,0:T(8,128)(2,1)S(1)}, u32[]{:S(2)}, u32[]{:S(2)}) async-start(bf16[8,576,128]{2,1,0:T(8,128)(2,1)} %shard_map.146), calls=%async_computation.1 | async-start | bytes 2359296 | tf_op jit(solution)/shard_map/all_to_all | solution.py:413
  45.5 1.8 %broadcast_multiply_fusion = f32[2,2,128,1024]{3,2,1,0:T(8,128)S(1)} fusion(f32[2,2,128,1024]{3,2,1,0:T(8,128)} %param.22), kind=kLoop, calls=%fused_computation.5 | loop fusion | flops 524288 | bytes 4194304 | tf_op jit(solution)/shard_map/mul | solution.py:414
  47.3 1.9 %copy.33.green = f32[2,1024,256]{2,1,0:T(8,128)} copy(f32[2,1024,256]{1,2,0:T(8,128)S(1)} %bitcast.77) | data formatting | bytes 4194304 | tf_op jit(solution)/shard_map/mul | solution.py:414
  49.1 0.7 constant_dynamic-update-slice_fusion.2
  49.9 0.7 constant_dynamic-update-slice_fusion
  50.6 5.0 %collective-permute-start.3 = (bf16[2,3,1,32,128]{4,3,2,1,0:T(8,128)(2,1)S(1)}, bf16[2,3,1,32,128]{4,3,2,1,0:T(8,128)(2,1)S(1)}, u32[]{:S(2)}, u32[]{:S(2)}) collective-permute-start(bf16[2,3,1,32,128]{4,3,2,1,0:T(8,128)(2,1)S(1)} %constant_dynamic-update-slice_fusion), channel_id=1, source_target_pairs={{1,0},{2,1},{3,2},{4,3},{5,4},{6,5},{7,6},{8,7},{9,8},{10,9},{11,1... | collective-permute-start | bytes 147464 | tf_op jit(solution)/shard_map/ppermute | solution.py:324
  55.6 1.0 pad_maximum_fusion.7
  56.6 4.8 %collective-permute-start.7 = (bf16[2,5,1,32,128]{4,0,3,2,1:T(2,128)(2,1)S(1)}, bf16[2,5,1,32,128]{4,0,3,2,1:T(2,128)(2,1)S(1)}, u32[]{:S(2)}, u32[]{:S(2)}) collective-permute-start(bf16[2,5,1,32,128]{4,0,3,2,1:T(2,128)(2,1)S(1)} %get-tuple-element.11), channel_id=1, source_target_pairs={{1,0},{2,1},{3,2},{4,3},{5,4},{6,5},{7,6},{8,7},{9,8},{10,9},{11,1... | collective-permute-start | bytes 245768 | tf_op jit(solution)/shard_map/ppermute | solution.py:324
  62.3 1.0 copy-done
  63.3 10.2 %shard_map.147 = bf16[8,576,128]{2,1,0:T(8,128)(2,1)} custom-call(bf16[8,576,128]{2,1,0:T(8,128)(2,1)} %copy-done, f32[2,1024,256]{2,1,0:T(8,128)} %copy.33.green, bf16[1024,1024]{1,0:T(8,128)(2,1)} %constant.7.clone.cos, bf16[1024,1024]{1,0:T(8,128)(2,1)} %constant.18.clone.sin), custom_call_target="tpu_custom_call" | custom-call | tf_op jit(solution)/shard_map/pallas_call | solution.py:306
  73.6 6.2 %all-to-all-start.2 = ((bf16[8,576,128]{2,1,0:T(8,128)(2,1)}), bf16[8,576,128]{2,1,0:T(8,128)(2,1)S(1)}, u32[]{:S(2)}, u32[]{:S(2)}) async-start(bf16[8,576,128]{2,1,0:T(8,128)(2,1)} %shard_map.147), calls=%async_computation.2 | async-start | bytes 2359296 | tf_op jit(solution)/shard_map/all_to_all | solution.py:424
  79.8 5.6 %convolution_bitcast_fusion = f32[128,2,2,128]{3,2,1,0:T(2,128)S(1)} fusion(bf16[128,2,128,128]{3,2,1,0:T(8,128)(2,1)} %param.16, bf16[2,128,128]{1,0,2:T(2,128)(2,1)S(1)} %copy.37), kind=kOutput, calls=%fused_computation | convolution fusion | flops 16777216 | bytes 8716288 | tf_op jit(solution)/shard_map/pcij,dpj->pcdi/dot_general | solution.py:366
  85.9 1.2 fusion.1
  87.1 9.2 %all-to-all-done.2.recv = bf16[8,576,128]{2,1,0:T(8,128)(2,1)S(1)} async-done(((bf16[8,576,128]{2,1,0:T(8,128)(2,1)}), bf16[8,576,128]{2,1,0:T(8,128)(2,1)S(1)}, u32[]{:S(2)}, u32[]{:S(2)}) %all-to-all-start.2) | async-done | bytes 1179680 | tf_op jit(solution)/shard_map/all_to_all | solution.py:424
  96.3 1.0 copy-done.1
  97.3 9.8 %shard_map.148 = bf16[512,128]{1,0:T(8,128)(2,1)} custom-call(bf16[8,576,128]{2,1,0:T(8,128)(2,1)} %copy-done.1, bf16[512,128]{1,0:T(8,128)(2,1)} %bitcast.82, bf16[128,2048]{1,0:T(8,128)(2,1)} %constant.23.clone.spread, bf16[1024,1024]{1,0:T(8,128)(2,1)} %constant.7.clone.cos, bf16[1024,1024]{1,0:T(8,128)(2,1)} %constant.18.clone.sin), custom_call_target="tpu_custom_call" | custom-call | tf_op jit(solution)/shard_map/pallas_call | solution.py:306
  107.1 5.5 %all-to-all-start.3 = ((bf16[16,32,128]{2,1,0:T(8,128)(2,1)}), bf16[16,32,128]{2,1,0:T(8,128)(2,1)S(1)}, u32[]{:S(2)}, u32[]{:S(2)}) async-start(bf16[16,32,128]{2,1,0:T(8,128)(2,1)} %bitcast.84), calls=%async_computation.3 | async-start | bytes 262144 | tf_op jit(solution)/shard_map/all_to_all | solution.py:441
  112.6 0.7 fusion.20.near
  113.3 6.2 %all-to-all-done.3.recv = bf16[16,32,128]{2,1,0:T(8,128)(2,1)S(1)} async-done(((bf16[16,32,128]{2,1,0:T(8,128)(2,1)}), bf16[16,32,128]{2,1,0:T(8,128)(2,1)S(1)}, u32[]{:S(2)}, u32[]{:S(2)}) %all-to-all-start.3) | async-done | bytes 131104 | tf_op jit(solution)/shard_map/all_to_all | solution.py:441
  119.5 0.7 copy-done.3
  120.1 8.9 %shard_map.149 = f32[32,2,128]{2,1,0:T(2,128)} custom-call(bf16[16,32,128]{2,1,0:T(8,128)(2,1)} %copy-done.3, f32[32,128,128]{2,1,0:T(8,128)} %proj.3, s32[32,128]{1,0:T(8,128)} %cells.3, f32[32,2,128]{2,1,0:T(2,128)} %fusion.20.near, bf16[512,512]{1,0:T(8,128)(2,1)} %constant.19.clone.tch, bf16[512,512]{1,0:T(8,128)(2,1)} %constant.20.clone.tcl, ...), custom_call_target="tpu_custom_call" | custom-call | tf_op jit(solution)/shard_map/pallas_call | solution.py:306
  (46 shorter events, 2.5 us)
Async XLA Ops:
  0.9 0.6 copy-start.4
  2.1 47.1 %collective-permute-start = (bf16[2,1,1,32,128]{4,3,2,1,0:T(8,128)(2,1)}, bf16[2,1,1,32,128]{4,3,2,1,0:T(8,128)(2,1)}, u32[]{:S(2)}, u32[]{:S(2)}) collective-permute-start(bf16[2,1,1,32,128]{4,3,2,1,0:T(8,128)(2,1)} %bitcast.75), channel_id=1, source_target_pairs={{0,16},{16,32},{32,48},{48,64},{64,80},{80,96},{96,112},{112,0},{1... | collective-permute-start | bytes 49160 | tf_op jit(solution)/shard_map/ppermute | solution.py:323
  5.1 44.8 %collective-permute-start.1 = (bf16[2,1,1,32,128]{4,3,2,1,0:T(8,128)(2,1)}, bf16[2,1,1,32,128]{4,3,2,1,0:T(8,128)(2,1)}, u32[]{:S(2)}, u32[]{:S(2)}) collective-permute-start(bf16[2,1,1,32,128]{4,3,2,1,0:T(8,128)(2,1)} %bitcast.75), channel_id=1, source_target_pairs={{16,0},{32,16},{48,32},{64,48},{80,64},{96,80},{112,96},{0,112},{1... | collective-permute-start | bytes 49160 | tf_op jit(solution)/shard_map/ppermute | solution.py:324
  5.1 16.5 %copy-start.6 = (s32[1,128]{1,0:T(1,128)S(1)}, s32[1,128]{1,0:T(1,128)}, u32[]{:S(2)}) copy-start(s32[1,128]{1,0:T(1,128)} %param.17) | copy-start | bytes 1540
  14.9 16.3 %all-to-all-start = ((bf16[16,32,128]{2,1,0:T(8,128)(2,1)}), bf16[16,32,128]{2,1,0:T(8,128)(2,1)S(1)}, u32[]{:S(2)}, u32[]{:S(2)}) async-start(bf16[16,32,128]{2,1,0:T(8,128)(2,1)} %shard_map.145), calls=%async_computation | async-start | bytes 262144 | tf_op jit(solution)/shard_map/all_to_all | solution.py:398
  21.9 5.8 %copy-start.10 = (s32[1,128]{1,0:T(1,128)S(1)}, s32[1,128]{1,0:T(1,128)}, u32[]{:S(2)}) copy-start(s32[1,128]{1,0:T(1,128)} %param.18) | copy-start | bytes 1540
  27.2 0.5 copy-start.8
  28.9 26.7 %collective-permute-start.5 = (bf16[2,1,3,32,128]{4,0,3,2,1:T(2,128)(2,1)}, bf16[2,1,3,32,128]{4,0,3,2,1:T(2,128)(2,1)}, u32[]{:S(2)}, u32[]{:S(2)}) collective-permute-start(bf16[2,1,3,32,128]{4,0,3,2,1:T(2,128)(2,1)} %get-tuple-element.13), channel_id=1, source_target_pairs={{16,0},{32,16},{48,32},{64,48},{80,64},{96,80},{112,96},{0,112},{1... | collective-permute-start | bytes 147464 | tf_op jit(solution)/shard_map/ppermute | solution.py:324
  31.1 24.4 %collective-permute-start.4 = (bf16[2,1,3,32,128]{4,0,3,2,1:T(2,128)(2,1)}, bf16[2,1,3,32,128]{4,0,3,2,1:T(2,128)(2,1)}, u32[]{:S(2)}, u32[]{:S(2)}) collective-permute-start(bf16[2,1,3,32,128]{4,0,3,2,1:T(2,128)(2,1)} %get-tuple-element.12), channel_id=1, source_target_pairs={{0,16},{16,32},{32,48},{48,64},{64,80},{80,96},{96,112},{112,0},{1... | collective-permute-start | bytes 147464 | tf_op jit(solution)/shard_map/ppermute | solution.py:323
  31.2 0.6 copy-start.2
  40.7 21.5 %all-to-all-start.1 = ((bf16[8,576,128]{2,1,0:T(8,128)(2,1)}), bf16[8,576,128]{2,1,0:T(8,128)(2,1)S(1)}, u32[]{:S(2)}, u32[]{:S(2)}) async-start(bf16[8,576,128]{2,1,0:T(8,128)(2,1)} %shard_map.146), calls=%async_computation.1 | async-start | bytes 2359296 | tf_op jit(solution)/shard_map/all_to_all | solution.py:413
  47.3 2.6 %copy-start.5 = (bf16[1,2,32,128]{3,1,2,0:T(2,128)(2,1)S(1)}, bf16[1,2,32,128]{3,1,2,0:T(2,128)(2,1)}, u32[]{:S(2)}) copy-start(bf16[1,2,32,128]{3,1,2,0:T(2,128)(2,1)} %copy-done.4) | copy-start | bytes 49156
  47.3 14.6 %copy-start.11 = (s32[1,128]{1,0:T(1,128)S(1)}, s32[1,128]{1,0:T(1,128)}, u32[]{:S(2)}) copy-start(s32[1,128]{1,0:T(1,128)} %param.18) | copy-start | bytes 1540
  50.6 10.9 %collective-permute-start.3 = (bf16[2,3,1,32,128]{4,3,2,1,0:T(8,128)(2,1)S(1)}, bf16[2,3,1,32,128]{4,3,2,1,0:T(8,128)(2,1)S(1)}, u32[]{:S(2)}, u32[]{:S(2)}) collective-permute-start(bf16[2,3,1,32,128]{4,3,2,1,0:T(8,128)(2,1)S(1)} %constant_dynamic-update-slice_fusion), channel_id=1, source_target_pairs={{1,0},{2,1},{3,2},{4,3},{5,4},{6,5},{7,6},{8,7},{9,8},{10,9},{11,1... | collective-permute-start | bytes 147464 | tf_op jit(solution)/shard_map/ppermute | solution.py:324
  55.6 6.3 %collective-permute-start.2 = (bf16[2,3,1,32,128]{4,3,2,1,0:T(8,128)(2,1)S(1)}, bf16[2,3,1,32,128]{4,3,2,1,0:T(8,128)(2,1)S(1)}, u32[]{:S(2)}, u32[]{:S(2)}) collective-permute-start(bf16[2,3,1,32,128]{4,3,2,1,0:T(8,128)(2,1)S(1)} %constant_dynamic-update-slice_fusion), channel_id=1, source_target_pairs={{0,1},{1,2},{2,3},{3,4},{4,5},{5,6},{6,7},{7,8},{8,9},{9,10},{10,1... | collective-permute-start | bytes 147464 | tf_op jit(solution)/shard_map/ppermute | solution.py:323
  56.6 29.3 %collective-permute-start.7 = (bf16[2,5,1,32,128]{4,0,3,2,1:T(2,128)(2,1)S(1)}, bf16[2,5,1,32,128]{4,0,3,2,1:T(2,128)(2,1)S(1)}, u32[]{:S(2)}, u32[]{:S(2)}) collective-permute-start(bf16[2,5,1,32,128]{4,0,3,2,1:T(2,128)(2,1)S(1)} %get-tuple-element.11), channel_id=1, source_target_pairs={{1,0},{2,1},{3,2},{4,3},{5,4},{6,5},{7,6},{8,7},{9,8},{10,9},{11,1... | collective-permute-start | bytes 245768 | tf_op jit(solution)/shard_map/ppermute | solution.py:324
  61.5 24.5 %collective-permute-start.6 = (bf16[2,5,1,32,128]{4,0,3,2,1:T(2,128)(2,1)S(1)}, bf16[2,5,1,32,128]{4,0,3,2,1:T(2,128)(2,1)S(1)}, u32[]{:S(2)}, u32[]{:S(2)}) collective-permute-start(bf16[2,5,1,32,128]{4,0,3,2,1:T(2,128)(2,1)S(1)} %get-tuple-element.10), channel_id=1, source_target_pairs={{0,1},{1,2},{2,3},{3,4},{4,5},{5,6},{6,7},{7,8},{8,9},{9,10},{10,1... | collective-permute-start | bytes 245768 | tf_op jit(solution)/shard_map/ppermute | solution.py:323
  62.3 1.0 copy-start
  73.6 22.7 %all-to-all-start.2 = ((bf16[8,576,128]{2,1,0:T(8,128)(2,1)}), bf16[8,576,128]{2,1,0:T(8,128)(2,1)S(1)}, u32[]{:S(2)}, u32[]{:S(2)}) async-start(bf16[8,576,128]{2,1,0:T(8,128)(2,1)} %shard_map.147), calls=%async_computation.2 | async-start | bytes 2359296 | tf_op jit(solution)/shard_map/all_to_all | solution.py:424
  79.8 5.9 %copy-start.7 = (s32[1,128]{1,0:T(1,128)S(1)}, s32[1,128]{1,0:T(1,128)}, u32[]{:S(2)}) copy-start(s32[1,128]{1,0:T(1,128)} %param.17) | copy-start | bytes 1540
  79.8 5.9 %copy-start.9 = (f32[128]{0:T(128)S(1)}, f32[128]{0:T(128)}, u32[]{:S(2)}) copy-start(f32[128]{0:T(128)} %copy-done.8) | copy-start | bytes 1540
  96.3 1.0 copy-start.1
  107.1 12.3 %all-to-all-start.3 = ((bf16[16,32,128]{2,1,0:T(8,128)(2,1)}), bf16[16,32,128]{2,1,0:T(8,128)(2,1)S(1)}, u32[]{:S(2)}, u32[]{:S(2)}) async-start(bf16[16,32,128]{2,1,0:T(8,128)(2,1)} %bitcast.84), calls=%async_computation.3 | async-start | bytes 262144 | tf_op jit(solution)/shard_map/all_to_all | solution.py:441
  119.5 0.7 copy-start.3

commit v2 on v1

--- a/solution.py
+++ b/solution.py
@@ -140,7 +140,7 @@
     return jnp.where(inside, 1.0, 0.0)
 
 
-def image_kernel(recv, spread, cos, sin, out, wide, starts, img):
+def build_image(recv, spread, wide, starts, img):
     def spread_rows(i, carry):
         rows = pl.ds(pl.multiple_of(i * 128, 128), 128)
         wide_rows = pl.ds(pl.multiple_of(i * 128 + NB, NB), 128)
@@ -163,52 +163,62 @@
         lhs = [jnp.where(offset == ex, 1.0, 0.0).astype(BF) for ex in range(4)]
         rhs = [wide[64 * q : 64 * q + 128, 512 * ex : 512 * ex + 512] * mask for ex in range(4)]
         cells = dot(jnp.concatenate(lhs, axis=1), jnp.concatenate(rhs, axis=0)).astype(BF)
-        for p in range(4):
-            img[XR * p : XR * p + XR, 128 * q : 128 * q + 128] = cells[:, 128 * p : 128 * p + 128]
-
-    def along_y(i, carry):
+        for kz in range(2):
+            for c in range(2):
+                p = 2 * c + kz
+                img[kz, XR * c : XR * c + XR, 128 * q : 128 * q + 128] = cells[:, 128 * p : 128 * p + 128]
+
+
+def forward_y(kz, img, cos, sin, out):
+    def lanes_of(i, carry):
         lanes = pl.ds(pl.multiple_of(i * 256, 256), 256)
-        real, imag = img[0 : 2 * XR, :], img[2 * XR :, :]
-        cos_i, sin_i = cos[:, lanes], sin[:, lanes]
-        out_real = (dot(real, cos_i) + dot(imag, sin_i)).astype(BF)
-        out_imag = (dot(imag, cos_i) - dot(real, sin_i)).astype(BF)
+        by_cos = dot(img[kz], cos[:, lanes])
+        by_sin = dot(img[kz], sin[:, lanes])
+        real = (by_cos[:XR] + by_sin[XR:]).astype(BF)
+        imag = (by_cos[XR:] - by_sin[:XR]).astype(BF)
         for j in range(2):
-            out[2 * i + j, 0 : 2 * XR, :] = out_real[:, 128 * j : 128 * j + 128]
-            out[2 * i + j, 2 * XR :, :] = out_imag[:, 128 * j : 128 * j + 128]
-        return carry
-
-    lax.fori_loop(0, 4, along_y, 0)
-
-
-def spectrum_kernel(recv, green, cos, sin, out, d_one, d_two, h_one, h_two):
+            out[kz, 2 * i + j, 0:XR, :] = real[:, 128 * j : 128 * j + 128]
+            out[kz, 2 * i + j, XR:, :] = imag[:, 128 * j : 128 * j + 128]
+        return carry
+
+    lax.fori_loop(0, 4, lanes_of, 0)
+
+
+def along_x(kz, recv, green, cos, sin, out, d_one, d_two, h_one, h_two):
     low_rows = iota((16, 128), 0) < 8
-    for r in range(NROW):
-        before, after = (r - 1) % NROW, (r + 1) % NROW
-        for p in range(4):
-            base = XR * p
-            main = recv[r, base : base + 128, :]
-            lower = recv[before, base + 128 : base + XR, :].astype(F32)
-            upper = recv[after, base + 128 : base + XR, :].astype(F32)
+
+    def gather_band(r, carry):
+        before, after = lax.rem(r + NROW - 1, NROW), lax.rem(r + 1, NROW)
+        rows = pl.ds(pl.multiple_of(r * 128, 128), 128)
+        for c in range(2):
+            base = XR * c
+            main = recv[kz, r, base : base + 128, :]
+            lower = recv[kz, before, base + 128 : base + XR, :].astype(F32)
+            upper = recv[kz, after, base + 128 : base + XR, :].astype(F32)
             head = main[0:16].astype(F32) + jnp.where(low_rows, lower, 0.0)
             tail = main[112:128].astype(F32) + jnp.where(low_rows, 0.0, upper)
             band = jnp.concatenate([head.astype(BF), main[16:112], tail.astype(BF)], axis=0)
-            d_one[128 * r : 128 * r + 128, 128 * p : 128 * p + 128] = band
-            if p < 2:
-                d_two[128 * r : 128 * r + 128, 256 + 128 * p : 384 + 128 * p] = -band
+            d_one[rows, 128 * c : 128 * c + 128] = band
+            if c == 0:
+                d_two[rows, 128:256] = -band
             else:
-                d_two[128 * r : 128 * r + 128, 128 * p - 256 : 128 * p - 128] = band
+                d_two[rows, 0:128] = band
+        return carry
+
+    lax.fori_loop(0, NROW, gather_band, 0)
 
     def forward(i, carry):
         rows = pl.ds(pl.multiple_of(i * 256, 256), 256)
         spec = dot(cos[rows, :], d_one[...]) + dot(sin[rows, :], d_two[...])
-        real, imag = spec[:, :256], spec[:, 256:]
-        g_real, g_imag = green[0, rows, :], green[1, rows, :]
+        real, imag = spec[:, :128], spec[:, 128:]
+        lanes = slice(128 * kz, 128 * kz + 128)
+        g_real, g_imag = green[0, rows, lanes], green[1, rows, lanes]
         h_real = (real * g_real - imag * g_imag).astype(BF)
         h_imag = (real * g_imag + imag * g_real).astype(BF)
-        h_one[rows, 0:256] = h_real
-        h_one[rows, 256:512] = h_imag
-        h_two[rows, 0:256] = -h_imag
-        h_two[rows, 256:512] = h_real
+        h_one[rows, 0:128] = h_real
+        h_one[rows, 128:256] = h_imag
+        h_two[rows, 0:128] = -h_imag
+        h_two[rows, 128:256] = h_real
         return carry
 
     lax.fori_loop(0, 4, forward, 0)
@@ -217,53 +227,119 @@
         rows = pl.ds(pl.multiple_of(i * 256, 256), 256)
         back = (dot(cos[rows, :], h_one[...]) + dot(sin[rows, :], h_two[...])).astype(BF)
         for j in range(2):
-            for p in range(4):
-                out[2 * i + j, XR * p : XR * p + 128, :] = back[
-                    128 * j : 128 * j + 128, 128 * p : 128 * p + 128
+            for c in range(2):
+                out[kz, 2 * i + j, XR * c : XR * c + 128, :] = back[
+                    128 * j : 128 * j + 128, 128 * c : 128 * c + 128
                 ]
         return carry
 
     lax.fori_loop(0, 4, inverse, 0)
+
+    def rims(r, carry):
+        before, after = lax.rem(r + NROW - 1, NROW), lax.rem(r + 1, NROW)
+        for c in range(2):
+            base = XR * c
+            above = out[kz, after, base : base + 16, :].astype(F32)
+            below = out[kz, before, base + 112 : base + 128, :].astype(F32)
+            out[kz, r, base + 128 : base + XR, :] = jnp.where(low_rows, above, below).astype(BF)
+        return carry
+
+    lax.fori_loop(0, NROW, rims, 0)
+
+
+def inverse_y(kz, recv, cos, sin, spec, pot):
     for r in range(NROW):
-        before, after = (r - 1) % NROW, (r + 1) % NROW
-        for p in range(4):
-            base = XR * p
-            above = out[after, base : base + 16, :].astype(F32)
-            below = out[before, base + 112 : base + 128, :].astype(F32)
-            out[r, base + 128 : base + XR, :] = jnp.where(low_rows, above, below).astype(BF)
-
-
-def gather_kernel(recv, near_info, spread, cos, sin, out, spec, pot, starts, hot, acc):
-    for r in range(NROW):
-        spec[:, 128 * r : 128 * r + 128] = recv[r]
-
-    def along_y(i, carry):
+        spec[:, 128 * r : 128 * r + 128] = recv[kz, r]
+
+    def lanes_of(i, carry):
         lanes = pl.ds(pl.multiple_of(i * 256, 256), 256)
-        real, imag = spec[0 : 2 * XR, :], spec[2 * XR :, :]
-        cos_i, sin_i = cos[:, lanes], sin[:, lanes]
-        pot[0 : 2 * XR, lanes] = (dot(real, cos_i) - dot(imag, sin_i)).astype(BF)
-        pot[2 * XR :, lanes] = (dot(imag, cos_i) + dot(real, sin_i)).astype(BF)
-        return carry
-
-    lax.fori_loop(0, 4, along_y, 0)
-    store_starts(near_info, starts)
+        by_cos = dot(spec[...], cos[:, lanes])
+        by_sin = dot(spec[...], sin[:, lanes])
+        pot[0:XR, lanes] = (by_cos[:XR] - by_sin[XR:]).astype(BF)
+        pot[XR:, lanes] = (by_cos[XR:] + by_sin[:XR]).astype(BF)
+        return carry
+
+    lax.fori_loop(0, 4, lanes_of, 0)
+
+
+def build_hot(recv, hot):
     local_x = local_x_of_row((512, XR), 1)
-    offset = local_x - near_info[:, 64:65].astype(jnp.int32)
+    offset = local_x - recv[:, 64:65].astype(jnp.int32)
     for ex in range(4):
         hot[ex, NB : NB + 512, :] = jnp.where(offset == ex, 1.0, 0.0).astype(BF)
     hot[:, 0:NB, :] = hot[:, 512 : 512 + NB, :]
     hot[:, NB + 512 :, :] = hot[:, NB : 2 * NB, :]
-    acc[...] = jnp.zeros_like(acc)
+
+
+def pick_cells(kz, pot, starts, hot, acc):
     for q in range(8):
         mask = chunk_mask(starts, q)
-        mask = jnp.concatenate([mask] * 4, axis=1)
-        cells = [pot[XR * p : XR * p + XR, 128 * q : 128 * q + 128] for p in range(4)]
+        mask = jnp.concatenate([mask] * 2, axis=1)
+        cells = [pot[XR * c : XR * c + XR, 128 * q : 128 * q + 128] for c in range(2)]
         cells = jnp.concatenate(cells, axis=1)
         rows = slice(64 * q, 64 * q + 128)
         for ex in range(4):
             taken = (dot(hot[ex, rows, :], cells) * mask).astype(BF)
-            lanes = slice(512 * ex, 512 * ex + 512)
-            acc[rows, lanes] = acc[rows, lanes] + taken
+            for c in range(2):
+                lane = 512 * ex + 256 * c + 128 * kz
+                lanes = slice(lane, lane + 128)
+                acc[rows, lanes] = acc[rows, lanes] + taken[:, 128 * c : 128 * c + 128]
+
+
+def middle_kernel(
+    recv, spread, green, cos, sin, out,
+    wide, starts, img, hot, acc, spec, pot, d_one, d_two, h_one, h_two,
+    send_a, recv_a, send_b, recv_b, sem_send_a, sem_recv_a, sem_send_b, sem_recv_b,
+):
+    me = lax.axis_index("row")
+    barrier = pltpu.get_barrier_semaphore()
+    for j in range(1, NROW):
+        peer = lax.rem(me + j, NROW)
+        pl.semaphore_signal(
+            barrier, inc=1, device_id={"row": peer}, device_id_type=pl.DeviceIdType.MESH
+        )
+
+    def copies(kz, source, target, sem_send, sem_recv):
+        result = []
+        for j in range(1, NROW):
+            peer = lax.rem(me + j, NROW)
+            result.append(
+                pltpu.make_async_remote_copy(
+                    src_ref=source.at[kz, peer],
+                    dst_ref=target.at[kz, me],
+                    send_sem=sem_send.at[kz, j],
+                    recv_sem=sem_recv.at[kz, j],
+                    device_id={"row": peer},
+                    device_id_type=pl.DeviceIdType.MESH,
+                )
+            )
+        return result
+
+    build_image(recv, spread, wide, starts, img)
+    first, second = [], []
+    for kz in range(2):
+        forward_y(kz, img, cos, sin, send_a)
+        if kz == 0:
+            pl.semaphore_wait(barrier, NROW - 1)
+        first.append(copies(kz, send_a, recv_a, sem_send_a, sem_recv_a))
+        for copy in first[kz]:
+            copy.start()
+        recv_a[kz, me] = send_a[kz, me]
+    build_hot(recv, hot)
+    acc[...] = jnp.zeros_like(acc)
+    for kz in range(2):
+        for copy in first[kz]:
+            copy.wait_recv()
+        along_x(kz, recv_a, green, cos, sin, send_b, d_one, d_two, h_one, h_two)
+        second.append(copies(kz, send_b, recv_b, sem_send_b, sem_recv_b))
+        for copy in second[kz]:
+            copy.start()
+        recv_b[kz, me] = send_b[kz, me]
+    for kz in range(2):
+        for copy in second[kz]:
+            copy.wait_recv()
+        inverse_y(kz, recv_b, cos, sin, spec, pot)
+        pick_cells(kz, pot, starts, hot, acc)
     acc[512 : 512 + NB, :] = acc[512 : 512 + NB, :] + acc[0:NB, :]
     acc[NB : 2 * NB, :] = acc[NB : 2 * NB, :] + acc[NB + 512 :, :]
 
@@ -274,6 +350,9 @@
         return carry
 
     lax.fori_loop(0, 4, fold, 0)
+    for kz in range(2):
+        for copy in first[kz] + second[kz]:
+            copy.wait_send()
 
 
 def back_kernel(recv, proj, cells, near, tch, tcl, tsh, tsl, out, codes, box_real, box_imag):
@@ -302,14 +381,14 @@
     lax.fori_loop(0, NB // 4, block, 0)
 
 
-def call(kernel, out_shape, scratch, *args):
+def call(kernel, out_shape, scratch, *args, **params):
     return pl.pallas_call(
         kernel,
         out_shape=out_shape,
         in_specs=[pl.BlockSpec(memory_space=pltpu.VMEM)] * len(args),
         out_specs=pl.BlockSpec(memory_space=pltpu.VMEM),
         scratch_shapes=scratch,
-        compiler_params=pltpu.CompilerParams(vmem_limit_bytes=VMEM_LIMIT),
+        compiler_params=pltpu.CompilerParams(vmem_limit_bytes=VMEM_LIMIT, **params),
     )(*args)
 
 
@@ -397,46 +476,30 @@
     )
     sources = lax.all_to_all(messages, "col", split_axis=0, concat_axis=0, tiled=True)
     sources = sources.reshape(NCOL * NB, 128)
-    bands = call(
-        image_kernel,
-        shape((NROW, 4 * XR, 128), BF),
+    turned = jnp.transpose(green, (0, 3, 1, 2)).reshape(2, N, 256) * (1.0 / (N * N * NGZ))
+    grid_bytes = (2, NROW, 2 * XR, 128)
+    taken = call(
+        middle_kernel,
+        shape((NCOL * NB, 128), BF),
         [
             pltpu.VMEM((512 + 2 * NB, 2048), BF),
             pltpu.VMEM((512 + 2 * NB, 128), jnp.int32),
-            pltpu.VMEM((4 * XR, N), BF),
-        ],
+            pltpu.VMEM((2, 2 * XR, N), BF),
+            pltpu.VMEM((4, 512 + 2 * NB, XR), BF),
+            pltpu.VMEM((512 + 2 * NB, 2048), BF),
+            pltpu.VMEM((2 * XR, N), BF),
+            pltpu.VMEM((2 * XR, N), BF),
+        ]
+        + [pltpu.VMEM((N, 256), BF)] * 4
+        + [pltpu.VMEM(grid_bytes, BF)] * 4
+        + [pltpu.SemaphoreType.DMA((2, NROW))] * 4,
         sources,
         spread,
-        cos,
-        sin,
-    )
-    pencils = lax.all_to_all(bands, "row", split_axis=0, concat_axis=0, tiled=True)
-    turned = jnp.transpose(green, (0, 3, 1, 2)).reshape(2, N, 256) * (1.0 / (N * N * NGZ))
-    pencils = call(
-        spectrum_kernel,
-        shape((NROW, 4 * XR, 128), BF),
-        [pltpu.VMEM((N, 512), BF)] * 4,
-        pencils,
         turned,
         cos,
         sin,
-    )
-    bands = lax.all_to_all(pencils, "row", split_axis=0, concat_axis=0, tiled=True)
-    taken = call(
-        gather_kernel,
-        shape((NCOL * NB, 128), BF),
-        [
-            pltpu.VMEM((4 * XR, N), BF),
-            pltpu.VMEM((4 * XR, N), BF),
-            pltpu.VMEM((512 + 2 * NB, 128), jnp.int32),
-            pltpu.VMEM((4, 512 + 2 * NB, XR), BF),
-            pltpu.VMEM((512 + 2 * NB, 2048), BF),
-        ],
-        bands,
-        sources,
-        spread,
-        cos,
-        sin,
+        collective_id=1,
+        has_side_effects=True,
     )
     messages = lax.all_to_all(
         taken.reshape(NCOL, NB, 128), "col", split_axis=0, concat_axis=0, tiled=True

time: 131 us -> 115 us (0.88); the launches traced: 129 us -> 115 us
  Pallas kernels: 47.7 us -> 63.2 us
  starting transfers between devices: 38.3 us -> 25 us
  waiting for transfers between devices: 15.7 us -> 6.08 us
  local copies, waits for them, and re-layouts: 9.37 us -> 3.49 us
  other arithmetic: 5.71 us -> 4.12 us
    pallas_call x5 -> x3, Pallas kernels: 47.7 us -> 63.2 us  [call(): pl.pallas_call(kernel, out_shape=out_shape, in_specs=[pl.BlockSpec(memory...]
    all_to_all x2 -> x0, starting transfers between devices: 11 us -> none  [the longest x1 6.23 us: per_device(): lax.all_to_all(pencils, 'row', split_axis=0, concat_axis=0, tiled=True)]
    all_to_all x2 -> x0, waiting for transfers between devices: 9.16 us -> none  [the longest x1 9.15 us: per_device(): lax.all_to_all(pencils, 'row', split_axis=0, concat_axis=0, tiled=True)]
    unnamed x28 -> x12, local copies, waits for them, and re-layouts: 5.95 us -> 1.44 us
    ppermute x4, starting transfers between devices: 12.1 us -> 8.46 us  [with_halo(): after = lax.ppermute(first, axis, down)]
    ppermute x4, starting transfers between devices: 3.04 us -> 6.3 us  [with_halo(): before = lax.ppermute(last, axis, up)]
    all_to_all x1, starting transfers between devices: 5.49 us -> 3.52 us  [per_device(): lax.all_to_all(taken.reshape(NCOL, NB, 128), 'col', split_axis=0, concat_...]
  transfers between devices with their start and end apart: 12 -> 10, of which waited for: 3 -> 1; matrix products, arithmetic and copies ran while one was open for 16% -> 15% of each run, Pallas kernels for 22% -> 47%
where the time goes in v2:
time: 115 us
  Pallas kernels  63.2 us (55%)
  starting transfers between devices  25 us (22%)
  matrix products  11.9 us (10%)
  waiting for transfers between devices  6.08 us (5%)
  other arithmetic  4.12 us (4%)
  local copies, waits for them, and re-layouts  3.49 us (3%)
    pallas_call x3, Pallas kernels, call(): pl.pallas_call(kernel, out_shape=out_shape, in_specs=[pl.BlockSpec(memory...  63.2 us
    ppermute x4, starting transfers between devices, with_halo(): after = lax.ppermute(first, axis, down)  8.46 us
    all_to_all x1, starting transfers between devices, per_device(): lax.all_to_all(messages, 'col', split_axis=0, concat_axis=0, tiled=True)  6.75 us
    ppermute x4, starting transfers between devices, with_halo(): before = lax.ppermute(last, axis, up)  6.3 us
    all_to_all x1, waiting for transfers between devices, per_device(): lax.all_to_all(taken.reshape(NCOL, NB, 128), 'col', split_axis=0, concat_...  6.06 us
    dot_general x1, matrix products, near_part(): jnp.einsum('pcij,dpj->pcdi', near_blocks, remote_vals, preferred_element_...  5.64 us
    dot_general x1, matrix products, near_part(): jnp.einsum('pcij,dpi->pcdj', near_blocks, local_vals, preferred_element_t...  4.58 us
    all_to_all x1, starting transfers between devices, per_device(): lax.all_to_all(taken.reshape(NCOL, NB, 128), 'col', split_axis=0, concat_...  3.52 us
  transfers between devices with their start and end apart: 10, of which 1 were waited for; matrix products, arithmetic and copies ran while one was open for 15% of the time, Pallas kernels for 47%

profile of v2, /device:TPU:1, one launch (start us, length us, event | category | flops | bytes accessed | tf_op | source)
XLA Modules:
  0.0 114.8 jit_solution(279024790304148042)
XLA Ops:
  0.0 0.9 convert_bitcast_fusion
  0.9 3.0 %collective-permute-start = (bf16[2,1,1,32,128]{4,3,2,1,0:T(8,128)(2,1)S(1)}, bf16[2,1,1,32,128]{4,3,2,1,0:T(8,128)(2,1)S(1)}, u32[]{:S(2)}, u32[]{:S(2)}) collective-permute-start(bf16[2,1,1,32,128]{4,3,2,1,0:T(8,128)(2,1)S(1)} %bitcast.89), channel_id=1, source_target_pairs={{0,16},{16,32},{32,48},{48,64},{64,80},{80,96},{96,112},{112,0},{1... | collective-permute-start | bytes 49160 | tf_op jit(solution)/shard_map/ppermute | solution.py:402
  3.9 0.9 convolution_convert_fusion.1
  4.8 0.0 copy-start.3
  4.8 4.6 %fusion.12 = f32[128,2,2,128]{3,1,2,0:T(2,128)S(1)} fusion(bf16[128,2,128,128]{3,2,1,0:T(8,128)(2,1)} %param.16, bf16[128,2,128]{2,0,1:T(8,128)(2,1)S(1)} %convolution_convert_fusion.1), kind=kOutput, calls=%fused_computation.29 | convolution fusion | flops 16777216 | bytes 8716288 | tf_op jit(solution)/shard_map/pcij,dpi->pcdj/dot_general | solution.py:446
  10.1 0.4 fusion
  10.5 0.1 copy.27
  10.6 0.1 fusion.30
  10.7 1.8 %collective-permute-start.4 = (bf16[2,1,3,32,128]{4,0,3,2,1:T(2,128)(2,1)S(1)}, bf16[2,1,3,32,128]{4,0,3,2,1:T(2,128)(2,1)S(1)}, u32[]{:S(2)}, u32[]{:S(2)}) collective-permute-start(bf16[2,1,3,32,128]{4,0,3,2,1:T(2,128)(2,1)S(1)} %get-tuple-element.12), channel_id=1, source_target_pairs={{0,16},{16,32},{32,48},{48,64},{64,80},{80,96},{96,112},{112,0},{1... | collective-permute-start | bytes 147464 | tf_op jit(solution)/shard_map/ppermute | solution.py:402
  12.4 0.3 collective-permute-start.5
  12.7 9.7 %shard_map.145 = bf16[16,32,128]{2,1,0:T(8,128)(2,1)} custom-call(f32[32,2,128]{2,1,0:T(2,128)} %bitcast.88, f32[32,128,128]{2,1,0:T(8,128)} %proj.3, s32[32,128]{1,0:T(8,128)} %cells.3, bf16[512,512]{1,0:T(8,128)(2,1)} %constant.19.clone.tch, bf16[512,512]{1,0:T(8,128)(2,1)} %constant.20.clone.tcl, bf16[512,512]{1,0:T(8,128)(2,1)} %constant.21.clone.tsh, ...), custom_call_target="tpu_custom_call" | custom-call | tf_op jit(solution)/shard_map/pallas_call | solution.py:385
  22.4 6.8 %all-to-all-start = ((bf16[16,32,128]{2,1,0:T(8,128)(2,1)}), bf16[16,32,128]{2,1,0:T(8,128)(2,1)S(1)}, u32[]{:S(2)}, u32[]{:S(2)}) async-start(bf16[16,32,128]{2,1,0:T(8,128)(2,1)} %shard_map.145), calls=%async_computation | async-start | bytes 262144 | tf_op jit(solution)/shard_map/all_to_all | solution.py:477
  29.2 1.8 %broadcast_multiply_fusion = f32[2,2,128,1024]{3,2,1,0:T(8,128)S(1)} fusion(f32[2,2,128,1024]{3,2,1,0:T(8,128)} %param.22), kind=kLoop, calls=%fused_computation.5 | loop fusion | flops 524288 | bytes 4194304 | tf_op jit(solution)/shard_map/mul | solution.py:479
  31.0 1.8 %copy.33.green = f32[2,1024,256]{2,1,0:T(8,128)} copy(f32[2,1024,256]{1,2,0:T(8,128)S(1)} %bitcast.77) | data formatting | bytes 4194304 | tf_op jit(solution)/shard_map/mul | solution.py:479
  32.9 1.4 %collective-permute-start.2 = (bf16[2,3,1,32,128]{4,3,2,1,0:T(8,128)(2,1)S(1)}, bf16[2,3,1,32,128]{4,3,2,1,0:T(8,128)(2,1)S(1)}, u32[]{:S(2)}, u32[]{:S(2)}) collective-permute-start(bf16[2,3,1,32,128]{4,3,2,1,0:T(8,128)(2,1)S(1)} %constant_dynamic-update-slice_fusion), channel_id=1, source_target_pairs={{0,1},{1,2},{2,3},{3,4},{4,5},{5,6},{6,7},{7,8},{8,9},{9,10},{10,1... | collective-permute-start | bytes 147464 | tf_op jit(solution)/shard_map/ppermute | solution.py:402
  34.3 3.4 %collective-permute-start.3 = (bf16[2,3,1,32,128]{4,3,2,1,0:T(8,128)(2,1)S(1)}, bf16[2,3,1,32,128]{4,3,2,1,0:T(8,128)(2,1)S(1)}, u32[]{:S(2)}, u32[]{:S(2)}) collective-permute-start(bf16[2,3,1,32,128]{4,3,2,1,0:T(8,128)(2,1)S(1)} %constant_dynamic-update-slice_fusion), channel_id=1, source_target_pairs={{1,0},{2,1},{3,2},{4,3},{5,4},{6,5},{7,6},{8,7},{9,8},{10,9},{11,1... | collective-permute-start | bytes 147464 | tf_op jit(solution)/shard_map/ppermute | solution.py:403
  37.7 0.2 pad_maximum_fusion.7
  38.0 0.1 collective-permute-start.6
  38.0 4.8 %collective-permute-start.7 = (bf16[2,5,1,32,128]{4,0,3,2,1:T(2,128)(2,1)S(1)}, bf16[2,5,1,32,128]{4,0,3,2,1:T(2,128)(2,1)S(1)}, u32[]{:S(2)}, u32[]{:S(2)}) collective-permute-start(bf16[2,5,1,32,128]{4,0,3,2,1:T(2,128)(2,1)S(1)} %get-tuple-element.11), channel_id=1, source_target_pairs={{1,0},{2,1},{3,2},{4,3},{5,4},{6,5},{7,6},{8,7},{9,8},{10,9},{11,1... | collective-permute-start | bytes 245768 | tf_op jit(solution)/shard_map/ppermute | solution.py:403
  42.8 0.3 convolution_convert_fusion.2
  43.1 0.1 copy.37
  43.3 5.6 %convolution_bitcast_fusion = f32[128,2,2,128]{3,2,1,0:T(2,128)S(1)} fusion(bf16[128,2,128,128]{3,2,1,0:T(8,128)(2,1)} %param.16, bf16[2,128,128]{1,0,2:T(2,128)(2,1)S(1)} %copy.37), kind=kOutput, calls=%fused_computation | convolution fusion | flops 16777216 | bytes 8716288 | tf_op jit(solution)/shard_map/pcij,dpj->pcdi/dot_general | solution.py:445
  48.9 0.2 fusion.29
  49.1 0.2 fusion.5
  49.4 0.6 copy-done
  50.0 44.5 %shard_map.146 = bf16[512,128]{1,0:T(8,128)(2,1)} custom-call(bf16[512,128]{1,0:T(8,128)(2,1)} %bitcast.82, bf16[128,2048]{1,0:T(8,128)(2,1)} %constant.23.clone.spread, f32[2,1024,256]{2,1,0:T(8,128)} %copy.33.green, bf16[1024,1024]{1,0:T(8,128)(2,1)} %constant.7.clone.cos, bf16[1024,1024]{1,0:T(8,128)(2,1)} %constant.18.clone.sin), custom_call_target="tpu_custom_call" | custom-call | tf_op jit(solution)/shard_map/pallas_call | solution.py:385
  94.6 3.5 %all-to-all-start.1 = ((bf16[16,32,128]{2,1,0:T(8,128)(2,1)}), bf16[16,32,128]{2,1,0:T(8,128)(2,1)S(1)}, u32[]{:S(2)}, u32[]{:S(2)}) async-start(bf16[16,32,128]{2,1,0:T(8,128)(2,1)} %bitcast.83), calls=%async_computation.1 | async-start | bytes 262144 | tf_op jit(solution)/shard_map/all_to_all | solution.py:504
  98.1 0.4 fusion.1
  98.5 0.7 fusion.20.near
  99.1 6.1 %all-to-all-done.1.recv = bf16[16,32,128]{2,1,0:T(8,128)(2,1)S(1)} async-done(((bf16[16,32,128]{2,1,0:T(8,128)(2,1)}), bf16[16,32,128]{2,1,0:T(8,128)(2,1)S(1)}, u32[]{:S(2)}, u32[]{:S(2)}) %all-to-all-start.1) | async-done | bytes 131104 | tf_op jit(solution)/shard_map/all_to_all | solution.py:504
  105.2 0.6 copy-done.1
  105.9 8.9 %shard_map.147 = f32[32,2,128]{2,1,0:T(2,128)} custom-call(bf16[16,32,128]{2,1,0:T(8,128)(2,1)} %copy-done.1, f32[32,128,128]{2,1,0:T(8,128)} %proj.3, s32[32,128]{1,0:T(8,128)} %cells.3, f32[32,2,128]{2,1,0:T(2,128)} %fusion.20.near, bf16[512,512]{1,0:T(8,128)(2,1)} %constant.19.clone.tch, bf16[512,512]{1,0:T(8,128)(2,1)} %constant.20.clone.tcl, ...), custom_call_target="tpu_custom_call" | custom-call | tf_op jit(solution)/shard_map/pallas_call | solution.py:385
  (24 shorter events, 0.1 us)
Async XLA Ops:
  0.9 31.9 %collective-permute-start = (bf16[2,1,1,32,128]{4,3,2,1,0:T(8,128)(2,1)S(1)}, bf16[2,1,1,32,128]{4,3,2,1,0:T(8,128)(2,1)S(1)}, u32[]{:S(2)}, u32[]{:S(2)}) collective-permute-start(bf16[2,1,1,32,128]{4,3,2,1,0:T(8,128)(2,1)S(1)} %bitcast.89), channel_id=1, source_target_pairs={{0,16},{16,32},{32,48},{48,64},{64,80},{80,96},{96,112},{112,0},{1... | collective-permute-start | bytes 49160 | tf_op jit(solution)/shard_map/ppermute | solution.py:402
  3.9 28.9 %collective-permute-start.1 = (bf16[2,1,1,32,128]{4,3,2,1,0:T(8,128)(2,1)S(1)}, bf16[2,1,1,32,128]{4,3,2,1,0:T(8,128)(2,1)S(1)}, u32[]{:S(2)}, u32[]{:S(2)}) collective-permute-start(bf16[2,1,1,32,128]{4,3,2,1,0:T(8,128)(2,1)S(1)} %bitcast.90), channel_id=1, source_target_pairs={{16,0},{32,16},{48,32},{64,48},{80,64},{96,80},{112,96},{0,112},{1... | collective-permute-start | bytes 49160 | tf_op jit(solution)/shard_map/ppermute | solution.py:403
  4.8 5.3 %copy-start.3 = (s32[1,128]{1,0:T(1,128)S(1)}, s32[1,128]{1,0:T(1,128)}, u32[]{:S(2)}) copy-start(s32[1,128]{1,0:T(1,128)} %param.18) | copy-start | bytes 1540
  10.7 27.0 %collective-permute-start.4 = (bf16[2,1,3,32,128]{4,0,3,2,1:T(2,128)(2,1)S(1)}, bf16[2,1,3,32,128]{4,0,3,2,1:T(2,128)(2,1)S(1)}, u32[]{:S(2)}, u32[]{:S(2)}) collective-permute-start(bf16[2,1,3,32,128]{4,0,3,2,1:T(2,128)(2,1)S(1)} %get-tuple-element.12), channel_id=1, source_target_pairs={{0,16},{16,32},{32,48},{48,64},{64,80},{80,96},{96,112},{112,0},{1... | collective-permute-start | bytes 147464 | tf_op jit(solution)/shard_map/ppermute | solution.py:402
  12.4 25.3 %collective-permute-start.5 = (bf16[2,1,3,32,128]{4,0,3,2,1:T(2,128)(2,1)S(1)}, bf16[2,1,3,32,128]{4,0,3,2,1:T(2,128)(2,1)S(1)}, u32[]{:S(2)}, u32[]{:S(2)}) collective-permute-start(bf16[2,1,3,32,128]{4,0,3,2,1:T(2,128)(2,1)S(1)} %get-tuple-element.13), channel_id=1, source_target_pairs={{16,0},{32,16},{48,32},{64,48},{80,64},{96,80},{112,96},{0,112},{1... | collective-permute-start | bytes 147464 | tf_op jit(solution)/shard_map/ppermute | solution.py:403
  22.4 26.9 %all-to-all-start = ((bf16[16,32,128]{2,1,0:T(8,128)(2,1)}), bf16[16,32,128]{2,1,0:T(8,128)(2,1)S(1)}, u32[]{:S(2)}, u32[]{:S(2)}) async-start(bf16[16,32,128]{2,1,0:T(8,128)(2,1)} %shard_map.145), calls=%async_computation | async-start | bytes 262144 | tf_op jit(solution)/shard_map/all_to_all | solution.py:477
  32.9 10.0 %collective-permute-start.2 = (bf16[2,3,1,32,128]{4,3,2,1,0:T(8,128)(2,1)S(1)}, bf16[2,3,1,32,128]{4,3,2,1,0:T(8,128)(2,1)S(1)}, u32[]{:S(2)}, u32[]{:S(2)}) collective-permute-start(bf16[2,3,1,32,128]{4,3,2,1,0:T(8,128)(2,1)S(1)} %constant_dynamic-update-slice_fusion), channel_id=1, source_target_pairs={{0,1},{1,2},{2,3},{3,4},{4,5},{5,6},{6,7},{7,8},{8,9},{9,10},{10,1... | collective-permute-start | bytes 147464 | tf_op jit(solution)/shard_map/ppermute | solution.py:402
  34.3 8.5 %collective-permute-start.3 = (bf16[2,3,1,32,128]{4,3,2,1,0:T(8,128)(2,1)S(1)}, bf16[2,3,1,32,128]{4,3,2,1,0:T(8,128)(2,1)S(1)}, u32[]{:S(2)}, u32[]{:S(2)}) collective-permute-start(bf16[2,3,1,32,128]{4,3,2,1,0:T(8,128)(2,1)S(1)} %constant_dynamic-update-slice_fusion), channel_id=1, source_target_pairs={{1,0},{2,1},{3,2},{4,3},{5,4},{6,5},{7,6},{8,7},{9,8},{10,9},{11,1... | collective-permute-start | bytes 147464 | tf_op jit(solution)/shard_map/ppermute | solution.py:403
  38.0 60.1 %collective-permute-start.6 = (bf16[2,5,1,32,128]{4,0,3,2,1:T(2,128)(2,1)S(1)}, bf16[2,5,1,32,128]{4,0,3,2,1:T(2,128)(2,1)S(1)}, u32[]{:S(2)}, u32[]{:S(2)}) collective-permute-start(bf16[2,5,1,32,128]{4,0,3,2,1:T(2,128)(2,1)S(1)} %get-tuple-element.10), channel_id=1, source_target_pairs={{0,1},{1,2},{2,3},{3,4},{4,5},{5,6},{6,7},{7,8},{8,9},{9,10},{10,1... | collective-permute-start | bytes 245768 | tf_op jit(solution)/shard_map/ppermute | solution.py:402
  38.0 60.1 %collective-permute-start.7 = (bf16[2,5,1,32,128]{4,0,3,2,1:T(2,128)(2,1)S(1)}, bf16[2,5,1,32,128]{4,0,3,2,1:T(2,128)(2,1)S(1)}, u32[]{:S(2)}, u32[]{:S(2)}) collective-permute-start(bf16[2,5,1,32,128]{4,0,3,2,1:T(2,128)(2,1)S(1)} %get-tuple-element.11), channel_id=1, source_target_pairs={{1,0},{2,1},{3,2},{4,3},{5,4},{6,5},{7,6},{8,7},{9,8},{10,9},{11,1... | collective-permute-start | bytes 245768 | tf_op jit(solution)/shard_map/ppermute | solution.py:403
  43.2 5.9 %copy-start.2 = (s32[1,128]{1,0:T(1,128)S(1)}, s32[1,128]{1,0:T(1,128)}, u32[]{:S(2)}) copy-start(s32[1,128]{1,0:T(1,128)} %param.17) | copy-start | bytes 1540
  49.4 0.6 copy-start
  94.6 10.6 %all-to-all-start.1 = ((bf16[16,32,128]{2,1,0:T(8,128)(2,1)}), bf16[16,32,128]{2,1,0:T(8,128)(2,1)S(1)}, u32[]{:S(2)}, u32[]{:S(2)}) async-start(bf16[16,32,128]{2,1,0:T(8,128)(2,1)} %bitcast.83), calls=%async_computation.1 | async-start | bytes 262144 | tf_op jit(solution)/shard_map/all_to_all | solution.py:504
  105.2 0.6 copy-start.1

commit v3 on v2

--- a/solution.py
+++ b/solution.py
@@ -15,6 +15,7 @@
 NCOL = 16
 NB = 32
 BLK = 128
+PAIRS = 128
 XR = 144
 WIDE_Y = 68
 BF = jnp.bfloat16
@@ -91,24 +92,34 @@
     return jnp.where(iota((512, 128), 0) == code_row, 1.0, 0.0).astype(BF)
 
 
-def project_kernel(cur, proj, cells, tch, tcl, tsh, tsl, out, codes, boxed):
+def project(cur, proj, cells, tch, tcl, tsh, tsl, out, codes, p_high, p_low, hots, vals, boxed):
     code, corner_x, corner_y = cell_codes(cells[...])
     codes[...] = code
 
-    def block(i, carry):
-        for u in range(4):
-            g = i * 4 + u
-            lhs = rows_high_low(cur[g])
-            p_high, p_low = high_low(proj[g])
-            first = dot_nt(lhs, p_high)
-            values = first[0:2] + first[2:4] + dot_nt(lhs, p_low)[0:2]
+    def values_of(i, carry):
+        for u in range(8):
+            g = i * 8 + u
+            lhs = rows_high_low(cur[:, pl.ds(pl.multiple_of(g * BLK, BLK), BLK)])
+            high, low = high_low(proj[g])
+            p_high[g] = high
+            p_low[g] = low
+            first = dot_nt(lhs, high)
+            vals[g] = first[0:2] + first[2:4] + dot_nt(lhs, low)[0:2]
+        return carry
+
+    lax.fori_loop(0, NB // 8, values_of, 0)
+
+    def boxes_of(i, carry):
+        for u in range(8):
+            g = i * 8 + u
             hot = one_hot_rows(codes[pl.ds(g, 1), :])
-            placed = dot_nt(rows_high_low(values), hot)
+            hots[g] = hot
+            placed = dot_nt(rows_high_low(vals[g]), hot)
             boxed[pl.ds(g, 1), :] = placed[0:1] + placed[2:3]
             boxed[pl.ds(NB + g, 1), :] = placed[1:2] + placed[3:4]
         return carry
 
-    lax.fori_loop(0, NB // 4, block, 0)
+    lax.fori_loop(0, NB // 8, boxes_of, 0)
     b_high, b_low = high_low(boxed[...])
     along_cos = dot(b_high, tch[...]) + dot(b_low, tch[...]) + dot(b_high, tcl[...])
     along_sin = dot(b_high, tsh[...]) + dot(b_low, tsh[...]) + dot(b_high, tsl[...])
@@ -118,7 +129,8 @@
     corners = jnp.where(lane == 0, corner_x, jnp.where(lane == 1, corner_y, 0)).astype(F32)
     for c in range(NCOL):
         part = slice(32 * c, 32 * c + 32)
-        out[c] = jnp.concatenate([real[:, part], imag[:, part], corners], axis=1).astype(BF)
+        message = jnp.concatenate([real[:, part], imag[:, part], corners], axis=1)
+        out[NB * c : NB * c + NB, :] = message.astype(BF)
 
 
 def local_x_of_row(shape, dim):
@@ -286,55 +298,243 @@
                 acc[rows, lanes] = acc[rows, lanes] + taken[:, 128 * c : 128 * c + 128]
 
 
-def middle_kernel(
-    recv, spread, green, cos, sin, out,
+def back_project(recv, near, tch, tcl, tsh, tsl, out, p_high, p_low, hots, box_real, box_imag, vals):
+    real = jnp.concatenate([recv[NB * c : NB * c + NB, 0:32] for c in range(NCOL)], axis=1)
+    imag = jnp.concatenate([recv[NB * c : NB * c + NB, 32:64] for c in range(NCOL)], axis=1)
+    both = jnp.concatenate([real, imag], axis=0)
+    along_cos = dot(both, tch[...]) + dot(both, tcl[...])
+    along_sin = dot(both, tsh[...]) + dot(both, tsl[...])
+    box_real[...] = along_cos[:NB] - along_sin[NB:]
+    box_imag[...] = along_cos[NB:] + along_sin[:NB]
+
+    def values_of(i, carry):
+        for u in range(8):
+            g = i * 8 + u
+            box = jnp.concatenate([box_real[pl.ds(g, 1), :], box_imag[pl.ds(g, 1), :]], axis=0)
+            picked = dot(rows_high_low(box), hots[g])
+            vals[g] = picked[0:2] + picked[2:4]
+        return carry
+
+    lax.fori_loop(0, NB // 8, values_of, 0)
+
+    def blocks_of(i, carry):
+        for u in range(8):
+            g = i * 8 + u
+            lhs = rows_high_low(vals[g])
+            first = dot(lhs, p_high[g])
+            far = first[0:2] + first[2:4] + dot(lhs, p_low[g])[0:2]
+            row = near[pl.ds(g, 1), :]
+            beside = jnp.concatenate([row[:, :BLK], row[:, BLK:]], axis=0)
+            out[:, pl.ds(pl.multiple_of(g * BLK, BLK), BLK)] = far + beside
+        return carry
+
+    lax.fori_loop(0, NB // 8, blocks_of, 0)
+
+
+def column_of(row):
+    return jnp.transpose(jnp.broadcast_to(row.astype(F32), (8, 128)))[:, 0:1].astype(jnp.int32)
+
+
+def near_backward(beside, owned, picks, count, matrices, back_a, lv_one, lv_two, spread_back):
+    hits = jnp.where(iota((PAIRS, NB), 1) == column_of(owned[...]), 1.0, 0.0).astype(BF)
+    local = dot(hits, beside[4])
+    real, imag = local[:, :BLK], local[:, BLK:]
+    lv_one[...] = jnp.concatenate([real, -imag], axis=1)
+    lv_two[...] = jnp.concatenate([imag, real], axis=1)
+    first_row = iota((8, 2 * BLK), 0) == 0
+
+    def pairs_of(i, carry):
+        for u in range(8):
+            p = i * 8 + u
+            lhs = jnp.where(first_row, lv_one[pl.ds(p, 1), :], lv_two[pl.ds(p, 1), :]).astype(BF)
+            got = dot(lhs, matrices[p])
+            back_a[pl.ds(p, 1), :] = jnp.concatenate([got[0:1], got[1:2]], axis=1)
+        return carry
+
+    lax.fori_loop(0, PAIRS // 8, pairs_of, 0)
+    alive = iota((9 * NB, PAIRS), 1) < count[0]
+    hits = (iota((9 * NB, PAIRS), 0) == picks[...]) & alive
+    table = jnp.where(hits, 1.0, 0.0).astype(BF)
+    high, low = high_low(back_a[...])
+    total = (dot(table, high) + dot(table, low)).astype(BF)
+    for n in range(9):
+        spread_back[n] = total[NB * n : NB * n + NB, :]
+
+
+def near_onward(beside, owned, picks, count, matrices, on_a, on_b, lv_one, near):
+    hits = jnp.where(iota((PAIRS, 9 * NB), 1) == column_of(picks[...]), 1.0, 0.0).astype(BF)
+    lv_one[...] = dot(hits, jnp.concatenate([beside[n] for n in range(9)], axis=0))
+    first_row = iota((8, BLK), 0) == 0
+
+    def pairs_of(i, carry):
+        for u in range(8):
+            p = i * 8 + u
+            row = lv_one[pl.ds(p, 1), :]
+            lhs = jnp.where(first_row, row[:, :BLK], row[:, BLK:]).astype(BF)
+            got = dot_nt(lhs, matrices[p])
+            on_a[pl.ds(p, 1), :] = got[0:1]
+            on_b[pl.ds(p, 1), :] = got[1:2]
+        return carry
+
+    lax.fori_loop(0, PAIRS // 8, pairs_of, 0)
+    real = on_a[:, :BLK] - on_b[:, BLK:]
+    imag = on_b[:, :BLK] + on_a[:, BLK:]
+    alive = iota((NB, PAIRS), 1) < count[0]
+    table = jnp.where((iota((NB, PAIRS), 0) == owned[...]) & alive, 1.0, 0.0).astype(BF)
+    high, low = high_low(jnp.concatenate([real, imag], axis=1))
+    near[...] = dot(table, high) + dot(table, low)
+
+
+def turn_green(green, turned):
+    for c in range(2):
+        for kz in range(2):
+
+            def part(i, carry):
+                rows = pl.ds(pl.multiple_of(i * 128, 128), 128)
+                block = jnp.transpose(green[c, kz, :, rows])
+                turned[c, rows, 128 * kz : 128 * kz + 128] = block * (1.0 / (N * N * NGZ))
+                return carry
+
+            lax.fori_loop(0, 8, part, 0)
+
+
+def whole_kernel(
+    cur, cells, owned, picks, count, near_hbm, proj_hbm, green_hbm,
+    tch_hbm, tcl_hbm, tsh_hbm, tsl_hbm, spread_hbm, cos_hbm, sin_hbm, out,
+    matrices, proj, green, tch, tcl, tsh, tsl, spread, cos, sin, load_sem,
+    codes, p_high, p_low, hots, vals, boxed, box_real, box_imag,
+    beside, spread_back, back, on_a, on_b, lv_one, lv_two, near, turned,
     wide, starts, img, hot, acc, spec, pot, d_one, d_two, h_one, h_two,
     send_a, recv_a, send_b, recv_b, sem_send_a, sem_recv_a, sem_send_b, sem_recv_b,
+    send_c, recv_c, send_d, recv_d, sem_send_c, sem_recv_c, sem_send_d, sem_recv_d,
+    sem_send_h, sem_recv_h, sem_send_r, sem_recv_r,
 ):
-    me = lax.axis_index("row")
+    row, col = lax.axis_index("row"), lax.axis_index("col")
+    mesh_ids = pl.DeviceIdType.MESH
+
+    def row_peer(j):
+        return (lax.rem(row + j, NROW), col)
+
+    def col_peer(j):
+        return (row, lax.rem(col + j, NCOL))
+
+    def tile_peer(n):
+        return (lax.rem(row + n // 3 - 1 + NROW, NROW), lax.rem(col + n % 3 - 1 + NCOL, NCOL))
+
     barrier = pltpu.get_barrier_semaphore()
-    for j in range(1, NROW):
-        peer = lax.rem(me + j, NROW)
-        pl.semaphore_signal(
-            barrier, inc=1, device_id={"row": peer}, device_id_type=pl.DeviceIdType.MESH
+    peers = [row_peer(j) for j in range(1, NROW)] + [col_peer(j) for j in range(1, NCOL)]
+    peers += [tile_peer(n) for n in (0, 2, 6, 8)]
+    for peer in peers:
+        pl.semaphore_signal(barrier, inc=1, device_id=peer, device_id_type=mesh_ids)
+
+    pairs = [
+        (proj_hbm, proj), (tch_hbm, tch), (tcl_hbm, tcl), (tsh_hbm, tsh), (tsl_hbm, tsl),
+        (near_hbm, matrices), (spread_hbm, spread), (cos_hbm, cos), (sin_hbm, sin),
+        (green_hbm, green),
+    ]
+    loads = [pltpu.make_async_copy(a, b, load_sem.at[i]) for i, (a, b) in enumerate(pairs)]
+    for load in loads:
+        load.start()
+
+    def remote(source, target, sem_send, sem_recv, peer):
+        return pltpu.make_async_remote_copy(
+            src_ref=source,
+            dst_ref=target,
+            send_sem=sem_send,
+            recv_sem=sem_recv,
+            device_id=peer,
+            device_id_type=mesh_ids,
         )
 
-    def copies(kz, source, target, sem_send, sem_recv):
-        result = []
-        for j in range(1, NROW):
-            peer = lax.rem(me + j, NROW)
-            result.append(
-                pltpu.make_async_remote_copy(
-                    src_ref=source.at[kz, peer],
-                    dst_ref=target.at[kz, me],
-                    send_sem=sem_send.at[kz, j],
-                    recv_sem=sem_recv.at[kz, j],
-                    device_id={"row": peer},
-                    device_id_type=pl.DeviceIdType.MESH,
-                )
+    def row_copies(kz, source, target, sem_send, sem_recv):
+        return [
+            remote(
+                source.at[kz, row_peer(j)[0]],
+                target.at[kz, row],
+                sem_send.at[kz, j],
+                sem_recv.at[kz, j],
+                row_peer(j),
             )
-        return result
-
-    build_image(recv, spread, wide, starts, img)
+            for j in range(1, NROW)
+        ]
+
+    def tile_rows(c):
+        return pl.ds(pl.multiple_of(c * NB, NB), NB)
+
+    def col_copies(source, target, sem_send, sem_recv):
+        return [
+            remote(
+                source.at[tile_rows(col_peer(j)[1])],
+                target.at[tile_rows(col)],
+                sem_send.at[j],
+                sem_recv.at[j],
+                col_peer(j),
+            )
+            for j in range(1, NCOL)
+        ]
+
+    for g in range(NB):
+        two = cur[:, BLK * g : BLK * g + BLK]
+        vals[g] = two
+    rounded = jnp.concatenate([vals[:, 0, :], vals[:, 1, :]], axis=1).astype(BF)
+    beside[4] = rounded
+    for load in loads[:5]:
+        load.wait()
+    project(cur, proj, cells, tch, tcl, tsh, tsl, send_c, codes, p_high, p_low, hots, vals, boxed)
+    pl.semaphore_wait(barrier, len(peers))
+    third = col_copies(send_c, recv_c, sem_send_c, sem_recv_c)
+    for copy in third:
+        copy.start()
+    halo = [
+        remote(beside.at[4], beside.at[8 - n], sem_send_h.at[n], sem_recv_h.at[n], tile_peer(n))
+        for n in range(9)
+        if n != 4
+    ]
+    for copy in halo:
+        copy.start()
+    recv_c[tile_rows(col), :] = send_c[tile_rows(col), :]
+    loads[5].wait()
+    near_backward(beside, owned, picks, count, matrices, on_a, lv_one, lv_two, spread_back)
+    back[4] = spread_back[4]
+    returns = [
+        remote(spread_back.at[n], back.at[8 - n], sem_send_r.at[n], sem_recv_r.at[n], tile_peer(n))
+        for n in range(9)
+        if n != 4
+    ]
+    for copy in returns:
+        copy.start()
+    for load in loads[6:]:
+        load.wait()
+    for copy in third:
+        copy.wait_recv()
+    build_image(recv_c, spread, wide, starts, img)
     first, second = [], []
     for kz in range(2):
         forward_y(kz, img, cos, sin, send_a)
-        if kz == 0:
-            pl.semaphore_wait(barrier, NROW - 1)
-        first.append(copies(kz, send_a, recv_a, sem_send_a, sem_recv_a))
+        first.append(row_copies(kz, send_a, recv_a, sem_send_a, sem_recv_a))
         for copy in first[kz]:
             copy.start()
-        recv_a[kz, me] = send_a[kz, me]
-    build_hot(recv, hot)
-    acc[...] = jnp.zeros_like(acc)
+        recv_a[kz, row] = send_a[kz, row]
+    turn_green(green, turned)
+    for copy in halo:
+        copy.wait_recv()
+    near_onward(beside, owned, picks, count, matrices, on_a, on_b, lv_one, near)
     for kz in range(2):
         for copy in first[kz]:
             copy.wait_recv()
-        along_x(kz, recv_a, green, cos, sin, send_b, d_one, d_two, h_one, h_two)
-        second.append(copies(kz, send_b, recv_b, sem_send_b, sem_recv_b))
+        along_x(kz, recv_a, turned, cos, sin, send_b, d_one, d_two, h_one, h_two)
+        second.append(row_copies(kz, send_b, recv_b, sem_send_b, sem_recv_b))
         for copy in second[kz]:
             copy.start()
-        recv_b[kz, me] = send_b[kz, me]
+        recv_b[kz, row] = send_b[kz, row]
+    build_hot(recv_c, hot)
+    acc[...] = jnp.zeros_like(acc)
+    for copy in returns:
+        copy.wait_recv()
+    total = near[...]
+    for n in range(9):
+        total = total + back[n].astype(F32)
+    near[...] = total
     for kz in range(2):
         for copy in second[kz]:
             copy.wait_recv()
@@ -346,175 +546,86 @@
     def fold(i, carry):
         rows = pl.ds(pl.multiple_of(i * 128, 128), 128)
         wide_rows = pl.ds(pl.multiple_of(i * 128 + NB, NB), 128)
-        out[rows, :] = dot_nt(acc[wide_rows, :], spread[...]).astype(BF)
+        send_d[rows, :] = dot_nt(acc[wide_rows, :], spread[...]).astype(BF)
         return carry
 
     lax.fori_loop(0, 4, fold, 0)
-    for kz in range(2):
-        for copy in first[kz] + second[kz]:
-            copy.wait_send()
-
-
-def back_kernel(recv, proj, cells, near, tch, tcl, tsh, tsl, out, codes, box_real, box_imag):
-    code, _, _ = cell_codes(cells[...])
-    codes[...] = code
-    real = jnp.concatenate([recv[c, :, 0:32] for c in range(NCOL)], axis=1)
-    imag = jnp.concatenate([recv[c, :, 32:64] for c in range(NCOL)], axis=1)
-    both = jnp.concatenate([real, imag], axis=0)
-    along_cos = dot(both, tch[...]) + dot(both, tcl[...])
-    along_sin = dot(both, tsh[...]) + dot(both, tsl[...])
-    box_real[...] = along_cos[:NB] - along_sin[NB:]
-    box_imag[...] = along_cos[NB:] + along_sin[:NB]
-
-    def block(i, carry):
-        for u in range(4):
-            g = i * 4 + u
-            box = jnp.concatenate([box_real[pl.ds(g, 1), :], box_imag[pl.ds(g, 1), :]], axis=0)
-            hot = one_hot_rows(codes[pl.ds(g, 1), :])
-            picked = dot(rows_high_low(box), hot)
-            lhs = rows_high_low(picked[0:2] + picked[2:4])
-            p_high, p_low = high_low(proj[g])
-            first = dot(lhs, p_high)
-            out[g] = first[0:2] + first[2:4] + dot(lhs, p_low)[0:2] + near[g]
-        return carry
-
-    lax.fori_loop(0, NB // 4, block, 0)
-
-
-def call(kernel, out_shape, scratch, *args, **params):
-    return pl.pallas_call(
-        kernel,
-        out_shape=out_shape,
-        in_specs=[pl.BlockSpec(memory_space=pltpu.VMEM)] * len(args),
-        out_specs=pl.BlockSpec(memory_space=pltpu.VMEM),
-        scratch_shapes=scratch,
-        compiler_params=pltpu.CompilerParams(vmem_limit_bytes=VMEM_LIMIT, **params),
-    )(*args)
-
-
-def with_halo(value, sides, width):
-    for axis, dim in sides:
-        peers, length = (lax.axis_size(axis), value.shape[dim])
-        up = [(i, (i + 1) % peers) for i in range(peers)]
-        down = [(j, i) for i, j in up]
-        last = lax.slice_in_dim(value, length - width, length, axis=dim)
-        first = lax.slice_in_dim(value, 0, width, axis=dim)
-        before = lax.ppermute(last, axis, up)
-        after = lax.ppermute(first, axis, down)
-        value = jnp.concatenate([before, value, after], axis=dim)
-    return value
-
-
-def combine_parts(products):
-    return jnp.stack(
-        [products[:, 0, 0] - products[:, 1, 1], products[:, 0, 1] + products[:, 1, 0]], axis=1
+    fourth = col_copies(send_d, recv_d, sem_send_d, sem_recv_d)
+    for copy in fourth:
+        copy.start()
+    recv_d[tile_rows(col), :] = send_d[tile_rows(col), :]
+    for copy in fourth:
+        copy.wait_recv()
+    back_project(
+        recv_d, near, tch, tcl, tsh, tsl, out, p_high, p_low, hots, box_real, box_imag, vals
     )
-
-
-def fold_rims(field, axis_pos, inner, width):
-    middle = lax.slice_in_dim(field, 2 * width, 2 * width + inner, axis=axis_pos)
-    lower = lax.slice_in_dim(field, 0, width, axis=axis_pos)
-    upper = lax.slice_in_dim(field, inner + 3 * width, inner + 4 * width, axis=axis_pos)
-    lower_pads = [(0, 0)] * field.ndim
-    upper_pads = [(0, 0)] * field.ndim
-    lower_pads[axis_pos] = (0, inner - width)
-    upper_pads[axis_pos] = (inner - width, 0)
-    return middle + jnp.pad(lower, lower_pads) + jnp.pad(upper, upper_pads)
-
-
-def near_part(blocks, near_blocks, pair_local, pair_ghost, pair_counts):
-    num_blocks, block_len = NB, BLK
-    pair_slots = pair_ghost.shape[1]
-    high = lax.Precision.HIGHEST
-    local_bf = blocks.astype(BF)
-    beside_all = with_halo(
-        local_bf.reshape(2, 1, 1, num_blocks, block_len), (("row", 1), ("col", 2)), 1
-    )
-    beside_all = beside_all.reshape(2, 9 * num_blocks, block_len)
-    picks = pair_ghost[0]
-    owned = pair_local[0]
-    living = (jnp.arange(pair_slots, dtype=jnp.int32) < pair_counts[0]).astype(F32)
-    owner_table = owned[:, None] == jnp.arange(num_blocks, dtype=jnp.int32)[None, :]
-    ghost_table = picks[:, None] == jnp.arange(9 * num_blocks, dtype=jnp.int32)[None, :]
-    remote_vals = jnp.einsum(
-        "ho,som->shm", ghost_table.astype(BF), beside_all, preferred_element_type=F32
-    ).astype(BF)
-    local_vals = jnp.einsum(
-        "ho,som->shm", owner_table.astype(BF), local_bf, preferred_element_type=F32
-    ).astype(BF)
-    onward = jnp.einsum("pcij,dpj->pcdi", near_blocks, remote_vals, preferred_element_type=F32)
-    backward = jnp.einsum("pcij,dpi->pcdj", near_blocks, local_vals, preferred_element_type=F32)
-    onward = combine_parts(onward) * living[:, None, None]
-    backward = combine_parts(backward) * living[:, None, None]
-    near_own = jnp.einsum("pn,pcb->cnb", owner_table.astype(F32), onward, precision=high)
-    spread_back = jnp.einsum("pn,pcb->cnb", ghost_table.astype(F32), backward, precision=high)
-    spread_back = spread_back.reshape(2, 3, 3, num_blocks, block_len)
-    widened_back = with_halo(spread_back.astype(BF), (("row", 1), ("col", 2)), 1).astype(F32)
-    returned = fold_rims(fold_rims(widened_back, 1, 1, 1), 2, 1, 1).reshape(
-        2, num_blocks, block_len
-    )
-    return near_own + returned
+    for copy in first[0] + first[1] + second[0] + second[1] + third + fourth + halo + returns:
+        copy.wait_send()
 
 
 def per_device(
     currents, near_blocks, pair_local, pair_ghost, pair_counts, projection, stencil_cells, green
 ):
-    cos, sin = (jnp.asarray(t) for t in grid_tables())
-    depth = [jnp.asarray(t) for t in depth_tables()]
-    spread = jnp.asarray(spread_table())
-    shape = jax.ShapeDtypeStruct
-    blocks = currents.reshape(2, NB, BLK)
-    near = near_part(blocks, near_blocks, pair_local, pair_ghost, pair_counts)
-    messages = call(
-        project_kernel,
-        shape((NCOL, NB, 128), BF),
-        [pltpu.VMEM((NB, 128), jnp.int32), pltpu.VMEM((2 * NB, 512), F32)],
-        jnp.transpose(blocks, (1, 0, 2)),
+    tables = [jnp.asarray(t) for t in depth_tables()]
+    tables.append(jnp.asarray(spread_table()))
+    tables += [jnp.asarray(t) for t in grid_tables()]
+    vmem, dma = pltpu.VMEM, pltpu.SemaphoreType.DMA
+    grid_part = (2, NROW, 2 * XR, 128)
+    wrapped = 512 + 2 * NB
+    scratch = [
+        vmem((PAIRS, 2 * BLK, BLK), BF),
+        vmem((NB, BLK, BLK), F32),
+        vmem((2, 2, 128, N), F32),
+        *[vmem((512, 512), BF)] * 4,
+        vmem((128, 2048), BF),
+        *[vmem((N, N), BF)] * 2,
+        dma((10,)),
+        vmem((NB, BLK), jnp.int32),
+        *[vmem((NB, BLK, BLK), BF)] * 2,
+        vmem((NB, 512, BLK), BF),
+        vmem((NB, 2, BLK), F32),
+        vmem((2 * NB, 512), F32),
+        *[vmem((NB, 512), F32)] * 2,
+        *[vmem((9, NB, 2 * BLK), BF)] * 3,
+        *[vmem((PAIRS, 2 * BLK), F32)] * 4,
+        vmem((NB, 2 * BLK), F32),
+        vmem((2, N, 256), F32),
+        vmem((wrapped, 2048), BF),
+        vmem((wrapped, 128), jnp.int32),
+        vmem((2, 2 * XR, N), BF),
+        vmem((4, wrapped, XR), BF),
+        vmem((wrapped, 2048), BF),
+        *[vmem((2 * XR, N), BF)] * 2,
+        *[vmem((N, 256), BF)] * 4,
+        *[vmem(grid_part, BF)] * 4,
+        *[dma((2, NROW))] * 4,
+        *[vmem((NCOL * NB, 128), BF)] * 4,
+        *[dma((NCOL,))] * 4,
+        *[dma((9,))] * 4,
+    ]
+    in_vmem = pl.BlockSpec(memory_space=pltpu.VMEM)
+    in_smem = pl.BlockSpec(memory_space=pltpu.SMEM)
+    anywhere = pl.BlockSpec(memory_space=pl.ANY)
+    return pl.pallas_call(
+        whole_kernel,
+        out_shape=jax.ShapeDtypeStruct((2, NB * BLK), F32),
+        in_specs=[in_vmem] * 4 + [in_smem] + [anywhere] * 10,
+        out_specs=in_vmem,
+        scratch_shapes=scratch,
+        compiler_params=pltpu.CompilerParams(
+            vmem_limit_bytes=VMEM_LIMIT, collective_id=1, has_side_effects=True
+        ),
+    )(
+        currents,
+        stencil_cells,
+        pair_local,
+        pair_ghost,
+        pair_counts,
+        near_blocks.reshape(PAIRS, 2 * BLK, BLK),
         projection,
-        stencil_cells,
-        *depth,
+        green,
+        *tables,
     )
-    sources = lax.all_to_all(messages, "col", split_axis=0, concat_axis=0, tiled=True)
-    sources = sources.reshape(NCOL * NB, 128)
-    turned = jnp.transpose(green, (0, 3, 1, 2)).reshape(2, N, 256) * (1.0 / (N * N * NGZ))
-    grid_bytes = (2, NROW, 2 * XR, 128)
-    taken = call(
-        middle_kernel,
-        shape((NCOL * NB, 128), BF),
-        [
-            pltpu.VMEM((512 + 2 * NB, 2048), BF),
-            pltpu.VMEM((512 + 2 * NB, 128), jnp.int32),
-            pltpu.VMEM((2, 2 * XR, N), BF),
-            pltpu.VMEM((4, 512 + 2 * NB, XR), BF),
-            pltpu.VMEM((512 + 2 * NB, 2048), BF),
-            pltpu.VMEM((2 * XR, N), BF),
-            pltpu.VMEM((2 * XR, N), BF),
-        ]
-        + [pltpu.VMEM((N, 256), BF)] * 4
-        + [pltpu.VMEM(grid_bytes, BF)] * 4
-        + [pltpu.SemaphoreType.DMA((2, NROW))] * 4,
-        sources,
-        spread,
-        turned,
-        cos,
-        sin,
-        collective_id=1,
-        has_side_effects=True,
-    )
-    messages = lax.all_to_all(
-        taken.reshape(NCOL, NB, 128), "col", split_axis=0, concat_axis=0, tiled=True
-    )
-    total = call(
-        back_kernel,
-        shape((NB, 2, BLK), F32),
-        [pltpu.VMEM((NB, 128), jnp.int32), pltpu.VMEM((NB, 512), F32), pltpu.VMEM((NB, 512), F32)],
-        messages,
-        projection,
-        stencil_cells,
-        jnp.transpose(near, (1, 0, 2)),
-        *depth,
-    )
-    return jnp.transpose(total, (1, 0, 2)).reshape(2, NB * BLK)
 
 
 def solution(mesh):

time: 115 us -> 66.9 us (0.58)
  starting transfers between devices: 25 us -> 0 us
  matrix products: 11.9 us -> 0 us
  waiting for transfers between devices: 6.08 us -> 0 us
  other arithmetic: 4.12 us -> 0 us
  local copies, waits for them, and re-layouts: 3.49 us -> 1.38 us
  Pallas kernels: 63.2 us -> 64.6 us
    ppermute x8 -> x0, starting transfers between devices: 14.8 us -> none  [the longest x4 8.46 us: with_halo(): after = lax.ppermute(first, axis, down)]
    dot_general x6 -> x0, matrix products: 11.9 us -> none  [the longest x1 5.64 us: near_part(): jnp.einsum('pcij,dpj->pcdi', near_blocks, remote_vals, preferred_element_...]
    all_to_all x2 -> x0, starting transfers between devices: 10.3 us -> none  [the longest x1 6.75 us: per_device(): lax.all_to_all(messages, 'col', split_axis=0, concat_axis=0, tiled=True)]
    all_to_all x2 -> x0, waiting for transfers between devices: 6.06 us -> none  [the longest x1 6.06 us: per_device(): lax.all_to_all(taken.reshape(NCOL, NB, 128), 'col', split_axis=0, concat_...]
    mul x1 -> x0, local copies, waits for them, and re-layouts: 1.84 us -> none  [per_device(): jnp.transpose(green, (0, 3, 1, 2)).reshape(2, N, 256)]
    mul x1 -> x0, other arithmetic: 1.77 us -> none  [per_device(): jnp.transpose(green, (0, 3, 1, 2)).reshape(2, N, 256)]
    pallas_call x3 -> x1, Pallas kernels: 63.2 us -> 64.6 us  [per_device(): pl.pallas_call(whole_kernel, out_shape=jax.ShapeDtypeStruct((2, NB * BLK)...]
  transfers between devices with their start and end apart: 10 -> 0, of which waited for: 1 -> 0; matrix products, arithmetic and copies ran while one was open for 15% -> 0% of each run, Pallas kernels for 47% -> 0%
where the time goes in v3:
time: 66.9 us; the launch traced here: 66.7 us
  Pallas kernels  64.6 us (97%)
  local copies, waits for them, and re-layouts  1.38 us (2%)
    pallas_call x1, Pallas kernels, per_device(): pl.pallas_call(whole_kernel, out_shape=jax.ShapeDtypeStruct((2, NB * BLK)...  64.6 us
    unnamed x1, local copies, waits for them, and re-layouts  1.38 us

profile of v3, /device:TPU:1, one launch (start us, length us, event | category | flops | bytes accessed | tf_op | source)
XLA Modules:
  0.0 66.7 jit_solution(7880649371311402830)
XLA Ops:
  0.7 64.6 %shard_map.145 = f32[2,4096]{1,0:T(2,128)} custom-call(f32[2,4096]{1,0:T(2,128)} %cur.1, s32[32,128]{1,0:T(8,128)} %cells.1, s32[1,128]{1,0:T(1,128)} %owned.1, s32[1,128]{1,0:T(1,128)} %picks.1, s32[1]{0:T(128)S(6)} %copy.17.count, bf16[128,256,128]{2,1,0:T(8,128)(2,1)} %bitcast.1, f32[32,128,128]{2,1,0:T(8,128)} %proj_hbm.1, ...), custom_call_target="tpu_custom_call" | custom-call | tf_op jit(solution)/shard_map/pallas_call | solution.py:609
  65.3 1.4 %copy.18 = f32[2,4096]{1,0:T(2,128)} copy(f32[2,4096]{1,0:T(2,128)} %shard_map.145) | data formatting | bytes 65536

commit v4 on v3

--- a/solution.py
+++ b/solution.py
@@ -181,19 +181,15 @@
                 img[kz, XR * c : XR * c + XR, 128 * q : 128 * q + 128] = cells[:, 128 * p : 128 * p + 128]
 
 
-def forward_y(kz, img, cos, sin, out):
-    def lanes_of(i, carry):
-        lanes = pl.ds(pl.multiple_of(i * 256, 256), 256)
-        by_cos = dot(img[kz], cos[:, lanes])
-        by_sin = dot(img[kz], sin[:, lanes])
-        real = (by_cos[:XR] + by_sin[XR:]).astype(BF)
-        imag = (by_cos[XR:] - by_sin[:XR]).astype(BF)
-        for j in range(2):
-            out[kz, 2 * i + j, 0:XR, :] = real[:, 128 * j : 128 * j + 128]
-            out[kz, 2 * i + j, XR:, :] = imag[:, 128 * j : 128 * j + 128]
-        return carry
-
-    lax.fori_loop(0, 4, lanes_of, 0)
+def forward_y(kz, chip, img, cos, sin, out, slot):
+    lanes = pl.ds(pl.multiple_of(chip * 256, 256), 256)
+    by_cos = dot(img[kz], cos[:, lanes])
+    by_sin = dot(img[kz], sin[:, lanes])
+    real = (by_cos[:XR] + by_sin[XR:]).astype(BF)
+    imag = (by_cos[XR:] - by_sin[:XR]).astype(BF)
+    for j in range(2):
+        out[kz, slot + j, 0:XR, :] = real[:, 128 * j : 128 * j + 128]
+        out[kz, slot + j, XR:, :] = imag[:, 128 * j : 128 * j + 128]
 
 
 def along_x(kz, recv, green, cos, sin, out, d_one, d_two, h_one, h_two):
@@ -259,14 +255,19 @@
     lax.fori_loop(0, NROW, rims, 0)
 
 
-def inverse_y(kz, recv, cos, sin, spec, pot):
-    for r in range(NROW):
-        spec[:, 128 * r : 128 * r + 128] = recv[kz, r]
+def inverse_y(kz, recv, slots, chips, cos, sin, spec, pot):
+    for m, slot in enumerate(slots):
+        for j in range(2):
+            spec[:, 256 * m + 128 * j : 256 * m + 128 * j + 128] = recv[kz, slot + j]
 
     def lanes_of(i, carry):
         lanes = pl.ds(pl.multiple_of(i * 256, 256), 256)
-        by_cos = dot(spec[...], cos[:, lanes])
-        by_sin = dot(spec[...], sin[:, lanes])
+        by_cos, by_sin = 0.0, 0.0
+        for m, chip in enumerate(chips):
+            rows = pl.ds(pl.multiple_of(chip * 256, 256), 256)
+            part = spec[:, 256 * m : 256 * m + 256]
+            by_cos = by_cos + dot(part, cos[rows, lanes])
+            by_sin = by_sin + dot(part, sin[rows, lanes])
         pot[0:XR, lanes] = (by_cos[:XR] - by_sin[XR:]).astype(BF)
         pot[XR:, lanes] = (by_cos[XR:] + by_sin[:XR]).astype(BF)
         return carry
@@ -298,6 +299,22 @@
                 acc[rows, lanes] = acc[rows, lanes] + taken[:, 128 * c : 128 * c + 128]
 
 
+def fold_cells(acc, spread, out, extra):
+    acc[512 : 512 + NB, :] = acc[512 : 512 + NB, :] + acc[0:NB, :]
+    acc[NB : 2 * NB, :] = acc[NB : 2 * NB, :] + acc[NB + 512 :, :]
+
+    def fold(i, carry):
+        rows = pl.ds(pl.multiple_of(i * 128, 128), 128)
+        wide_rows = pl.ds(pl.multiple_of(i * 128 + NB, NB), 128)
+        cells = dot_nt(acc[wide_rows, :], spread[...])
+        if extra is not None:
+            cells = cells + extra[rows, :].astype(F32)
+        out[rows, :] = cells.astype(BF)
+        return carry
+
+    lax.fori_loop(0, 4, fold, 0)
+
+
 def back_project(recv, near, tch, tcl, tsh, tsl, out, p_high, p_low, hots, box_real, box_imag, vals):
     real = jnp.concatenate([recv[NB * c : NB * c + NB, 0:32] for c in range(NCOL)], axis=1)
     imag = jnp.concatenate([recv[NB * c : NB * c + NB, 32:64] for c in range(NCOL)], axis=1)
@@ -408,6 +425,7 @@
     send_a, recv_a, send_b, recv_b, sem_send_a, sem_recv_a, sem_send_b, sem_recv_b,
     send_c, recv_c, send_d, recv_d, sem_send_c, sem_recv_c, sem_send_d, sem_recv_d,
     sem_send_h, sem_recv_h, sem_send_r, sem_recv_r,
+    far_c, far_starts, far_hot, far_a, recv_f, send_q, recv_q, sem_far,
 ):
     row, col = lax.axis_index("row"), lax.axis_index("col")
     mesh_ids = pl.DeviceIdType.MESH
@@ -429,8 +447,8 @@
 
     pairs = [
         (proj_hbm, proj), (tch_hbm, tch), (tcl_hbm, tcl), (tsh_hbm, tsh), (tsl_hbm, tsl),
-        (near_hbm, matrices), (spread_hbm, spread), (cos_hbm, cos), (sin_hbm, sin),
-        (green_hbm, green),
+        (green_hbm, green), (near_hbm, matrices), (spread_hbm, spread), (cos_hbm, cos),
+        (sin_hbm, sin),
     ]
     loads = [pltpu.make_async_copy(a, b, load_sem.at[i]) for i, (a, b) in enumerate(pairs)]
     for load in loads:
@@ -446,17 +464,13 @@
             device_id_type=mesh_ids,
         )
 
-    def row_copies(kz, source, target, sem_send, sem_recv):
-        return [
-            remote(
-                source.at[kz, row_peer(j)[0]],
-                target.at[kz, row],
-                sem_send.at[kz, j],
-                sem_recv.at[kz, j],
-                row_peer(j),
-            )
-            for j in range(1, NROW)
-        ]
+    z, core = row // 2, lax.rem(row, 2)
+    sibling = 2 * z + 1 - core
+    far, far_sibling = lax.rem(row + 4, NROW), lax.rem(sibling + 4, NROW)
+    chips = [lax.rem(z + 1, 4), lax.rem(z + 3, 4)]
+
+    def row_copy(kz, source, target, sems, j, peer):
+        return remote(source, target, sems[0].at[kz, j], sems[1].at[kz, j], (peer, col))
 
     def tile_rows(c):
         return pl.ds(pl.multiple_of(c * NB, NB), NB)
@@ -481,6 +495,8 @@
     for load in loads[:5]:
         load.wait()
     project(cur, proj, cells, tch, tcl, tsh, tsl, send_c, codes, p_high, p_low, hots, vals, boxed)
+    loads[5].wait()
+    turn_green(green, turned)
     pl.semaphore_wait(barrier, len(peers))
     third = col_copies(send_c, recv_c, sem_send_c, sem_recv_c)
     for copy in third:
@@ -493,7 +509,7 @@
     for copy in halo:
         copy.start()
     recv_c[tile_rows(col), :] = send_c[tile_rows(col), :]
-    loads[5].wait()
+    loads[6].wait()
     near_backward(beside, owned, picks, count, matrices, on_a, lv_one, lv_two, spread_back)
     back[4] = spread_back[4]
     returns = [
@@ -503,63 +519,94 @@
     ]
     for copy in returns:
         copy.start()
-    for load in loads[6:]:
+    for load in loads[7:]:
         load.wait()
     for copy in third:
         copy.wait_recv()
+    over = remote(recv_c, far_c, sem_far.at[0], sem_far.at[1], (far, col))
+    over.start()
     build_image(recv_c, spread, wide, starts, img)
-    first, second = [], []
+    sems_a, sems_b = (sem_send_a, sem_recv_a), (sem_send_b, sem_recv_b)
+    first, second, beyond = [[], []], [[], []], [[], []]
     for kz in range(2):
-        forward_y(kz, img, cos, sin, send_a)
-        first.append(row_copies(kz, send_a, recv_a, sem_send_a, sem_recv_a))
-        for copy in first[kz]:
-            copy.start()
+        for m in range(2):
+            forward_y(kz, chips[m], img, cos, sin, send_a, 2 * chips[m])
+            for j in range(2):
+                peer = 2 * chips[m] + lax.rem(core + j, 2)
+                copy = row_copy(
+                    kz, send_a.at[kz, peer], recv_a.at[kz, row], sems_a, 2 * m + j, peer
+                )
+                copy.start()
+                first[kz].append(copy)
+        forward_y(kz, z, img, cos, sin, send_a, 2 * z)
+        copy = row_copy(kz, send_a.at[kz, sibling], recv_a.at[kz, row], sems_a, 4, sibling)
+        copy.start()
+        first[kz].append(copy)
         recv_a[kz, row] = send_a[kz, row]
-    turn_green(green, turned)
-    for copy in halo:
-        copy.wait_recv()
-    near_onward(beside, owned, picks, count, matrices, on_a, on_b, lv_one, near)
+    over.wait_recv()
+    build_image(far_c, spread, wide, far_starts, img)
+    for kz in range(2):
+        forward_y(kz, z, img, cos, sin, far_a, 0)
+        copy = row_copy(kz, far_a.at[kz, 1 - core], recv_a.at[kz, far], sems_a, 5, sibling)
+        copy.start()
+        first[kz].append(copy)
+        recv_a[kz, far] = far_a[kz, core]
+    build_hot(recv_c, hot)
+    build_hot(far_c, far_hot)
+    acc[...] = jnp.zeros_like(acc)
     for kz in range(2):
         for copy in first[kz]:
             copy.wait_recv()
         along_x(kz, recv_a, turned, cos, sin, send_b, d_one, d_two, h_one, h_two)
-        second.append(row_copies(kz, send_b, recv_b, sem_send_b, sem_recv_b))
+        targets = [2 * chip + lax.rem(core + j, 2) for chip in chips for j in range(2)]
+        targets.append(sibling)
+        for j, peer in enumerate(targets):
+            copy = row_copy(kz, send_b.at[kz, peer], recv_b.at[kz, row], sems_b, j, peer)
+            copy.start()
+            second[kz].append(copy)
+        copy = row_copy(kz, send_b.at[kz, far_sibling], recv_f.at[kz, core], sems_b, 5, sibling)
+        copy.start()
+        beyond[kz].append(copy)
+        recv_b[kz, row] = send_b[kz, row]
+        recv_f[kz, core] = send_b[kz, far]
+    for kz in range(2):
+        beyond[kz][0].wait_recv()
+        inverse_y(kz, recv_f, [0], [z], cos, sin, spec, pot)
+        pick_cells(kz, pot, far_starts, far_hot, acc)
+    fold_cells(acc, spread, send_q, None)
+    home = remote(send_q, recv_q, sem_far.at[2], sem_far.at[3], (far, col))
+    home.start()
+    acc[...] = jnp.zeros_like(acc)
+    held = [z] + chips
+    for kz in range(2):
         for copy in second[kz]:
-            copy.start()
-        recv_b[kz, row] = send_b[kz, row]
-    build_hot(recv_c, hot)
-    acc[...] = jnp.zeros_like(acc)
+            copy.wait_recv()
+        inverse_y(kz, recv_b, [2 * chip for chip in held], held, cos, sin, spec, pot)
+        pick_cells(kz, pot, starts, hot, acc)
+    home.wait_recv()
+    fold_cells(acc, spread, send_d, recv_q)
+    fourth = col_copies(send_d, recv_d, sem_send_d, sem_recv_d)
+    for copy in fourth:
+        copy.start()
+    recv_d[tile_rows(col), :] = send_d[tile_rows(col), :]
+    for copy in halo:
+        copy.wait_recv()
+    near_onward(beside, owned, picks, count, matrices, on_a, on_b, lv_one, near)
     for copy in returns:
         copy.wait_recv()
     total = near[...]
     for n in range(9):
         total = total + back[n].astype(F32)
     near[...] = total
-    for kz in range(2):
-        for copy in second[kz]:
-            copy.wait_recv()
-        inverse_y(kz, recv_b, cos, sin, spec, pot)
-        pick_cells(kz, pot, starts, hot, acc)
-    acc[512 : 512 + NB, :] = acc[512 : 512 + NB, :] + acc[0:NB, :]
-    acc[NB : 2 * NB, :] = acc[NB : 2 * NB, :] + acc[NB + 512 :, :]
-
-    def fold(i, carry):
-        rows = pl.ds(pl.multiple_of(i * 128, 128), 128)
-        wide_rows = pl.ds(pl.multiple_of(i * 128 + NB, NB), 128)
-        send_d[rows, :] = dot_nt(acc[wide_rows, :], spread[...]).astype(BF)
-        return carry
-
-    lax.fori_loop(0, 4, fold, 0)
-    fourth = col_copies(send_d, recv_d, sem_send_d, sem_recv_d)
-    for copy in fourth:
-        copy.start()
-    recv_d[tile_rows(col), :] = send_d[tile_rows(col), :]
     for copy in fourth:
         copy.wait_recv()
     back_project(
         recv_d, near, tch, tcl, tsh, tsl, out, p_high, p_low, hots, box_real, box_imag, vals
     )
-    for copy in first[0] + first[1] + second[0] + second[1] + third + fourth + halo + returns:
+    for kz in range(2):
+        for copy in first[kz] + second[kz] + beyond[kz]:
+            copy.wait_send()
+    for copy in third + fourth + halo + returns + [over, home]:
         copy.wait_send()
 
 
@@ -602,6 +649,12 @@
         *[vmem((NCOL * NB, 128), BF)] * 4,
         *[dma((NCOL,))] * 4,
         *[dma((9,))] * 4,
+        vmem((NCOL * NB, 128), BF),
+        vmem((wrapped, 128), jnp.int32),
+        vmem((4, wrapped, XR), BF),
+        *[vmem((2, 2, 2 * XR, 128), BF)] * 2,
+        *[vmem((NCOL * NB, 128), BF)] * 2,
+        dma((4,)),
     ]
     in_vmem = pl.BlockSpec(memory_space=pltpu.VMEM)
     in_smem = pl.BlockSpec(memory_space=pltpu.SMEM)

time: 66.9 us -> 63.6 us (0.951)
  Pallas kernels: 64.6 us -> 61.4 us
    pallas_call x1, Pallas kernels: 64.6 us -> 61.4 us  [per_device(): pl.pallas_call(whole_kernel, out_shape=jax.ShapeDtypeStruct((2, NB * BLK)...]
where the time goes in v4:
time: 63.6 us; the launch traced here: 63.4 us
  Pallas kernels  61.4 us (97%)
  local copies, waits for them, and re-layouts  1.38 us (2%)
  between operations  0.66 us (1%)
    pallas_call x1, Pallas kernels, per_device(): pl.pallas_call(whole_kernel, out_shape=jax.ShapeDtypeStruct((2, NB * BLK)...  61.4 us
    unnamed x1, local copies, waits for them, and re-layouts  1.38 us

profile of v4, /device:TPU:1, one launch (start us, length us, event | category | flops | bytes accessed | tf_op | source)
XLA Modules:
  0.0 63.4 jit_solution(17562200327632940733)
XLA Ops:
  0.7 61.4 %shard_map.145 = f32[2,4096]{1,0:T(2,128)} custom-call(f32[2,4096]{1,0:T(2,128)} %cur.1, s32[32,128]{1,0:T(8,128)} %cells.1, s32[1,128]{1,0:T(1,128)} %owned.1, s32[1,128]{1,0:T(1,128)} %picks.1, s32[1]{0:T(128)S(6)} %copy.17.count, bf16[128,256,128]{2,1,0:T(8,128)(2,1)} %bitcast.1, f32[32,128,128]{2,1,0:T(8,128)} %proj_hbm.1, ...), custom_call_target="tpu_custom_call" | custom-call | tf_op jit(solution)/shard_map/pallas_call | solution.py:662
  62.0 1.4 %copy.18 = f32[2,4096]{1,0:T(2,128)} copy(f32[2,4096]{1,0:T(2,128)} %shard_map.145) | data formatting | bytes 65536

commit v5 on v4

--- a/solution.py
+++ b/solution.py
@@ -33,8 +33,8 @@
 
 
 def grid_tables():
-    index = np.arange(N)[:, None] * np.arange(N)[None, :] % N
-    angle = index * (2.0 * math.pi / N)
+    odd = 2 * np.arange(N) + 1
+    angle = (odd[:, None] * odd[None, :] % (4 * N)) * (math.pi / (2 * N))
     return bf(np.cos(angle)), bf(np.sin(angle))
 
 
@@ -47,12 +47,14 @@
     return cos_high, cos_low, sin_high, sin_low
 
 
-def spread_table():
+def spread_tables():
     lane = np.arange(128)[:, None]
     plane, ex, b = lane // 16, lane // 4 % 4, lane % 4
     wide = np.arange(2048)[None, :]
-    hits = (wide // 512 == ex) & (wide // 128 % 4 == plane) & ((wide + 2) % 4 == b) & (lane < 64)
-    return bf(hits.astype(np.float64))
+    hits = (wide // 512 == ex) & (wide // 128 % 4 == plane) & (lane < 64)
+    ahead = hits & ((wide + 2) % 4 == b)
+    backwards = hits & ((wide + 2) % 4 == 3 - b)
+    return bf(ahead.astype(np.float64)), bf(backwards.astype(np.float64))
 
 
 def dot(a, b):
@@ -92,7 +94,18 @@
     return jnp.where(iota((512, 128), 0) == code_row, 1.0, 0.0).astype(BF)
 
 
-def project(cur, proj, cells, tch, tcl, tsh, tsl, out, codes, p_high, p_low, hots, vals, boxed):
+def store_twist(corner_x, corner_y, row, col, twist):
+    lane = iota((NB, 128), 1)
+    x = (corner_x + ((lane >> 2) & 3) + 128 * row - 2) & (N - 1)
+    y = (corner_y + ((lane - corner_y) & 3) + 64 * col - 2) & (N - 1)
+    angle = (x + y).astype(F32) * (math.pi / N)
+    twist[0] = jnp.concatenate([jnp.cos(angle)] * 4, axis=1)
+    twist[1] = jnp.concatenate([jnp.sin(angle)] * 4, axis=1)
+
+
+def project(
+    cur, proj, cells, tch, tcl, tsh, tsl, out, codes, p_high, p_low, hots, vals, boxed, row, col, twist
+):
     code, corner_x, corner_y = cell_codes(cells[...])
     codes[...] = code
 
@@ -123,8 +136,11 @@
     b_high, b_low = high_low(boxed[...])
     along_cos = dot(b_high, tch[...]) + dot(b_low, tch[...]) + dot(b_high, tcl[...])
     along_sin = dot(b_high, tsh[...]) + dot(b_low, tsh[...]) + dot(b_high, tsl[...])
-    real = along_cos[:NB] + along_sin[NB:]
-    imag = along_cos[NB:] - along_sin[:NB]
+    store_twist(corner_x, corner_y, row, col, twist)
+    plain_real = along_cos[:NB] + along_sin[NB:]
+    plain_imag = along_cos[NB:] - along_sin[:NB]
+    real = plain_real * twist[0] - plain_imag * twist[1]
+    imag = plain_real * twist[1] + plain_imag * twist[0]
     lane = iota((NB, 64), 1)
     corners = jnp.where(lane == 0, corner_x, jnp.where(lane == 1, corner_y, 0)).astype(F32)
     for c in range(NCOL):
@@ -133,9 +149,15 @@
         out[NB * c : NB * c + NB, :] = message.astype(BF)
 
 
-def local_x_of_row(shape, dim):
+def local_x_of_row(shape, dim, band):
     row = iota(shape, dim)
-    return jnp.where(row < 130, row + 2, jnp.where(row >= 142, row - 142, -64))
+    tile = row - 128
+    main = jnp.where(band >= 4, 129 - row, row + 2)
+    upper = jnp.where(lax.rem(band + 1, NROW) >= 4, 137 - tile, 130 + tile)
+    upper = jnp.where((upper >= 130) & (upper < 132), upper, -64)
+    lower = jnp.where(lax.rem(band + NROW - 1, NROW) >= 4, 9 - tile, tile - 14)
+    lower = jnp.where((lower >= 0) & (lower < 2), lower, -64)
+    return jnp.where(row < 128, main, jnp.where(tile < 8, upper, lower))
 
 
 def store_starts(recv, starts):
@@ -147,44 +169,56 @@
 
 
 def chunk_mask(starts, q):
-    cell = 128 * q + iota((128, 128), 1)
+    lane = iota((128, 128), 1)
+    cell = 128 * q + lane if q < 4 else 128 * q + 127 - lane
     inside = ((cell - starts[64 * q : 64 * q + 128, :]) & (N - 1)) < 4
     return jnp.where(inside, 1.0, 0.0)
 
 
-def build_image(recv, spread, wide, starts, img):
-    def spread_rows(i, carry):
-        rows = pl.ds(pl.multiple_of(i * 128, 128), 128)
-        wide_rows = pl.ds(pl.multiple_of(i * 128 + NB, NB), 128)
-        wide[wide_rows, :] = dot(recv[rows, :], spread[...]).astype(BF)
-        return carry
-
-    lax.fori_loop(0, 4, spread_rows, 0)
-    wide[0:NB, :] = wide[512 : 512 + NB, :]
-    wide[NB + 512 :, :] = wide[NB : 2 * NB, :]
+def image_chunk(q, corner, local_x, wides, starts):
+    first = 64 * q if q < 4 else 64 * q - 256
+    wide = wides[0] if q < 4 else wides[1]
+    mask = chunk_mask(starts, q).astype(BF)
+    mask = jnp.concatenate([mask] * 4, axis=1)
+    offset = local_x - corner[0:1, 64 * q : 64 * q + 128].astype(jnp.int32)
+    lhs = [jnp.where(offset == ex, 1.0, 0.0).astype(BF) for ex in range(4)]
+    rhs = [wide[first : first + 128, 512 * ex : 512 * ex + 512] * mask for ex in range(4)]
+    return dot(jnp.concatenate(lhs, axis=1), jnp.concatenate(rhs, axis=0))
+
+
+def build_image(recv, band, spreads, padded, wides, starts, odd, even):
+    padded[0:NB, :] = recv[512 - NB :, :]
+    padded[NB : NB + 512, :] = recv[...]
+    padded[NB + 512 :, :] = recv[0:NB, :]
+
+    def spread_lanes(i, carry):
+        lanes = pl.ds(pl.multiple_of(i * 512, 512), 512)
+        wides[0][:, lanes] = dot(padded[0:320, :], spreads[0][:, lanes]).astype(BF)
+        wides[1][:, lanes] = dot(padded[256:576, :], spreads[1][:, lanes]).astype(BF)
+        return carry
+
+    lax.fori_loop(0, 4, spread_lanes, 0)
     store_starts(recv, starts)
     pick = jnp.where(iota((16, 128), 1) == 64, 1.0, 0.0).astype(BF)
     corner = dot_nt(pick, recv[...])[0:8]
     corner = jnp.concatenate([corner[:, 480:], corner, corner[:, :NB]], axis=1)
-    local_x = local_x_of_row((XR, 128), 0)
-    for q in range(8):
-        mask = chunk_mask(starts, q).astype(BF)
-        mask = jnp.concatenate([mask] * 4, axis=1)
-        corner_q = corner[0:1, 64 * q : 64 * q + 128].astype(jnp.int32)
-        offset = local_x - corner_q
-        lhs = [jnp.where(offset == ex, 1.0, 0.0).astype(BF) for ex in range(4)]
-        rhs = [wide[64 * q : 64 * q + 128, 512 * ex : 512 * ex + 512] * mask for ex in range(4)]
-        cells = dot(jnp.concatenate(lhs, axis=1), jnp.concatenate(rhs, axis=0)).astype(BF)
+    local_x = local_x_of_row((XR, 128), 0, band)
+    for q in range(4):
+        ahead = image_chunk(q, corner, local_x, wides, starts)
+        backwards = image_chunk(7 - q, corner, local_x, wides, starts)
+        minus, plus = (ahead - backwards).astype(BF), (ahead + backwards).astype(BF)
         for kz in range(2):
             for c in range(2):
                 p = 2 * c + kz
-                img[kz, XR * c : XR * c + XR, 128 * q : 128 * q + 128] = cells[:, 128 * p : 128 * p + 128]
-
-
-def forward_y(kz, chip, img, cos, sin, out, slot):
+                place = (kz, slice(XR * c, XR * c + XR), slice(128 * q, 128 * q + 128))
+                odd[place] = minus[:, 128 * p : 128 * p + 128]
+                even[place] = plus[:, 128 * p : 128 * p + 128]
+
+
+def forward_y(kz, chip, odd, even, cos, sin, out, slot):
     lanes = pl.ds(pl.multiple_of(chip * 256, 256), 256)
-    by_cos = dot(img[kz], cos[:, lanes])
-    by_sin = dot(img[kz], sin[:, lanes])
+    by_cos = dot(odd[kz], cos[0:512, lanes])
+    by_sin = dot(even[kz], sin[0:512, lanes])
     real = (by_cos[:XR] + by_sin[XR:]).astype(BF)
     imag = (by_cos[XR:] - by_sin[:XR]).astype(BF)
     for j in range(2):
@@ -193,66 +227,69 @@
 
 
 def along_x(kz, recv, green, cos, sin, out, d_one, d_two, h_one, h_two):
-    low_rows = iota((16, 128), 0) < 8
-
-    def gather_band(r, carry):
-        before, after = lax.rem(r + NROW - 1, NROW), lax.rem(r + 1, NROW)
-        rows = pl.ds(pl.multiple_of(r * 128, 128), 128)
+    none = jnp.zeros((8, 128), F32)
+    for r in range(NROW):
+        before, after = (r - 1) % NROW, (r + 1) % NROW
+        back = r >= 4
+        start = 512 + 128 * (7 - r) if back else 128 * r
+        rows = slice(start, start + 128)
         for c in range(2):
             base = XR * c
             main = recv[kz, r, base : base + 128, :]
-            lower = recv[kz, before, base + 128 : base + XR, :].astype(F32)
-            upper = recv[kz, after, base + 128 : base + XR, :].astype(F32)
-            head = main[0:16].astype(F32) + jnp.where(low_rows, lower, 0.0)
-            tail = main[112:128].astype(F32) + jnp.where(low_rows, 0.0, upper)
+            upper = recv[kz, before, base + 128 : base + XR, :].astype(F32)[0:8]
+            lower = recv[kz, after, base + 128 : base + XR, :].astype(F32)[8:16]
+            head, tail = (lower, upper) if back else (upper, lower)
+            head = main[0:16].astype(F32) + jnp.concatenate([head, none], axis=0)
+            tail = main[112:128].astype(F32) + jnp.concatenate([none, tail], axis=0)
             band = jnp.concatenate([head.astype(BF), main[16:112], tail.astype(BF)], axis=0)
-            d_one[rows, 128 * c : 128 * c + 128] = band
-            if c == 0:
-                d_two[rows, 128:256] = -band
-            else:
-                d_two[rows, 0:128] = band
-        return carry
-
-    lax.fori_loop(0, NROW, gather_band, 0)
+            d_one[rows, 128 * c : 128 * c + 128] = -band if back else band
+            d_two[rows, 128 - 128 * c : 256 - 128 * c] = -band if c == 0 else band
 
     def forward(i, carry):
         rows = pl.ds(pl.multiple_of(i * 256, 256), 256)
-        spec = dot(cos[rows, :], d_one[...]) + dot(sin[rows, :], d_two[...])
-        real, imag = spec[:, :128], spec[:, 128:]
+        high_rows = pl.ds(pl.multiple_of(i * 256 + 512, 256), 256)
+        cos_i, sin_i = cos[rows, 0:512], sin[rows, 0:512]
+        by_cos = dot(cos_i, d_one[0:512, :]) + dot(cos_i, d_one[512:, :])
+        by_sin = dot(sin_i, d_two[0:512, :]) + dot(sin_i, d_two[512:, :])
         lanes = slice(128 * kz, 128 * kz + 128)
-        g_real, g_imag = green[0, rows, lanes], green[1, rows, lanes]
-        h_real = (real * g_real - imag * g_imag).astype(BF)
-        h_imag = (real * g_imag + imag * g_real).astype(BF)
-        h_one[rows, 0:128] = h_real
-        h_one[rows, 128:256] = h_imag
-        h_two[rows, 0:128] = -h_imag
-        h_two[rows, 128:256] = h_real
-        return carry
-
-    lax.fori_loop(0, 4, forward, 0)
+        parts = []
+        for spec, where in ((by_sin + by_cos, rows), (by_sin - by_cos, high_rows)):
+            real, imag = spec[:, :128], spec[:, 128:]
+            g_real, g_imag = green[0, where, lanes], green[1, where, lanes]
+            parts.append((real * g_real - imag * g_imag, real * g_imag + imag * g_real))
+        (low_real, low_imag), (high_real, high_imag) = parts
+        h_one[rows, 0:128] = (low_real - high_real).astype(BF)
+        h_one[rows, 128:256] = (low_imag - high_imag).astype(BF)
+        h_two[rows, 0:128] = -(low_imag + high_imag).astype(BF)
+        h_two[rows, 128:256] = (low_real + high_real).astype(BF)
+        return carry
+
+    lax.fori_loop(0, 2, forward, 0)
 
     def inverse(i, carry):
         rows = pl.ds(pl.multiple_of(i * 256, 256), 256)
-        back = (dot(cos[rows, :], h_one[...]) + dot(sin[rows, :], h_two[...])).astype(BF)
+        by_cos = dot(cos[rows, 0:512], h_one[...])
+        by_sin = dot(sin[rows, 0:512], h_two[...])
+        low, high = (by_sin + by_cos).astype(BF), (by_sin - by_cos).astype(BF)
         for j in range(2):
             for c in range(2):
-                out[kz, 2 * i + j, XR * c : XR * c + 128, :] = back[
-                    128 * j : 128 * j + 128, 128 * c : 128 * c + 128
-                ]
-        return carry
-
-    lax.fori_loop(0, 4, inverse, 0)
-
-    def rims(r, carry):
-        before, after = lax.rem(r + NROW - 1, NROW), lax.rem(r + 1, NROW)
+                place = (slice(128 * j, 128 * j + 128), slice(128 * c, 128 * c + 128))
+                out[kz, 2 * i + j, XR * c : XR * c + 128, :] = low[place]
+                out[kz, 7 - 2 * i - j, XR * c : XR * c + 128, :] = high[place]
+        return carry
+
+    lax.fori_loop(0, 2, inverse, 0)
+    for r in range(NROW):
+        before, after = (r - 1) % NROW, (r + 1) % NROW
         for c in range(2):
             base = XR * c
-            above = out[kz, after, base : base + 16, :].astype(F32)
-            below = out[kz, before, base + 112 : base + 128, :].astype(F32)
-            out[kz, r, base + 128 : base + XR, :] = jnp.where(low_rows, above, below).astype(BF)
-        return carry
-
-    lax.fori_loop(0, NROW, rims, 0)
+            above = out[kz, after, base : base + 16, :].astype(F32)[0:8]
+            if after >= 4:
+                above = out[kz, after, base + 112 : base + 128, :].astype(F32)[8:16]
+            below = out[kz, before, base + 112 : base + 128, :].astype(F32)[8:16]
+            if before >= 4:
+                below = out[kz, before, base : base + 16, :].astype(F32)[0:8]
+            out[kz, r, base + 128 : base + XR, :] = jnp.concatenate([above, below], axis=0).astype(BF)
 
 
 def inverse_y(kz, recv, slots, chips, cos, sin, spec, pot):
@@ -268,15 +305,18 @@
             part = spec[:, 256 * m : 256 * m + 256]
             by_cos = by_cos + dot(part, cos[rows, lanes])
             by_sin = by_sin + dot(part, sin[rows, lanes])
+        high_lanes = pl.ds(pl.multiple_of(i * 256 + 512, 256), 256)
         pot[0:XR, lanes] = (by_cos[:XR] - by_sin[XR:]).astype(BF)
         pot[XR:, lanes] = (by_cos[XR:] + by_sin[:XR]).astype(BF)
-        return carry
-
-    lax.fori_loop(0, 4, lanes_of, 0)
-
-
-def build_hot(recv, hot):
-    local_x = local_x_of_row((512, XR), 1)
+        pot[0:XR, high_lanes] = -(by_cos[:XR] + by_sin[XR:]).astype(BF)
+        pot[XR:, high_lanes] = (by_sin[:XR] - by_cos[XR:]).astype(BF)
+        return carry
+
+    lax.fori_loop(0, 2, lanes_of, 0)
+
+
+def build_hot(recv, band, hot):
+    local_x = local_x_of_row((512, XR), 1, band)
     offset = local_x - recv[:, 64:65].astype(jnp.int32)
     for ex in range(4):
         hot[ex, NB : NB + 512, :] = jnp.where(offset == ex, 1.0, 0.0).astype(BF)
@@ -284,43 +324,50 @@
     hot[:, NB + 512 :, :] = hot[:, NB : 2 * NB, :]
 
 
-def pick_cells(kz, pot, starts, hot, acc):
+def pick_cells(kz, pot, starts, hot, accs):
     for q in range(8):
         mask = chunk_mask(starts, q)
         mask = jnp.concatenate([mask] * 2, axis=1)
-        cells = [pot[XR * c : XR * c + XR, 128 * q : 128 * q + 128] for c in range(2)]
+        lane = 128 * q if q < 4 else 512 + 128 * (7 - q)
+        cells = [pot[XR * c : XR * c + XR, lane : lane + 128] for c in range(2)]
         cells = jnp.concatenate(cells, axis=1)
-        rows = slice(64 * q, 64 * q + 128)
+        first = 64 * q if q < 4 else 64 * q - 256
+        rows = slice(first, first + 128)
+        acc = accs[0] if q < 4 else accs[1]
         for ex in range(4):
-            taken = (dot(hot[ex, rows, :], cells) * mask).astype(BF)
+            taken = (dot(hot[ex, 64 * q : 64 * q + 128, :], cells) * mask).astype(BF)
             for c in range(2):
                 lane = 512 * ex + 256 * c + 128 * kz
                 lanes = slice(lane, lane + 128)
                 acc[rows, lanes] = acc[rows, lanes] + taken[:, 128 * c : 128 * c + 128]
 
 
-def fold_cells(acc, spread, out, extra):
-    acc[512 : 512 + NB, :] = acc[512 : 512 + NB, :] + acc[0:NB, :]
-    acc[NB : 2 * NB, :] = acc[NB : 2 * NB, :] + acc[NB + 512 :, :]
-
-    def fold(i, carry):
-        rows = pl.ds(pl.multiple_of(i * 128, 128), 128)
-        wide_rows = pl.ds(pl.multiple_of(i * 128 + NB, NB), 128)
-        cells = dot_nt(acc[wide_rows, :], spread[...])
-        if extra is not None:
-            cells = cells + extra[rows, :].astype(F32)
-        out[rows, :] = cells.astype(BF)
-        return carry
-
-    lax.fori_loop(0, 4, fold, 0)
-
-
-def back_project(recv, near, tch, tcl, tsh, tsl, out, p_high, p_low, hots, box_real, box_imag, vals):
+def clear_cells(accs):
+    for acc in accs:
+        acc[...] = jnp.zeros_like(acc)
+
+
+def fold_cells(accs, spreads, out, extra):
+    a = dot_nt(accs[0][...], spreads[0][...])
+    b = dot_nt(accs[1][...], spreads[1][...])
+    pieces = [a[32:64] + b[288:320], a[64:256], a[256:320] + b[0:64], b[64:256], b[256:288] + a[0:32]]
+    cells = jnp.concatenate(pieces, axis=0)
+    if extra is not None:
+        cells = cells + extra[...].astype(F32)
+    out[...] = cells.astype(BF)
+
+
+def back_project(
+    recv, near, tch, tcl, tsh, tsl, out, p_high, p_low, hots, box_real, box_imag, vals, twist
+):
     real = jnp.concatenate([recv[NB * c : NB * c + NB, 0:32] for c in range(NCOL)], axis=1)
     imag = jnp.concatenate([recv[NB * c : NB * c + NB, 32:64] for c in range(NCOL)], axis=1)
-    both = jnp.concatenate([real, imag], axis=0)
-    along_cos = dot(both, tch[...]) + dot(both, tcl[...])
-    along_sin = dot(both, tsh[...]) + dot(both, tsl[...])
+    real, imag = real.astype(F32), imag.astype(F32)
+    turned_real = real * twist[0] + imag * twist[1]
+    turned_imag = imag * twist[0] - real * twist[1]
+    b_high, b_low = high_low(jnp.concatenate([turned_real, turned_imag], axis=0))
+    along_cos = dot(b_high, tch[...]) + dot(b_low, tch[...]) + dot(b_high, tcl[...])
+    along_sin = dot(b_high, tsh[...]) + dot(b_low, tsh[...]) + dot(b_high, tsl[...])
     box_real[...] = along_cos[:NB] - along_sin[NB:]
     box_imag[...] = along_cos[NB:] + along_sin[:NB]
 
@@ -403,25 +450,31 @@
 
 
 def turn_green(green, turned):
+    turn = jnp.where(iota((128, 128), 0) + iota((128, 128), 1) == 127, 1.0, 0.0).astype(BF)
     for c in range(2):
         for kz in range(2):
 
             def part(i, carry):
                 rows = pl.ds(pl.multiple_of(i * 128, 128), 128)
-                block = jnp.transpose(green[c, kz, :, rows])
-                turned[c, rows, 128 * kz : 128 * kz + 128] = block * (1.0 / (N * N * NGZ))
+                high_rows = pl.ds(pl.multiple_of(896 - i * 128, 128), 128)
+                target = pl.ds(pl.multiple_of(i * 128 + 512, 128), 128)
+                lanes = slice(128 * kz, 128 * kz + 128)
+                scale = 1.0 / (N * N * NGZ)
+                turned[c, rows, lanes] = jnp.transpose(green[c, kz, :, rows]) * scale
+                high, low = high_low(green[c, kz, :, high_rows] * scale)
+                turned[c, target, lanes] = dot_nt(turn, high) + dot_nt(turn, low)
                 return carry
 
-            lax.fori_loop(0, 8, part, 0)
+            lax.fori_loop(0, 4, part, 0)
 
 
 def whole_kernel(
     cur, cells, owned, picks, count, near_hbm, proj_hbm, green_hbm,
-    tch_hbm, tcl_hbm, tsh_hbm, tsl_hbm, spread_hbm, cos_hbm, sin_hbm, out,
-    matrices, proj, green, tch, tcl, tsh, tsl, spread, cos, sin, load_sem,
+    tch_hbm, tcl_hbm, tsh_hbm, tsl_hbm, ahead_hbm, backwards_hbm, cos_hbm, sin_hbm, out,
+    matrices, proj, green, tch, tcl, tsh, tsl, ahead, backwards, cos, sin, load_sem, twist,
     codes, p_high, p_low, hots, vals, boxed, box_real, box_imag,
     beside, spread_back, back, on_a, on_b, lv_one, lv_two, near, turned,
-    wide, starts, img, hot, acc, spec, pot, d_one, d_two, h_one, h_two,
+    padded, wide_a, wide_b, starts, odd, even, hot, acc_a, acc_b, spec, pot, d_one, d_two, h_one, h_two,
     send_a, recv_a, send_b, recv_b, sem_send_a, sem_recv_a, sem_send_b, sem_recv_b,
     send_c, recv_c, send_d, recv_d, sem_send_c, sem_recv_c, sem_send_d, sem_recv_d,
     sem_send_h, sem_recv_h, sem_send_r, sem_recv_r,
@@ -447,8 +500,8 @@
 
     pairs = [
         (proj_hbm, proj), (tch_hbm, tch), (tcl_hbm, tcl), (tsh_hbm, tsh), (tsl_hbm, tsl),
-        (green_hbm, green), (near_hbm, matrices), (spread_hbm, spread), (cos_hbm, cos),
-        (sin_hbm, sin),
+        (near_hbm, matrices), (ahead_hbm, ahead), (backwards_hbm, backwards), (cos_hbm, cos),
+        (sin_hbm, sin), (green_hbm, green),
     ]
     loads = [pltpu.make_async_copy(a, b, load_sem.at[i]) for i, (a, b) in enumerate(pairs)]
     for load in loads:
@@ -494,9 +547,11 @@
     beside[4] = rounded
     for load in loads[:5]:
         load.wait()
-    project(cur, proj, cells, tch, tcl, tsh, tsl, send_c, codes, p_high, p_low, hots, vals, boxed)
-    loads[5].wait()
-    turn_green(green, turned)
+    spreads, wides, accs = (ahead, backwards), (wide_a, wide_b), (acc_a, acc_b)
+    project(
+        cur, proj, cells, tch, tcl, tsh, tsl, send_c, codes, p_high, p_low, hots, vals, boxed,
+        row, col, twist,
+    )
     pl.semaphore_wait(barrier, len(peers))
     third = col_copies(send_c, recv_c, sem_send_c, sem_recv_c)
     for copy in third:
@@ -509,7 +564,7 @@
     for copy in halo:
         copy.start()
     recv_c[tile_rows(col), :] = send_c[tile_rows(col), :]
-    loads[6].wait()
+    loads[5].wait()
     near_backward(beside, owned, picks, count, matrices, on_a, lv_one, lv_two, spread_back)
     back[4] = spread_back[4]
     returns = [
@@ -519,18 +574,18 @@
     ]
     for copy in returns:
         copy.start()
-    for load in loads[7:]:
+    for load in loads[6:]:
         load.wait()
     for copy in third:
         copy.wait_recv()
     over = remote(recv_c, far_c, sem_far.at[0], sem_far.at[1], (far, col))
     over.start()
-    build_image(recv_c, spread, wide, starts, img)
+    build_image(recv_c, row, spreads, padded, wides, starts, odd, even)
     sems_a, sems_b = (sem_send_a, sem_recv_a), (sem_send_b, sem_recv_b)
     first, second, beyond = [[], []], [[], []], [[], []]
     for kz in range(2):
         for m in range(2):
-            forward_y(kz, chips[m], img, cos, sin, send_a, 2 * chips[m])
+            forward_y(kz, chips[m], odd, even, cos, sin, send_a, 2 * chips[m])
             for j in range(2):
                 peer = 2 * chips[m] + lax.rem(core + j, 2)
                 copy = row_copy(
@@ -538,22 +593,23 @@
                 )
                 copy.start()
                 first[kz].append(copy)
-        forward_y(kz, z, img, cos, sin, send_a, 2 * z)
+        forward_y(kz, z, odd, even, cos, sin, send_a, 2 * z)
         copy = row_copy(kz, send_a.at[kz, sibling], recv_a.at[kz, row], sems_a, 4, sibling)
         copy.start()
         first[kz].append(copy)
         recv_a[kz, row] = send_a[kz, row]
     over.wait_recv()
-    build_image(far_c, spread, wide, far_starts, img)
+    build_image(far_c, far, spreads, padded, wides, far_starts, odd, even)
     for kz in range(2):
-        forward_y(kz, z, img, cos, sin, far_a, 0)
+        forward_y(kz, z, odd, even, cos, sin, far_a, 0)
         copy = row_copy(kz, far_a.at[kz, 1 - core], recv_a.at[kz, far], sems_a, 5, sibling)
         copy.start()
         first[kz].append(copy)
         recv_a[kz, far] = far_a[kz, core]
-    build_hot(recv_c, hot)
-    build_hot(far_c, far_hot)
-    acc[...] = jnp.zeros_like(acc)
+    turn_green(green, turned)
+    build_hot(recv_c, row, hot)
+    build_hot(far_c, far, far_hot)
+    clear_cells(accs)
     for kz in range(2):
         for copy in first[kz]:
             copy.wait_recv()
@@ -572,19 +628,19 @@
     for kz in range(2):
         beyond[kz][0].wait_recv()
         inverse_y(kz, recv_f, [0], [z], cos, sin, spec, pot)
-        pick_cells(kz, pot, far_starts, far_hot, acc)
-    fold_cells(acc, spread, send_q, None)
+        pick_cells(kz, pot, far_starts, far_hot, accs)
+    fold_cells(accs, spreads, send_q, None)
     home = remote(send_q, recv_q, sem_far.at[2], sem_far.at[3], (far, col))
     home.start()
-    acc[...] = jnp.zeros_like(acc)
+    clear_cells(accs)
     held = [z] + chips
     for kz in range(2):
         for copy in second[kz]:
             copy.wait_recv()
         inverse_y(kz, recv_b, [2 * chip for chip in held], held, cos, sin, spec, pot)
-        pick_cells(kz, pot, starts, hot, acc)
+        pick_cells(kz, pot, starts, hot, accs)
     home.wait_recv()
-    fold_cells(acc, spread, send_d, recv_q)
+    fold_cells(accs, spreads, send_d, recv_q)
     fourth = col_copies(send_d, recv_d, sem_send_d, sem_recv_d)
     for copy in fourth:
         copy.start()
@@ -601,7 +657,7 @@
     for copy in fourth:
         copy.wait_recv()
     back_project(
-        recv_d, near, tch, tcl, tsh, tsl, out, p_high, p_low, hots, box_real, box_imag, vals
+        recv_d, near, tch, tcl, tsh, tsl, out, p_high, p_low, hots, box_real, box_imag, vals, twist
     )
     for kz in range(2):
         for copy in first[kz] + second[kz] + beyond[kz]:
@@ -614,7 +670,7 @@
     currents, near_blocks, pair_local, pair_ghost, pair_counts, projection, stencil_cells, green
 ):
     tables = [jnp.asarray(t) for t in depth_tables()]
-    tables.append(jnp.asarray(spread_table()))
+    tables += [jnp.asarray(t) for t in spread_tables()]
     tables += [jnp.asarray(t) for t in grid_tables()]
     vmem, dma = pltpu.VMEM, pltpu.SemaphoreType.DMA
     grid_part = (2, NROW, 2 * XR, 128)
@@ -624,9 +680,10 @@
         vmem((NB, BLK, BLK), F32),
         vmem((2, 2, 128, N), F32),
         *[vmem((512, 512), BF)] * 4,
-        vmem((128, 2048), BF),
+        *[vmem((128, 2048), BF)] * 2,
         *[vmem((N, N), BF)] * 2,
-        dma((10,)),
+        dma((11,)),
+        vmem((2, NB, 512), F32),
         vmem((NB, BLK), jnp.int32),
         *[vmem((NB, BLK, BLK), BF)] * 2,
         vmem((NB, 512, BLK), BF),
@@ -637,13 +694,15 @@
         *[vmem((PAIRS, 2 * BLK), F32)] * 4,
         vmem((NB, 2 * BLK), F32),
         vmem((2, N, 256), F32),
-        vmem((wrapped, 2048), BF),
+        vmem((wrapped, 128), BF),
+        *[vmem((320, 2048), BF)] * 2,
         vmem((wrapped, 128), jnp.int32),
-        vmem((2, 2 * XR, N), BF),
+        *[vmem((2, 2 * XR, 512), BF)] * 2,
         vmem((4, wrapped, XR), BF),
-        vmem((wrapped, 2048), BF),
+        *[vmem((320, 2048), BF)] * 2,
         *[vmem((2 * XR, N), BF)] * 2,
-        *[vmem((N, 256), BF)] * 4,
+        *[vmem((N, 256), BF)] * 2,
+        *[vmem((512, 256), BF)] * 2,
         *[vmem(grid_part, BF)] * 4,
         *[dma((2, NROW))] * 4,
         *[vmem((NCOL * NB, 128), BF)] * 4,
@@ -662,7 +721,7 @@
     return pl.pallas_call(
         whole_kernel,
         out_shape=jax.ShapeDtypeStruct((2, NB * BLK), F32),
-        in_specs=[in_vmem] * 4 + [in_smem] + [anywhere] * 10,
+        in_specs=[in_vmem] * 4 + [in_smem] + [anywhere] * 11,
         out_specs=in_vmem,
         scratch_shapes=scratch,
         compiler_params=pltpu.CompilerParams(

time: 63.6 us -> 57 us (0.90)
  Pallas kernels: 61.4 us -> 54.7 us
    pallas_call x1, Pallas kernels: 61.4 us -> 54.7 us  [per_device(): pl.pallas_call(whole_kernel, out_shape=jax.ShapeDtypeStruct((2, NB * BLK)...]
where the time goes in v5:
time: 57 us; the launch traced here: 56.7 us
  Pallas kernels  54.7 us (96%)
  local copies, waits for them, and re-layouts  1.38 us (2%)
  between operations  0.66 us (1%)
    pallas_call x1, Pallas kernels, per_device(): pl.pallas_call(whole_kernel, out_shape=jax.ShapeDtypeStruct((2, NB * BLK)...  54.7 us
    unnamed x1, local copies, waits for them, and re-layouts  1.38 us

profile of v5, /device:TPU:1, one launch (start us, length us, event | category | flops | bytes accessed | tf_op | source)
XLA Modules:
  0.0 56.7 jit_solution(1032671660949968056)
XLA Ops:
  0.7 54.7 %shard_map.154 = f32[2,4096]{1,0:T(2,128)} custom-call(f32[2,4096]{1,0:T(2,128)} %cur.1, s32[32,128]{1,0:T(8,128)} %cells.1, s32[1,128]{1,0:T(1,128)} %owned.1, s32[1,128]{1,0:T(1,128)} %picks.1, s32[1]{0:T(128)S(6)} %copy.18.count, bf16[128,256,128]{2,1,0:T(8,128)(2,1)} %bitcast.1, f32[32,128,128]{2,1,0:T(8,128)} %proj_hbm.1, ...), custom_call_target="tpu_custom_call" | custom-call | tf_op jit(solution)/shard_map/pallas_call | solution.py:721
  55.3 1.4 %copy.19 = f32[2,4096]{1,0:T(2,128)} copy(f32[2,4096]{1,0:T(2,128)} %shard_map.154) | data formatting | bytes 65536

commit v6 on v5

--- a/solution.py
+++ b/solution.py
@@ -401,7 +401,7 @@
 
 def near_backward(beside, owned, picks, count, matrices, back_a, lv_one, lv_two, spread_back):
     hits = jnp.where(iota((PAIRS, NB), 1) == column_of(owned[...]), 1.0, 0.0).astype(BF)
-    local = dot(hits, beside[4])
+    local = dot(hits, beside[1, NB : 2 * NB, :])
     real, imag = local[:, :BLK], local[:, BLK:]
     lv_one[...] = jnp.concatenate([real, -imag], axis=1)
     lv_two[...] = jnp.concatenate([imag, real], axis=1)
@@ -422,12 +422,14 @@
     high, low = high_low(back_a[...])
     total = (dot(table, high) + dot(table, low)).astype(BF)
     for n in range(9):
-        spread_back[n] = total[NB * n : NB * n + NB, :]
+        rows = slice(NB * (n // 3), NB * (n // 3) + NB)
+        spread_back[n % 3, rows, :] = total[NB * n : NB * n + NB, :]
 
 
 def near_onward(beside, owned, picks, count, matrices, on_a, on_b, lv_one, near):
     hits = jnp.where(iota((PAIRS, 9 * NB), 1) == column_of(picks[...]), 1.0, 0.0).astype(BF)
-    lv_one[...] = dot(hits, jnp.concatenate([beside[n] for n in range(9)], axis=0))
+    tiles = [beside[n % 3, NB * (n // 3) : NB * (n // 3) + NB, :] for n in range(9)]
+    lv_one[...] = dot(hits, jnp.concatenate(tiles, axis=0))
     first_row = iota((8, BLK), 0) == 0
 
     def pairs_of(i, carry):
@@ -449,23 +451,22 @@
     near[...] = dot(table, high) + dot(table, low)
 
 
-def turn_green(green, turned):
+def turn_green(kz, green, turned):
     turn = jnp.where(iota((128, 128), 0) + iota((128, 128), 1) == 127, 1.0, 0.0).astype(BF)
     for c in range(2):
-        for kz in range(2):
-
-            def part(i, carry):
-                rows = pl.ds(pl.multiple_of(i * 128, 128), 128)
-                high_rows = pl.ds(pl.multiple_of(896 - i * 128, 128), 128)
-                target = pl.ds(pl.multiple_of(i * 128 + 512, 128), 128)
-                lanes = slice(128 * kz, 128 * kz + 128)
-                scale = 1.0 / (N * N * NGZ)
-                turned[c, rows, lanes] = jnp.transpose(green[c, kz, :, rows]) * scale
-                high, low = high_low(green[c, kz, :, high_rows] * scale)
-                turned[c, target, lanes] = dot_nt(turn, high) + dot_nt(turn, low)
-                return carry
-
-            lax.fori_loop(0, 4, part, 0)
+
+        def part(i, carry):
+            rows = pl.ds(pl.multiple_of(i * 128, 128), 128)
+            high_rows = pl.ds(pl.multiple_of(896 - i * 128, 128), 128)
+            target = pl.ds(pl.multiple_of(i * 128 + 512, 128), 128)
+            lanes = slice(128 * kz, 128 * kz + 128)
+            scale = 1.0 / (N * N * NGZ)
+            turned[c, rows, lanes] = jnp.transpose(green[c, kz, :, rows]) * scale
+            high, low = high_low(green[c, kz, :, high_rows] * scale)
+            turned[c, target, lanes] = dot_nt(turn, high) + dot_nt(turn, low)
+            return carry
+
+        lax.fori_loop(0, 4, part, 0)
 
 
 def whole_kernel(
@@ -473,7 +474,7 @@
     tch_hbm, tcl_hbm, tsh_hbm, tsl_hbm, ahead_hbm, backwards_hbm, cos_hbm, sin_hbm, out,
     matrices, proj, green, tch, tcl, tsh, tsl, ahead, backwards, cos, sin, load_sem, twist,
     codes, p_high, p_low, hots, vals, boxed, box_real, box_imag,
-    beside, spread_back, back, on_a, on_b, lv_one, lv_two, near, turned,
+    beside, spread_back, back, kept, edges, edges_in, on_a, on_b, lv_one, lv_two, near, turned,
     padded, wide_a, wide_b, starts, odd, even, hot, acc_a, acc_b, spec, pot, d_one, d_two, h_one, h_two,
     send_a, recv_a, send_b, recv_b, sem_send_a, sem_recv_a, sem_send_b, sem_recv_b,
     send_c, recv_c, send_d, recv_d, sem_send_c, sem_recv_c, sem_send_d, sem_recv_d,
@@ -489,12 +490,13 @@
     def col_peer(j):
         return (row, lax.rem(col + j, NCOL))
 
-    def tile_peer(n):
-        return (lax.rem(row + n // 3 - 1 + NROW, NROW), lax.rem(col + n % 3 - 1 + NCOL, NCOL))
+    def beside_peer(dim, step):
+        if dim == 0:
+            return (lax.rem(row + step + NROW, NROW), col)
+        return (row, lax.rem(col + step + NCOL, NCOL))
 
     barrier = pltpu.get_barrier_semaphore()
     peers = [row_peer(j) for j in range(1, NROW)] + [col_peer(j) for j in range(1, NCOL)]
-    peers += [tile_peer(n) for n in (0, 2, 6, 8)]
     for peer in peers:
         pl.semaphore_signal(barrier, inc=1, device_id=peer, device_id_type=mesh_ids)
 
@@ -504,7 +506,7 @@
         (sin_hbm, sin), (green_hbm, green),
     ]
     loads = [pltpu.make_async_copy(a, b, load_sem.at[i]) for i, (a, b) in enumerate(pairs)]
-    for load in loads:
+    for load in loads[:5]:
         load.start()
 
     def remote(source, target, sem_send, sem_recv, peer):
@@ -544,9 +546,11 @@
         two = cur[:, BLK * g : BLK * g + BLK]
         vals[g] = two
     rounded = jnp.concatenate([vals[:, 0, :], vals[:, 1, :]], axis=1).astype(BF)
-    beside[4] = rounded
+    beside[1, NB : 2 * NB, :] = rounded
     for load in loads[:5]:
         load.wait()
+    for load in loads[5:]:
+        load.start()
     spreads, wides, accs = (ahead, backwards), (wide_a, wide_b), (acc_a, acc_b)
     project(
         cur, proj, cells, tch, tcl, tsh, tsl, send_c, codes, p_high, p_low, hots, vals, boxed,
@@ -556,23 +560,39 @@
     third = col_copies(send_c, recv_c, sem_send_c, sem_recv_c)
     for copy in third:
         copy.start()
+    middle = pl.ds(NB, NB)
     halo = [
-        remote(beside.at[4], beside.at[8 - n], sem_send_h.at[n], sem_recv_h.at[n], tile_peer(n))
-        for n in range(9)
-        if n != 4
+        remote(
+            beside.at[1, middle],
+            beside.at[1, pl.ds(NB * place, NB)],
+            sem_send_h.at[place],
+            sem_recv_h.at[place],
+            beside_peer(0, step),
+        )
+        for step, place in ((1, 0), (-1, 2))
     ]
     for copy in halo:
         copy.start()
     recv_c[tile_rows(col), :] = send_c[tile_rows(col), :]
     loads[5].wait()
     near_backward(beside, owned, picks, count, matrices, on_a, lv_one, lv_two, spread_back)
-    back[4] = spread_back[4]
+    for copy in halo:
+        copy.wait_recv()
+    wide_halo = [
+        remote(
+            beside.at[1], beside.at[place], sem_send_h.at[3 + place], sem_recv_h.at[3 + place],
+            beside_peer(1, step),
+        )
+        for step, place in ((1, 0), (-1, 2))
+    ]
     returns = [
-        remote(spread_back.at[n], back.at[8 - n], sem_send_r.at[n], sem_recv_r.at[n], tile_peer(n))
-        for n in range(9)
-        if n != 4
+        remote(
+            spread_back.at[place], back.at[place], sem_send_r.at[place], sem_recv_r.at[place],
+            beside_peer(1, step),
+        )
+        for step, place in ((-1, 0), (1, 2))
     ]
-    for copy in returns:
+    for copy in returns + wide_halo:
         copy.start()
     for load in loads[6:]:
         load.wait()
@@ -593,6 +613,7 @@
                 )
                 copy.start()
                 first[kz].append(copy)
+    for kz in range(2):
         forward_y(kz, z, odd, even, cos, sin, send_a, 2 * z)
         copy = row_copy(kz, send_a.at[kz, sibling], recv_a.at[kz, row], sems_a, 4, sibling)
         copy.start()
@@ -606,11 +627,26 @@
         copy.start()
         first[kz].append(copy)
         recv_a[kz, far] = far_a[kz, core]
-    turn_green(green, turned)
+    for copy in returns:
+        copy.wait_recv()
+    column = spread_back[1].astype(F32) + back[0].astype(F32) + back[2].astype(F32)
+    kept[...] = column[NB : 2 * NB]
+    edges[0] = column[:NB].astype(BF)
+    edges[1] = column[2 * NB :].astype(BF)
+    edge_copies = [
+        remote(
+            edges.at[place], edges_in.at[place], sem_send_r.at[3 + place], sem_recv_r.at[3 + place],
+            beside_peer(0, step),
+        )
+        for step, place in ((-1, 0), (1, 1))
+    ]
+    for copy in edge_copies:
+        copy.start()
     build_hot(recv_c, row, hot)
     build_hot(far_c, far, far_hot)
     clear_cells(accs)
     for kz in range(2):
+        turn_green(kz, green, turned)
         for copy in first[kz]:
             copy.wait_recv()
         along_x(kz, recv_a, turned, cos, sin, send_b, d_one, d_two, h_one, h_two)
@@ -645,15 +681,13 @@
     for copy in fourth:
         copy.start()
     recv_d[tile_rows(col), :] = send_d[tile_rows(col), :]
-    for copy in halo:
+    for copy in wide_halo:
         copy.wait_recv()
     near_onward(beside, owned, picks, count, matrices, on_a, on_b, lv_one, near)
-    for copy in returns:
+    for copy in edge_copies:
         copy.wait_recv()
-    total = near[...]
-    for n in range(9):
-        total = total + back[n].astype(F32)
-    near[...] = total
+    edge_sum = edges_in[0].astype(F32) + edges_in[1].astype(F32)
+    near[...] = near[...] + kept[...] + edge_sum
     for copy in fourth:
         copy.wait_recv()
     back_project(
@@ -662,7 +696,7 @@
     for kz in range(2):
         for copy in first[kz] + second[kz] + beyond[kz]:
             copy.wait_send()
-    for copy in third + fourth + halo + returns + [over, home]:
+    for copy in third + fourth + halo + wide_halo + returns + edge_copies + [over, home]:
         copy.wait_send()
 
 
@@ -690,7 +724,9 @@
         vmem((NB, 2, BLK), F32),
         vmem((2 * NB, 512), F32),
         *[vmem((NB, 512), F32)] * 2,
-        *[vmem((9, NB, 2 * BLK), BF)] * 3,
+        *[vmem((3, 3 * NB, 2 * BLK), BF)] * 3,
+        vmem((NB, 2 * BLK), F32),
+        *[vmem((2, NB, 2 * BLK), BF)] * 2,
         *[vmem((PAIRS, 2 * BLK), F32)] * 4,
         vmem((NB, 2 * BLK), F32),
         vmem((2, N, 256), F32),

time: 57 us -> 55.3 us (0.970)
  Pallas kernels: 54.7 us -> 53.1 us
    pallas_call x1, Pallas kernels: 54.7 us -> 53.1 us  [per_device(): pl.pallas_call(whole_kernel, out_shape=jax.ShapeDtypeStruct((2, NB * BLK)...]
where the time goes in v6:
time: 55.3 us; the launch traced here: 55.1 us
  Pallas kernels  53.1 us (96%)
  local copies, waits for them, and re-layouts  1.38 us (2%)
  between operations  0.66 us (1%)
    pallas_call x1, Pallas kernels, per_device(): pl.pallas_call(whole_kernel, out_shape=jax.ShapeDtypeStruct((2, NB * BLK)...  53.1 us
    unnamed x1, local copies, waits for them, and re-layouts  1.38 us

profile of v6, /device:TPU:1, one launch (start us, length us, event | category | flops | bytes accessed | tf_op | source)
XLA Modules:
  0.0 55.1 jit_solution(14066761546537648268)
XLA Ops:
  0.7 53.1 %shard_map.154 = f32[2,4096]{1,0:T(2,128)} custom-call(f32[2,4096]{1,0:T(2,128)} %cur.1, s32[32,128]{1,0:T(8,128)} %cells.1, s32[1,128]{1,0:T(1,128)} %owned.1, s32[1,128]{1,0:T(1,128)} %picks.1, s32[1]{0:T(128)S(6)} %copy.18.count, bf16[128,256,128]{2,1,0:T(8,128)(2,1)} %bitcast.1, f32[32,128,128]{2,1,0:T(8,128)} %proj_hbm.1, ...), custom_call_target="tpu_custom_call" | custom-call | tf_op jit(solution)/shard_map/pallas_call | solution.py:757
  53.7 1.4 %copy.19 = f32[2,4096]{1,0:T(2,128)} copy(f32[2,4096]{1,0:T(2,128)} %shard_map.154) | data formatting | bytes 65536

commit v7 on v6

--- a/solution.py
+++ b/solution.py
@@ -134,8 +134,10 @@
 
     lax.fori_loop(0, NB // 8, boxes_of, 0)
     b_high, b_low = high_low(boxed[...])
-    along_cos = dot(b_high, tch[...]) + dot(b_low, tch[...]) + dot(b_high, tcl[...])
-    along_sin = dot(b_high, tsh[...]) + dot(b_low, tsh[...]) + dot(b_high, tsl[...])
+    both_parts = jnp.concatenate([b_high, b_low], axis=0)
+    by_cos, by_sin = dot(both_parts, tch[...]), dot(both_parts, tsh[...])
+    along_cos = by_cos[: 2 * NB] + by_cos[2 * NB :] + dot(b_high, tcl[...])
+    along_sin = by_sin[: 2 * NB] + by_sin[2 * NB :] + dot(b_high, tsl[...])
     store_twist(corner_x, corner_y, row, col, twist)
     plain_real = along_cos[:NB] + along_sin[NB:]
     plain_imag = along_cos[NB:] - along_sin[:NB]
@@ -353,7 +355,8 @@
     pieces = [a[32:64] + b[288:320], a[64:256], a[256:320] + b[0:64], b[64:256], b[256:288] + a[0:32]]
     cells = jnp.concatenate(pieces, axis=0)
     if extra is not None:
-        cells = cells + extra[...].astype(F32)
+        halves = [unpack_half(extra, 0), unpack_half(extra, 1)]
+        cells = cells + jnp.concatenate(halves, axis=0)
     out[...] = cells.astype(BF)
 
 
@@ -366,8 +369,10 @@
     turned_real = real * twist[0] + imag * twist[1]
     turned_imag = imag * twist[0] - real * twist[1]
     b_high, b_low = high_low(jnp.concatenate([turned_real, turned_imag], axis=0))
-    along_cos = dot(b_high, tch[...]) + dot(b_low, tch[...]) + dot(b_high, tcl[...])
-    along_sin = dot(b_high, tsh[...]) + dot(b_low, tsh[...]) + dot(b_high, tsl[...])
+    both_parts = jnp.concatenate([b_high, b_low], axis=0)
+    by_cos, by_sin = dot(both_parts, tch[...]), dot(both_parts, tsh[...])
+    along_cos = by_cos[: 2 * NB] + by_cos[2 * NB :] + dot(b_high, tcl[...])
+    along_sin = by_sin[: 2 * NB] + by_sin[2 * NB :] + dot(b_high, tsl[...])
     box_real[...] = along_cos[:NB] - along_sin[NB:]
     box_imag[...] = along_cos[NB:] + along_sin[:NB]
 
@@ -469,6 +474,37 @@
         lax.fori_loop(0, 4, part, 0)
 
 
+def pack_halves(source, target):
+    low = iota((256, 128), 1) < 64
+    upper = pltpu.roll(source[256:512, :].astype(F32), 64, 1)
+    target[0:256, :] = jnp.where(low, source[0:256, :].astype(F32), upper).astype(BF)
+
+
+def unpack_half(packed, half):
+    rows = packed[0:256, :].astype(F32)
+    return rows if half == 0 else pltpu.roll(rows, 64, 1)
+
+
+def pack_sources(source, target):
+    pack_halves(source, target)
+    which = iota((16, 128), 1) - 64
+    pick = jnp.where((which == iota((16, 128), 0)) & (which < 2), 1.0, 0.0).astype(BF)
+    corners = dot_nt(pick, source[...])
+    rows = [corners[c : c + 1, 128 * m : 128 * m + 128] for c in range(2) for m in range(4)]
+    target[256:272, :] = jnp.concatenate(rows + [jnp.zeros((8, 128), F32)], axis=0).astype(BF)
+
+
+def unpack_sources(packed, target):
+    corners = jnp.transpose(packed[256:272, :].astype(F32)[0:8])
+    lane = iota((128, 128), 1)
+    for m in range(4):
+        part = unpack_half(packed, m // 2)[128 * (m % 2) : 128 * (m % 2) + 128]
+        part = jnp.where(lane < 64, part, 0.0)
+        part = jnp.where(lane == 64, corners[:, m : m + 1], part)
+        part = jnp.where(lane == 65, corners[:, 4 + m : 5 + m], part)
+        target[128 * m : 128 * m + 128, :] = part.astype(BF)
+
+
 def whole_kernel(
     cur, cells, owned, picks, count, near_hbm, proj_hbm, green_hbm,
     tch_hbm, tcl_hbm, tsh_hbm, tsl_hbm, ahead_hbm, backwards_hbm, cos_hbm, sin_hbm, out,
@@ -479,7 +515,7 @@
     send_a, recv_a, send_b, recv_b, sem_send_a, sem_recv_a, sem_send_b, sem_recv_b,
     send_c, recv_c, send_d, recv_d, sem_send_c, sem_recv_c, sem_send_d, sem_recv_d,
     sem_send_h, sem_recv_h, sem_send_r, sem_recv_r,
-    far_c, far_starts, far_hot, far_a, recv_f, send_q, recv_q, sem_far,
+    far_c, send_o, recv_o, far_starts, far_hot, far_a, recv_f, send_q, recv_q, sem_far,
 ):
     row, col = lax.axis_index("row"), lax.axis_index("col")
     mesh_ids = pl.DeviceIdType.MESH
@@ -596,9 +632,12 @@
         copy.start()
     for load in loads[6:]:
         load.wait()
+    for kz in range(2):
+        turn_green(kz, green, turned)
     for copy in third:
         copy.wait_recv()
-    over = remote(recv_c, far_c, sem_far.at[0], sem_far.at[1], (far, col))
+    pack_sources(recv_c, send_o)
+    over = remote(send_o, recv_o, sem_far.at[0], sem_far.at[1], (far, col))
     over.start()
     build_image(recv_c, row, spreads, padded, wides, starts, odd, even)
     sems_a, sems_b = (sem_send_a, sem_recv_a), (sem_send_b, sem_recv_b)
@@ -620,6 +659,7 @@
         first[kz].append(copy)
         recv_a[kz, row] = send_a[kz, row]
     over.wait_recv()
+    unpack_sources(recv_o, far_c)
     build_image(far_c, far, spreads, padded, wides, far_starts, odd, even)
     for kz in range(2):
         forward_y(kz, z, odd, even, cos, sin, far_a, 0)
@@ -646,7 +686,6 @@
     build_hot(far_c, far, far_hot)
     clear_cells(accs)
     for kz in range(2):
-        turn_green(kz, green, turned)
         for copy in first[kz]:
             copy.wait_recv()
         along_x(kz, recv_a, turned, cos, sin, send_b, d_one, d_two, h_one, h_two)
@@ -665,7 +704,8 @@
         beyond[kz][0].wait_recv()
         inverse_y(kz, recv_f, [0], [z], cos, sin, spec, pot)
         pick_cells(kz, pot, far_starts, far_hot, accs)
-    fold_cells(accs, spreads, send_q, None)
+    fold_cells(accs, spreads, send_d, None)
+    pack_halves(send_d, send_q)
     home = remote(send_q, recv_q, sem_far.at[2], sem_far.at[3], (far, col))
     home.start()
     clear_cells(accs)
@@ -745,10 +785,11 @@
         *[dma((NCOL,))] * 4,
         *[dma((9,))] * 4,
         vmem((NCOL * NB, 128), BF),
+        *[vmem((272, 128), BF)] * 2,
         vmem((wrapped, 128), jnp.int32),
         vmem((4, wrapped, XR), BF),
         *[vmem((2, 2, 2 * XR, 128), BF)] * 2,
-        *[vmem((NCOL * NB, 128), BF)] * 2,
+        *[vmem((256, 128), BF)] * 2,
         dma((4,)),
     ]
     in_vmem = pl.BlockSpec(memory_space=pltpu.VMEM)

time: 55.3 us -> 54.8 us (level)
  Pallas kernels: 53.1 us -> 52.5 us
    pallas_call x1, Pallas kernels: 53.1 us -> 52.5 us  [per_device(): pl.pallas_call(whole_kernel, out_shape=jax.ShapeDtypeStruct((2, NB * BLK)...]
where the time goes in v7:
time: 54.8 us; the launch traced here: 54.5 us
  Pallas kernels  52.5 us (96%)
  local copies, waits for them, and re-layouts  1.38 us (3%)
  between operations  0.66 us (1%)
    pallas_call x1, Pallas kernels, per_device(): pl.pallas_call(whole_kernel, out_shape=jax.ShapeDtypeStruct((2, NB * BLK)...  52.5 us
    unnamed x1, local copies, waits for them, and re-layouts  1.38 us

profile of v7, /device:TPU:1, one launch (start us, length us, event | category | flops | bytes accessed | tf_op | source)
XLA Modules:
  0.0 54.5 jit_solution(2417387947805341179)
XLA Ops:
  0.7 52.5 %shard_map.154 = f32[2,4096]{1,0:T(2,128)} custom-call(f32[2,4096]{1,0:T(2,128)} %cur.1, s32[32,128]{1,0:T(8,128)} %cells.1, s32[1,128]{1,0:T(1,128)} %owned.1, s32[1,128]{1,0:T(1,128)} %picks.1, s32[1]{0:T(128)S(6)} %copy.18.count, bf16[128,256,128]{2,1,0:T(8,128)(2,1)} %bitcast.1, f32[32,128,128]{2,1,0:T(8,128)} %proj_hbm.1, ...), custom_call_target="tpu_custom_call" | custom-call | tf_op jit(solution)/shard_map/pallas_call | solution.py:798
  53.1 1.4 %copy.19 = f32[2,4096]{1,0:T(2,128)} copy(f32[2,4096]{1,0:T(2,128)} %shard_map.154) | data formatting | bytes 65536

commit v8 on v7

--- a/solution.py
+++ b/solution.py
@@ -177,18 +177,19 @@
     return jnp.where(inside, 1.0, 0.0)
 
 
-def image_chunk(q, corner, local_x, wides, starts):
+def image_chunk(q, corner, local_x, wides, starts, masks):
     first = 64 * q if q < 4 else 64 * q - 256
     wide = wides[0] if q < 4 else wides[1]
-    mask = chunk_mask(starts, q).astype(BF)
-    mask = jnp.concatenate([mask] * 4, axis=1)
+    mask = chunk_mask(starts, q)
+    masks[q] = mask
+    mask = jnp.concatenate([mask.astype(BF)] * 4, axis=1)
     offset = local_x - corner[0:1, 64 * q : 64 * q + 128].astype(jnp.int32)
     lhs = [jnp.where(offset == ex, 1.0, 0.0).astype(BF) for ex in range(4)]
     rhs = [wide[first : first + 128, 512 * ex : 512 * ex + 512] * mask for ex in range(4)]
     return dot(jnp.concatenate(lhs, axis=1), jnp.concatenate(rhs, axis=0))
 
 
-def build_image(recv, band, spreads, padded, wides, starts, odd, even):
+def build_image(recv, band, spreads, padded, wides, starts, masks, odd, even):
     padded[0:NB, :] = recv[512 - NB :, :]
     padded[NB : NB + 512, :] = recv[...]
     padded[NB + 512 :, :] = recv[0:NB, :]
@@ -206,8 +207,8 @@
     corner = jnp.concatenate([corner[:, 480:], corner, corner[:, :NB]], axis=1)
     local_x = local_x_of_row((XR, 128), 0, band)
     for q in range(4):
-        ahead = image_chunk(q, corner, local_x, wides, starts)
-        backwards = image_chunk(7 - q, corner, local_x, wides, starts)
+        ahead = image_chunk(q, corner, local_x, wides, starts, masks)
+        backwards = image_chunk(7 - q, corner, local_x, wides, starts, masks)
         minus, plus = (ahead - backwards).astype(BF), (ahead + backwards).astype(BF)
         for kz in range(2):
             for c in range(2):
@@ -326,10 +327,9 @@
     hot[:, NB + 512 :, :] = hot[:, NB : 2 * NB, :]
 
 
-def pick_cells(kz, pot, starts, hot, accs):
+def pick_cells(kz, pot, masks, hot, accs):
     for q in range(8):
-        mask = chunk_mask(starts, q)
-        mask = jnp.concatenate([mask] * 2, axis=1)
+        mask = jnp.concatenate([masks[q]] * 2, axis=1)
         lane = 128 * q if q < 4 else 512 + 128 * (7 - q)
         cells = [pot[XR * c : XR * c + XR, lane : lane + 128] for c in range(2)]
         cells = jnp.concatenate(cells, axis=1)
@@ -515,7 +515,7 @@
     send_a, recv_a, send_b, recv_b, sem_send_a, sem_recv_a, sem_send_b, sem_recv_b,
     send_c, recv_c, send_d, recv_d, sem_send_c, sem_recv_c, sem_send_d, sem_recv_d,
     sem_send_h, sem_recv_h, sem_send_r, sem_recv_r,
-    far_c, send_o, recv_o, far_starts, far_hot, far_a, recv_f, send_q, recv_q, sem_far,
+    far_c, send_o, recv_o, masks, far_masks, far_hot, far_a, recv_f, send_q, recv_q, sem_far,
 ):
     row, col = lax.axis_index("row"), lax.axis_index("col")
     mesh_ids = pl.DeviceIdType.MESH
@@ -639,7 +639,7 @@
     pack_sources(recv_c, send_o)
     over = remote(send_o, recv_o, sem_far.at[0], sem_far.at[1], (far, col))
     over.start()
-    build_image(recv_c, row, spreads, padded, wides, starts, odd, even)
+    build_image(recv_c, row, spreads, padded, wides, starts, masks, odd, even)
     sems_a, sems_b = (sem_send_a, sem_recv_a), (sem_send_b, sem_recv_b)
     first, second, beyond = [[], []], [[], []], [[], []]
     for kz in range(2):
@@ -660,31 +660,13 @@
         recv_a[kz, row] = send_a[kz, row]
     over.wait_recv()
     unpack_sources(recv_o, far_c)
-    build_image(far_c, far, spreads, padded, wides, far_starts, odd, even)
+    build_image(far_c, far, spreads, padded, wides, starts, far_masks, odd, even)
     for kz in range(2):
         forward_y(kz, z, odd, even, cos, sin, far_a, 0)
         copy = row_copy(kz, far_a.at[kz, 1 - core], recv_a.at[kz, far], sems_a, 5, sibling)
         copy.start()
         first[kz].append(copy)
         recv_a[kz, far] = far_a[kz, core]
-    for copy in returns:
-        copy.wait_recv()
-    column = spread_back[1].astype(F32) + back[0].astype(F32) + back[2].astype(F32)
-    kept[...] = column[NB : 2 * NB]
-    edges[0] = column[:NB].astype(BF)
-    edges[1] = column[2 * NB :].astype(BF)
-    edge_copies = [
-        remote(
-            edges.at[place], edges_in.at[place], sem_send_r.at[3 + place], sem_recv_r.at[3 + place],
-            beside_peer(0, step),
-        )
-        for step, place in ((-1, 0), (1, 1))
-    ]
-    for copy in edge_copies:
-        copy.start()
-    build_hot(recv_c, row, hot)
-    build_hot(far_c, far, far_hot)
-    clear_cells(accs)
     for kz in range(2):
         for copy in first[kz]:
             copy.wait_recv()
@@ -700,10 +682,29 @@
         beyond[kz].append(copy)
         recv_b[kz, row] = send_b[kz, row]
         recv_f[kz, core] = send_b[kz, far]
+        if kz == 0:
+            for copy in returns:
+                copy.wait_recv()
+            column = spread_back[1].astype(F32) + back[0].astype(F32) + back[2].astype(F32)
+            kept[...] = column[NB : 2 * NB]
+            edges[0] = column[:NB].astype(BF)
+            edges[1] = column[2 * NB :].astype(BF)
+            edge_copies = [
+                remote(
+                    edges.at[place], edges_in.at[place], sem_send_r.at[3 + place], sem_recv_r.at[3 + place],
+                    beside_peer(0, step),
+                )
+                for step, place in ((-1, 0), (1, 1))
+            ]
+            for copy in edge_copies:
+                copy.start()
+            build_hot(recv_c, row, hot)
+            build_hot(far_c, far, far_hot)
+            clear_cells(accs)
     for kz in range(2):
         beyond[kz][0].wait_recv()
         inverse_y(kz, recv_f, [0], [z], cos, sin, spec, pot)
-        pick_cells(kz, pot, far_starts, far_hot, accs)
+        pick_cells(kz, pot, far_masks, far_hot, accs)
     fold_cells(accs, spreads, send_d, None)
     pack_halves(send_d, send_q)
     home = remote(send_q, recv_q, sem_far.at[2], sem_far.at[3], (far, col))
@@ -714,7 +715,7 @@
         for copy in second[kz]:
             copy.wait_recv()
         inverse_y(kz, recv_b, [2 * chip for chip in held], held, cos, sin, spec, pot)
-        pick_cells(kz, pot, starts, hot, accs)
+        pick_cells(kz, pot, masks, hot, accs)
     home.wait_recv()
     fold_cells(accs, spreads, send_d, recv_q)
     fourth = col_copies(send_d, recv_d, sem_send_d, sem_recv_d)
@@ -786,7 +787,7 @@
         *[dma((9,))] * 4,
         vmem((NCOL * NB, 128), BF),
         *[vmem((272, 128), BF)] * 2,
-        vmem((wrapped, 128), jnp.int32),
+        *[vmem((8, 128, 128), F32)] * 2,
         vmem((4, wrapped, XR), BF),
         *[vmem((2, 2, 2 * XR, 128), BF)] * 2,
         *[vmem((256, 128), BF)] * 2,

time: 54.8 us -> 55.9 us (1.020)
  the two profiles are of different devices: /device:TPU:1 before, /device:TPU:0 now
where the time goes in v8:
time: 55.9 us; the launch traced here: 55.7 us
  Pallas kernels  53.6 us (96%)
  local copies, waits for them, and re-layouts  1.38 us (2%)
  between operations  0.66 us (1%)
    pallas_call x1, Pallas kernels, per_device(): pl.pallas_call(whole_kernel, out_shape=jax.ShapeDtypeStruct((2, NB * BLK)...  53.6 us
    unnamed x1, local copies, waits for them, and re-layouts  1.38 us

profile of v8, /device:TPU:0, one launch (start us, length us, event | category | flops | bytes accessed | tf_op | source)
XLA Modules:
  0.0 55.7 jit_solution(319349483397258464)
XLA Ops:
  0.7 53.6 %shard_map.154 = f32[2,4096]{1,0:T(2,128)} custom-call(f32[2,4096]{1,0:T(2,128)} %cur.1, s32[32,128]{1,0:T(8,128)} %cells.1, s32[1,128]{1,0:T(1,128)} %owned.1, s32[1,128]{1,0:T(1,128)} %picks.1, s32[1]{0:T(128)S(6)} %copy.18.count, bf16[128,256,128]{2,1,0:T(8,128)(2,1)} %bitcast.1, f32[32,128,128]{2,1,0:T(8,128)} %proj_hbm.1, ...), custom_call_target="tpu_custom_call" | custom-call | tf_op jit(solution)/shard_map/pallas_call | solution.py:799
  54.3 1.4 %copy.19 = f32[2,4096]{1,0:T(2,128)} copy(f32[2,4096]{1,0:T(2,128)} %shard_map.154) | data formatting | bytes 65536

commit v9 on v7

--- a/solution.py
+++ b/solution.py
@@ -110,8 +110,8 @@
     codes[...] = code
 
     def values_of(i, carry):
-        for u in range(8):
-            g = i * 8 + u
+        for u in range(16):
+            g = i * 16 + u
             lhs = rows_high_low(cur[:, pl.ds(pl.multiple_of(g * BLK, BLK), BLK)])
             high, low = high_low(proj[g])
             p_high[g] = high
@@ -120,11 +120,11 @@
             vals[g] = first[0:2] + first[2:4] + dot_nt(lhs, low)[0:2]
         return carry
 
-    lax.fori_loop(0, NB // 8, values_of, 0)
+    lax.fori_loop(0, NB // 16, values_of, 0)
 
     def boxes_of(i, carry):
-        for u in range(8):
-            g = i * 8 + u
+        for u in range(16):
+            g = i * 16 + u
             hot = one_hot_rows(codes[pl.ds(g, 1), :])
             hots[g] = hot
             placed = dot_nt(rows_high_low(vals[g]), hot)
@@ -132,7 +132,7 @@
             boxed[pl.ds(NB + g, 1), :] = placed[1:2] + placed[3:4]
         return carry
 
-    lax.fori_loop(0, NB // 8, boxes_of, 0)
+    lax.fori_loop(0, NB // 16, boxes_of, 0)
     b_high, b_low = high_low(boxed[...])
     both_parts = jnp.concatenate([b_high, b_low], axis=0)
     by_cos, by_sin = dot(both_parts, tch[...]), dot(both_parts, tsh[...])
@@ -177,18 +177,19 @@
     return jnp.where(inside, 1.0, 0.0)
 
 
-def image_chunk(q, corner, local_x, wides, starts):
+def image_chunk(q, corner, local_x, wides, starts, masks):
     first = 64 * q if q < 4 else 64 * q - 256
     wide = wides[0] if q < 4 else wides[1]
-    mask = chunk_mask(starts, q).astype(BF)
-    mask = jnp.concatenate([mask] * 4, axis=1)
+    mask = chunk_mask(starts, q)
+    masks[q] = mask
+    mask = jnp.concatenate([mask.astype(BF)] * 4, axis=1)
     offset = local_x - corner[0:1, 64 * q : 64 * q + 128].astype(jnp.int32)
     lhs = [jnp.where(offset == ex, 1.0, 0.0).astype(BF) for ex in range(4)]
     rhs = [wide[first : first + 128, 512 * ex : 512 * ex + 512] * mask for ex in range(4)]
     return dot(jnp.concatenate(lhs, axis=1), jnp.concatenate(rhs, axis=0))
 
 
-def build_image(recv, band, spreads, padded, wides, starts, odd, even):
+def build_image(recv, band, spreads, padded, wides, starts, masks, odd, even):
     padded[0:NB, :] = recv[512 - NB :, :]
     padded[NB : NB + 512, :] = recv[...]
     padded[NB + 512 :, :] = recv[0:NB, :]
@@ -206,8 +207,8 @@
     corner = jnp.concatenate([corner[:, 480:], corner, corner[:, :NB]], axis=1)
     local_x = local_x_of_row((XR, 128), 0, band)
     for q in range(4):
-        ahead = image_chunk(q, corner, local_x, wides, starts)
-        backwards = image_chunk(7 - q, corner, local_x, wides, starts)
+        ahead = image_chunk(q, corner, local_x, wides, starts, masks)
+        backwards = image_chunk(7 - q, corner, local_x, wides, starts, masks)
         minus, plus = (ahead - backwards).astype(BF), (ahead + backwards).astype(BF)
         for kz in range(2):
             for c in range(2):
@@ -326,10 +327,9 @@
     hot[:, NB + 512 :, :] = hot[:, NB : 2 * NB, :]
 
 
-def pick_cells(kz, pot, starts, hot, accs):
+def pick_cells(kz, pot, masks, hot, accs):
     for q in range(8):
-        mask = chunk_mask(starts, q)
-        mask = jnp.concatenate([mask] * 2, axis=1)
+        mask = jnp.concatenate([masks[q]] * 2, axis=1)
         lane = 128 * q if q < 4 else 512 + 128 * (7 - q)
         cells = [pot[XR * c : XR * c + XR, lane : lane + 128] for c in range(2)]
         cells = jnp.concatenate(cells, axis=1)
@@ -377,18 +377,18 @@
     box_imag[...] = along_cos[NB:] + along_sin[:NB]
 
     def values_of(i, carry):
-        for u in range(8):
-            g = i * 8 + u
+        for u in range(16):
+            g = i * 16 + u
             box = jnp.concatenate([box_real[pl.ds(g, 1), :], box_imag[pl.ds(g, 1), :]], axis=0)
             picked = dot(rows_high_low(box), hots[g])
             vals[g] = picked[0:2] + picked[2:4]
         return carry
 
-    lax.fori_loop(0, NB // 8, values_of, 0)
+    lax.fori_loop(0, NB // 16, values_of, 0)
 
     def blocks_of(i, carry):
-        for u in range(8):
-            g = i * 8 + u
+        for u in range(16):
+            g = i * 16 + u
             lhs = rows_high_low(vals[g])
             first = dot(lhs, p_high[g])
             far = first[0:2] + first[2:4] + dot(lhs, p_low[g])[0:2]
@@ -397,7 +397,7 @@
             out[:, pl.ds(pl.multiple_of(g * BLK, BLK), BLK)] = far + beside
         return carry
 
-    lax.fori_loop(0, NB // 8, blocks_of, 0)
+    lax.fori_loop(0, NB // 16, blocks_of, 0)
 
 
 def column_of(row):
@@ -515,7 +515,7 @@
     send_a, recv_a, send_b, recv_b, sem_send_a, sem_recv_a, sem_send_b, sem_recv_b,
     send_c, recv_c, send_d, recv_d, sem_send_c, sem_recv_c, sem_send_d, sem_recv_d,
     sem_send_h, sem_recv_h, sem_send_r, sem_recv_r,
-    far_c, send_o, recv_o, far_starts, far_hot, far_a, recv_f, send_q, recv_q, sem_far,
+    far_c, send_o, recv_o, masks, far_masks, far_hot, far_a, recv_f, send_q, recv_q, sem_far,
 ):
     row, col = lax.axis_index("row"), lax.axis_index("col")
     mesh_ids = pl.DeviceIdType.MESH
@@ -639,7 +639,7 @@
     pack_sources(recv_c, send_o)
     over = remote(send_o, recv_o, sem_far.at[0], sem_far.at[1], (far, col))
     over.start()
-    build_image(recv_c, row, spreads, padded, wides, starts, odd, even)
+    build_image(recv_c, row, spreads, padded, wides, starts, masks, odd, even)
     sems_a, sems_b = (sem_send_a, sem_recv_a), (sem_send_b, sem_recv_b)
     first, second, beyond = [[], []], [[], []], [[], []]
     for kz in range(2):
@@ -660,7 +660,7 @@
         recv_a[kz, row] = send_a[kz, row]
     over.wait_recv()
     unpack_sources(recv_o, far_c)
-    build_image(far_c, far, spreads, padded, wides, far_starts, odd, even)
+    build_image(far_c, far, spreads, padded, wides, starts, far_masks, odd, even)
     for kz in range(2):
         forward_y(kz, z, odd, even, cos, sin, far_a, 0)
         copy = row_copy(kz, far_a.at[kz, 1 - core], recv_a.at[kz, far], sems_a, 5, sibling)
@@ -703,7 +703,7 @@
     for kz in range(2):
         beyond[kz][0].wait_recv()
         inverse_y(kz, recv_f, [0], [z], cos, sin, spec, pot)
-        pick_cells(kz, pot, far_starts, far_hot, accs)
+        pick_cells(kz, pot, far_masks, far_hot, accs)
     fold_cells(accs, spreads, send_d, None)
     pack_halves(send_d, send_q)
     home = remote(send_q, recv_q, sem_far.at[2], sem_far.at[3], (far, col))
@@ -714,7 +714,7 @@
         for copy in second[kz]:
             copy.wait_recv()
         inverse_y(kz, recv_b, [2 * chip for chip in held], held, cos, sin, spec, pot)
-        pick_cells(kz, pot, starts, hot, accs)
+        pick_cells(kz, pot, masks, hot, accs)
     home.wait_recv()
     fold_cells(accs, spreads, send_d, recv_q)
     fourth = col_copies(send_d, recv_d, sem_send_d, sem_recv_d)
@@ -786,7 +786,7 @@
         *[dma((9,))] * 4,
         vmem((NCOL * NB, 128), BF),
         *[vmem((272, 128), BF)] * 2,
-        vmem((wrapped, 128), jnp.int32),
+        *[vmem((8, 128, 128), F32)] * 2,
         vmem((4, wrapped, XR), BF),
         *[vmem((2, 2, 2 * XR, 128), BF)] * 2,
         *[vmem((256, 128), BF)] * 2,

time: 54.8 us -> 53.8 us (0.982)
  Pallas kernels: 52.5 us -> 51.5 us
    pallas_call x1, Pallas kernels: 52.5 us -> 51.5 us  [per_device(): pl.pallas_call(whole_kernel, out_shape=jax.ShapeDtypeStruct((2, NB * BLK)...]
where the time goes in v9:
time: 53.8 us; the launch traced here: 53.5 us
  Pallas kernels  51.5 us (96%)
  local copies, waits for them, and re-layouts  1.38 us (3%)
  between operations  0.66 us (1%)
    pallas_call x1, Pallas kernels, per_device(): pl.pallas_call(whole_kernel, out_shape=jax.ShapeDtypeStruct((2, NB * BLK)...  51.5 us
    unnamed x1, local copies, waits for them, and re-layouts  1.38 us

profile of v9, /device:TPU:1, one launch (start us, length us, event | category | flops | bytes accessed | tf_op | source)
XLA Modules:
  0.0 53.5 jit_solution(1902424779558756556)
XLA Ops:
  0.7 51.5 %shard_map.154 = f32[2,4096]{1,0:T(2,128)} custom-call(f32[2,4096]{1,0:T(2,128)} %cur.1, s32[32,128]{1,0:T(8,128)} %cells.1, s32[1,128]{1,0:T(1,128)} %owned.1, s32[1,128]{1,0:T(1,128)} %picks.1, s32[1]{0:T(128)S(6)} %copy.18.count, bf16[128,256,128]{2,1,0:T(8,128)(2,1)} %bitcast.1, f32[32,128,128]{2,1,0:T(8,128)} %proj_hbm.1, ...), custom_call_target="tpu_custom_call" | custom-call | tf_op jit(solution)/shard_map/pallas_call | solution.py:798
  52.1 1.4 %copy.19 = f32[2,4096]{1,0:T(2,128)} copy(f32[2,4096]{1,0:T(2,128)} %shard_map.154) | data formatting | bytes 65536
